TPU v7x, 512 devices: a whole 4x4x16 slice. The times are simulated.
512 devices in a mesh: outer: 4 (over x), shard: 4 (over z_hi, core), tensor: 32 (over y, z_lo).
Axes of the slice: x: 4, y: 4, z: 16 (z_hi: 2, z_lo: 8; z = z_hi * 8 + z_lo), core: 2. Of those that a mesh axis runs over, the one named last changes fastest.
Arguments:
- quantized: bfloat16 [2048, 4096], P(('outer', 'shard'), 'tensor'), may hold values from -6 to 6
- scales: float32 [2048, 32], P(('outer', 'shard'), 'tensor'), may hold values from 0.3 to 3
- d_hidden: bfloat16 [2048, 16384], P(('outer', 'shard'), 'tensor'), may hold values from -6 to 6
- w_gate: bfloat16 [4096, 16384], P('shard', 'tensor'), may hold values from -0.09375 to 0.09375
- w_up: bfloat16 [4096, 16384], P('shard', 'tensor'), may hold values from -0.09375 to 0.09375
Outputs:
- d_input: bfloat16 [2048, 4096], P(('outer', 'shard'), 'tensor')
- d_gate_weight: bfloat16 [4096, 16384], P('shard', 'tensor')
- d_up_weight: bfloat16 [4096, 16384], P('shard', 'tensor')
All inputs are finite; a program needn't handle non-finite values.
Results may differ from a plain program's by a relative error of at most 0.03.
Values may be sent and summed in bfloat16 or wider, within the bound.
No kernel may reach another device: no remote copies, remote signals or barrier semaphores. Data moves between devices by JAX's collectives and lax.ppermute only.
A program may use at most 64 MiB of HBM per device.

v0:
```python
import jax
import jax.numpy as jnp
from jax import lax
from jax.sharding import PartitionSpec as P


def shards(quantized, scales, d_hidden, w_gate, w_up):
    count, width = quantized.shape
    blocks = scales.shape[1]
    local_inputs = (
        (quantized.astype(jnp.float32).reshape(count, blocks, width // blocks) * scales[:, :, None])
        .reshape(count, width)
        .astype(jnp.bfloat16)
    )
    inputs = lax.all_gather(local_inputs, "tensor", axis=1, tiled=True)
    column_rows = lax.all_to_all(inputs, "shard", split_axis=1, concat_axis=0, tiled=True)
    gate_full, up_full = (
        lax.all_gather(w_gate, "shard", axis=0, tiled=True),
        lax.all_gather(w_up, "shard", axis=0, tiled=True),
    )
    gate = jnp.dot(inputs, gate_full, preferred_element_type=jnp.float32)
    up = jnp.dot(inputs, up_full, preferred_element_type=jnp.float32)
    sig = jax.nn.sigmoid(gate)
    grad_out = d_hidden.astype(jnp.float32)
    d_gate = (grad_out * up * sig * (1.0 + gate * (1.0 - sig))).astype(jnp.bfloat16)
    d_up = (grad_out * gate * sig).astype(jnp.bfloat16)
    gate_rows, up_rows = (
        lax.all_gather(d_gate, "shard", axis=0, tiled=True),
        lax.all_gather(d_up, "shard", axis=0, tiled=True),
    )
    gate_weight_part = jnp.einsum(
        "td,tf->df", column_rows, gate_rows, preferred_element_type=jnp.float32
    )
    up_weight_part = jnp.einsum(
        "td,tf->df", column_rows, up_rows, preferred_element_type=jnp.float32
    )
    d_gate_weight, d_up_weight = (
        lax.psum(gate_weight_part.astype(jnp.bfloat16), "outer").astype(jnp.float32),
        lax.psum(up_weight_part.astype(jnp.bfloat16), "outer").astype(jnp.float32),
    )
    partial_value = jnp.einsum("tf,df->td", d_gate, gate_full, preferred_element_type=jnp.float32)
    partial_value = partial_value + jnp.einsum(
        "tf,df->td", d_up, up_full, preferred_element_type=jnp.float32
    )
    d_input = lax.psum_scatter(
        partial_value.astype(jnp.bfloat16), "tensor", scatter_dimension=1, tiled=True
    )
    return (d_input, d_gate_weight.astype(jnp.bfloat16), d_up_weight.astype(jnp.bfloat16))


def solution(mesh):
    in_specs = (
        P(("outer", "shard"), "tensor"),
        P(("outer", "shard"), "tensor"),
        P(("outer", "shard"), "tensor"),
        P("shard", "tensor"),
        P("shard", "tensor"),
    )
    out_specs = (P(("outer", "shard"), "tensor"), P("shard", "tensor"), P("shard", "tensor"))
    return jax.shard_map(shards, mesh=mesh, in_specs=in_specs, out_specs=out_specs, check_vma=False)
```

profile of v0, /device:TPU:25, one launch (start us, length us, event | category | flops | bytes accessed | tf_op | source)
XLA Modules:
  0.0 832.0 jit_solution(8049162093942858173)
XLA Ops:
  7.2 0.0 all-gather.4.cloned.1.call-start
  7.2 0.9 copy.10
  8.1 1.3 multiply_convert_fusion
  9.4 0.0 all-gather.4.cloned.1.call-update
  9.4 0.0 all-gather.8.cloned.1.call-start
  9.5 0.7 all-gather.8.cloned.1.call-update
  10.2 0.0 all-gather.6.cloned.1.call-start
  10.2 0.7 all-gather.6.cloned.1.call-update
  10.9 186.9 %all-gather.4.cloned.1.call-done = bf16[128,4096]{0,1:T(8,128)(2,1)} async-done(((bf16[128,128]{0,1:T(8,128)(2,1)}), bf16[128,4096]{0,1:T(8,128)(2,1)}) %all-gather.4.cloned.1.call-update) | async-done | bytes 1048592 | tf_op jit(solution)/shard_map/all_gather | solution.py:15
  197.9 34.6 %all-to-all-start = ((bf16[128,4,1024]{0,2,1:T(8,128)(2,1)}), bf16[128,4,1024]{0,2,1:T(8,128)(2,1)S(1)}, u32[]{:S(2)}, u32[]{:S(2)}) async-start(bf16[128,4,1024]{0,2,1:T(8,128)(2,1)} %bitcast.18), calls=%async_computation | async-start | bytes 2097152 | tf_op jit(solution)/shard_map/all_to_all | solution.py:16
  232.5 107.8 %all-gather.8.cloned.1.call-done = bf16[4096,512]{1,0:T(8,128)(2,1)} async-done(((bf16[1024,512]{1,0:T(8,128)(2,1)}), bf16[4096,512]{1,0:T(8,128)(2,1)}) %all-gather.8.cloned.1.call-update) | async-done | bytes 4194320 | tf_op jit(solution)/shard_map/all_gather | solution.py:18
  340.3 3.3 fusion.5
  343.6 160.2 %all-gather.6.cloned.1.call-done = bf16[4096,512]{1,0:T(8,128)(2,1)} async-done(((bf16[1024,512]{1,0:T(8,128)(2,1)}), bf16[4096,512]{1,0:T(8,128)(2,1)}) %all-gather.6.cloned.1.call-update) | async-done | bytes 4194320 | tf_op jit(solution)/shard_map/all_gather | solution.py:19
  503.8 3.1 fusion.3
  506.9 0.3 copy-done.1
  507.2 1.5 fusion.6
  508.7 0.7 copy-done
  509.4 1.5 fusion
  510.9 1.3 copy.12
  512.2 0.0 reduce-scatter.4.cloned.1.call-update
  512.2 0.0 all-reduce.3.cloned.1.call-start
  512.3 0.5 copy.11
  512.8 18.8 %all_gather.19 = bf16[512,512]{1,0:T(8,128)(2,1)S(1)} all-gather(bf16[128,512]{1,0:T(8,128)(2,1)S(1)} %get-tuple-element.5), channel_id=1, replica_groups=mesh['outer'=4,'shard'=4,'tensor'=32] {'shard'}, dimensions={0}, use_global_device_ids=true | all-gather | bytes 655360 | tf_op jit(solution)/shard_map/all_gather | solution.py:29
  531.6 18.5 %all_gather.18 = bf16[512,512]{1,0:T(8,128)(2,1)S(1)} all-gather(bf16[128,512]{1,0:T(8,128)(2,1)S(1)} %fusion.3), channel_id=1, replica_groups=mesh['outer'=4,'shard'=4,'tensor'=32] {'shard'}, dimensions={0}, use_global_device_ids=true | all-gather | bytes 655360 | tf_op jit(solution)/shard_map/all_gather | solution.py:28
  550.1 1.7 convolution_convert_fusion.1
  551.8 1.7 convolution_convert_fusion
  553.6 0.0 all-reduce.3.cloned.1.call-update
  553.6 151.8 %reduce-scatter.4.cloned.1.call-done = bf16[128,128]{1,0:T(8,128)(2,1)} async-done(((bf16[4096,128]{1,0:T(8,128)(2,1)}), bf16[128,128]{1,0:T(8,128)(2,1)}) %reduce-scatter.4.cloned.1.call-update) | async-done | bytes 32784
  705.4 1.5 copy.13
  706.9 114.1 %all-reduce.3.cloned.1.call-done = (bf16[1024,512]{1,0:T(8,128)(2,1)}, bf16[1024,512]{1,0:T(8,128)(2,1)}) async-done(((bf16[1024,512]{1,0:T(8,128)(2,1)}, bf16[1024,512]{1,0:T(8,128)(2,1)}), (bf16[1024,512]{1,0:T(8,128)(2,1)}, bf16[1024,512]{1,0:T(8,128)(2,1)})) %all-reduce.3.cloned.1.call-update) | async-done | bytes 2097168 | tf_op jit(solution)/shard_map/psum | solution.py:38
  820.9 2.3 copy.16
  823.2 2.3 copy.17
  (8 shorter events, 0.0 us)
Async XLA Ops:
  7.2 333.1 %copy-start.3 = (bf16[128,512]{1,0:T(8,128)(2,1)S(1)}, bf16[128,512]{1,0:T(8,128)(2,1)}, u32[]{:S(2)}) copy-start(bf16[128,512]{1,0:T(8,128)(2,1)} %param.7) | copy-start | bytes 393220
  7.2 190.7 %all-gather.4.cloned.1.call-start = ((), (), s32[]{:S(2)}) async-start(), calls=%async_computation.2 | async-start | bytes 1081344 | tf_op jit(solution)/shard_map/all_gather | solution.py:15
  9.4 330.9 %all-gather.8.cloned.1.call-start = ((), (), s32[]{:S(2)}) async-start(), calls=%async_computation.4 | async-start | bytes 5242880 | tf_op jit(solution)/shard_map/all_gather | solution.py:18
  10.2 493.6 %all-gather.6.cloned.1.call-start = ((), (), s32[]{:S(2)}) async-start(), calls=%async_computation.3 | async-start | bytes 5242880 | tf_op jit(solution)/shard_map/all_gather | solution.py:19
  197.9 305.9 %copy-start.2 = (bf16[128,4096]{0,1:T(8,128)(2,1)S(1)}, bf16[128,4096]{0,1:T(8,128)(2,1)}, u32[]{:S(2)}) copy-start(bf16[128,4096]{0,1:T(8,128)(2,1)} %all-gather.4.cloned.1.call-done) | copy-start | bytes 3145732
  197.9 314.4 %all-to-all-start = ((bf16[128,4,1024]{0,2,1:T(8,128)(2,1)}), bf16[128,4,1024]{0,2,1:T(8,128)(2,1)S(1)}, u32[]{:S(2)}, u32[]{:S(2)}) async-start(bf16[128,4,1024]{0,2,1:T(8,128)(2,1)} %bitcast.18), calls=%async_computation | async-start | bytes 2097152 | tf_op jit(solution)/shard_map/all_to_all | solution.py:16
  232.5 472.9 %reduce-scatter.4.cloned.1.call-start = ((), (), s32[]{:S(2)}) async-start(), calls=%async_computation.5 | async-start | bytes 1081344
  503.7 3.4 copy-start.1
  507.2 2.2 copy-start
  512.2 308.7 %all-reduce.3.cloned.1.call-start = ((), (), s32[]{:S(2)}) async-start(), calls=%async_computation.6 | async-start | bytes 4194304 | tf_op jit(solution)/shard_map/psum | solution.py:38
Sparse Core Ops, SparseCore 0:
  10.7 187.1 all-gather.3
  200.0 140.2 all-gather.7
  342.4 161.3 all-gather.5
  512.3 192.9 reduce-scatter.3
  708.4 112.4 all-reduce.2
where the time goes:
time: 833 us; the launch traced here: 832 us
  waiting for transfers between devices  722 us (87%)
  blocking collectives  37.3 us (4%)
  starting transfers between devices  34.8 us (4%)
  between operations  13.8 us (2%)
  matrix products  12.8 us (2%)
  local copies, waits for them, and re-layouts  9.78 us (1%)
    all_gather x1, waiting for transfers between devices, shards(): inputs = lax.all_gather(local_inputs, 'tensor', axis=1, tiled=True)  187 us
    all_gather x1, waiting for transfers between devices, shards(): lax.all_gather(w_up, 'shard', axis=0, tiled=True)  160 us
    unnamed x6, waiting for transfers between devices  153 us
    psum x1, waiting for transfers between devices, shards(): lax.psum(gate_weight_part.astype(jnp.bfloat16), 'outer').astype(jnp.float32)  114 us
    all_gather x1, waiting for transfers between devices, shards(): lax.all_gather(w_gate, 'shard', axis=0, tiled=True)  108 us
    all_to_all x1, starting transfers between devices, shards(): lax.all_to_all(inputs, 'shard', split_axis=1, concat_axis=0, tiled=True)  34.6 us
    all_gather x1, blocking collectives, shards(): lax.all_gather(d_up, 'shard', axis=0, tiled=True)  18.8 us
    all_gather x1, blocking collectives, shards(): lax.all_gather(d_gate, 'shard', axis=0, tiled=True)  18.5 us
  transfers between devices with their start and end apart: 6, of which 5 were waited for; matrix products, arithmetic and copies ran while one was open for 2% of the time, Pallas kernels for 0%

commit v1 on v0

v1 whole, which is shorter than its diff:
```python
import jax
import jax.numpy as jnp
import numpy as np
from jax import lax
from jax.sharding import Mesh, PartitionSpec as P

AXES = ("x", "zh", "c", "y", "zl")
SIZES = {"x": 4, "zh": 2, "c": 2, "y": 4, "zl": 8}
ROWS = ("x", "zh", "c")
COLS = ("y", "zl")
SHARD = ("zh", "c")
F32 = jnp.float32
BF16 = jnp.bfloat16


def permute(value, axes, target):
    sizes = [SIZES[a] for a in axes]
    pairs = []
    for i in range(int(np.prod(sizes))):
        at = dict(zip(axes, map(int, np.unravel_index(i, sizes))))
        to = target(at)
        pairs.append((i, int(np.ravel_multi_index([to[a] for a in axes], sizes))))
    return lax.ppermute(value, axes if len(axes) > 1 else axes[0], pairs)


def swap_shard_y(value):
    return permute(
        value,
        ("zh", "c", "y"),
        lambda d: {"zh": d["y"] // 2, "c": d["y"] % 2, "y": d["zh"] * 2 + d["c"]},
    )


def swap_core(value):
    return permute(value, ("c",), lambda d: {"c": 1 - d["c"]})


def swap_half(value):
    return permute(value, ("zh",), lambda d: {"zh": 1 - d["zh"]})


def spread(value, axis):
    n = SIZES[axis]
    return lax.all_to_all(jnp.broadcast_to(value[None], (n,) + value.shape), axis, 0, 0)


def relative(blocks):
    s = lax.axis_index("zh") * 2 + lax.axis_index("c")
    return jnp.stack([lax.dynamic_index_in_dim(blocks, s ^ r, 0, keepdims=False) for r in range(4)])


def shards(quantized, scales, d_hidden, w_gate, w_up):
    count, width = quantized.shape
    ff = w_gate.shape[1]
    rows = w_gate.shape[0]
    local = (quantized.astype(F32) * scales).astype(BF16)
    with jax.named_scope("gather_inputs"):
        held = spread(swap_shard_y(local), "zl")
        held = held.transpose(1, 0, 2).reshape(count, rows)
        held = spread(held, "y")
        inputs = relative(held)
    with jax.named_scope("partial_gate_up"):
        w = jnp.concatenate([w_gate, w_up], axis=1)
        parts = jnp.dot(inputs.reshape(4 * count, rows), w, preferred_element_type=F32)
        parts = parts.reshape(2, 2, count, 2 * ff)
    with jax.named_scope("core_sum"):
        parts = parts[:, 0] + swap_core(parts[:, 1].astype(BF16)).astype(F32)
    with jax.named_scope("half_sum"):
        pre = parts[0] + swap_half(parts[1].astype(BF16)).astype(F32)
    with jax.named_scope("elementwise"):
        gate, up = pre[:, :ff], pre[:, ff:]
        sig = jax.nn.sigmoid(gate)
        grad_out = d_hidden.astype(F32)
        d_gate = (grad_out * up * sig * (1.0 + gate * (1.0 - sig))).astype(BF16)
        d_up = (grad_out * gate * sig).astype(BF16)
        d = jnp.concatenate([d_gate, d_up], axis=1)
    with jax.named_scope("d_half"):
        d = jnp.stack([d, swap_half(d)])
    with jax.named_scope("d_core"):
        d = jnp.stack([d, swap_core(d)], axis=1)
    d = d.reshape(4 * count, 2 * ff)
    with jax.named_scope("weight_grads"):
        dw = jnp.dot(inputs.reshape(4 * count, rows).T, d, preferred_element_type=F32).astype(BF16)
        dw = lax.psum(dw, "x")
    with jax.named_scope("d_input"):
        di = lax.dot_general(d, w, (((1,), (1,)), ((), ())), preferred_element_type=F32).astype(BF16)
        di = relative(di.reshape(4, count, rows))
        di = jnp.sum(lax.all_to_all(di, "y", 0, 0).astype(F32), axis=0).astype(BF16)
        di = di.reshape(count, 8, width).transpose(1, 0, 2)
        di = jnp.sum(lax.all_to_all(di, "zl", 0, 0).astype(F32), axis=0).astype(BF16)
        di = swap_shard_y(di)
    return di, dw[:, :ff], dw[:, ff:]


def solution(mesh):
    fine = Mesh(mesh.devices.reshape([SIZES[a] for a in AXES]), AXES)
    in_specs = (P(ROWS, COLS), P(ROWS, COLS), P(ROWS, COLS), P(SHARD, COLS), P(SHARD, COLS))
    out_specs = (P(ROWS, COLS), P(SHARD, COLS), P(SHARD, COLS))
    return jax.shard_map(shards, mesh=fine, in_specs=in_specs, out_specs=out_specs, check_vma=False)
```

time: 833 us -> 228 us (0.27)
  waiting for transfers between devices: 722 us -> 61.2 us
  blocking collectives: 37.3 us -> 71.4 us
  starting transfers between devices: 34.8 us -> 61.5 us
    all_gather x3 -> x0, waiting for transfers between devices: 455 us -> none  [the longest x1 187 us: shards(): inputs = lax.all_gather(local_inputs, 'tensor', axis=1, tiled=True)]
    unnamed x6 -> x1, waiting for transfers between devices: 153 us -> 0.02 us
    psum x1, waiting for transfers between devices: 114 us -> 14.8 us  [shards(): dw = lax.psum(dw, 'x')]
    all_to_all x0 -> x3, blocking collectives: none -> 71.4 us  [the longest x1 32.4 us: shards(): lax.all_to_all(di, 'zl', 0, 0).astype(F32)]
    ppermute x0 -> x6, starting transfers between devices: none -> 57.4 us  [permute(): return lax.ppermute(value, axes if len(axes) > 1 else axes[0], pairs)]
    ppermute x0 -> x6, waiting for transfers between devices: none -> 40.6 us  [permute(): return lax.ppermute(value, axes if len(axes) > 1 else axes[0], pairs)]
    all_gather x2 -> x0, blocking collectives: 37.3 us -> none  [the longest x1 18.8 us: shards(): lax.all_gather(d_up, 'shard', axis=0, tiled=True)]
    all_to_all x1, starting transfers between devices: 34.6 us -> 4.08 us  [spread(): lax.all_to_all(jnp.broadcast_to(value[None], (n,) + value.shape), axis, 0...]
  transfers between devices with their start and end apart: 6 -> 8, of which waited for: 5 -> 8; matrix products, arithmetic and copies ran while one was open for 2% -> 3% of each run, Pallas kernels for 0% -> 0%
where the time goes in v1:
time: 228 us; the launch traced here: 227 us
  blocking collectives  71.4 us (31%)
  starting transfers between devices  61.5 us (27%)
  waiting for transfers between devices  61.2 us (27%)
  between operations  14.2 us (6%)
  matrix products  8.35 us (4%)
  local copies, waits for them, and re-layouts  8.01 us (4%)
    ppermute x6, starting transfers between devices, permute(): return lax.ppermute(value, axes if len(axes) > 1 else axes[0], pairs)  57.4 us
    ppermute x6, waiting for transfers between devices, permute(): return lax.ppermute(value, axes if len(axes) > 1 else axes[0], pairs)  40.6 us
    all_to_all x1, blocking collectives, shards(): lax.all_to_all(di, 'zl', 0, 0).astype(F32)  32.4 us
    all_to_all x1, blocking collectives, spread(): lax.all_to_all(jnp.broadcast_to(value[None], (n,) + value.shape), axis, 0...  22.8 us
    all_to_all x1, blocking collectives, shards(): di = jnp.sum(lax.all_to_all(di, 'y', 0, 0).astype(F32), axis=0).astype(BF16)  16.2 us
    psum x1, waiting for transfers between devices, shards(): dw = lax.psum(dw, 'x')  14.8 us
    all_to_all x1, waiting for transfers between devices, spread(): lax.all_to_all(jnp.broadcast_to(value[None], (n,) + value.shape), axis, 0...  5.77 us
  transfers between devices with their start and end apart: 8, of which 8 were waited for; matrix products, arithmetic and copies ran while one was open for 3% of the time, Pallas kernels for 0%

profile of v1, /device:TPU:25, one launch (start us, length us, event | category | flops | bytes accessed | tf_op | source)
XLA Modules:
  0.0 226.7 jit_solution(2050595942325906496)
XLA Ops:
  7.2 0.8 multiply_convert_fusion
  8.0 16.1 %collective-permute-start = (bf16[128,128]{1,0:T(8,128)(2,1)S(1)}, bf16[128,128]{1,0:T(8,128)(2,1)S(1)}, u32[]{:S(2)}, u32[]{:S(2)}) collective-permute-start(bf16[128,128]{1,0:T(8,128)(2,1)S(1)} %multiply_convert_fusion), channel_id=1, source_target_pairs={{0,0},{8,32},{16,64},{24,96},{32,8},{40,40},{48,72},{56,104},{64,1... | collective-permute-start | bytes 98312 | tf_op jit(solution)/shard_map/gather_inputs/ppermute | solution.py:23
  24.1 1.4 collective-permute-done
  25.6 22.8 %all_to_all.20 = bf16[8,128,128]{2,1,0:T(8,128)(2,1)S(1)} all-to-all(bf16[8,128,128]{2,1,0:T(8,128)(2,1)S(1)} %broadcast_in_dim.6), channel_id=1, replica_groups=mesh['x'=4,'zh'=2,'c'=2,'y'=4,'zl'=8] {'zl'}, dimensions={0} | all-to-all | bytes 524288 | tf_op jit(solution)/shard_map/gather_inputs/all_to_all | solution.py:44
  48.4 0.2 copy.18
  48.8 1.1 broadcast_in_dim.15
  49.9 4.1 %all-to-all-start.1 = ((bf16[4,128,1024]{2,1,0:T(8,128)(2,1)}), bf16[4,128,1024]{2,1,0:T(8,128)(2,1)S(1)}, u32[]{:S(2)}, u32[]{:S(2)}) async-start(bf16[4,128,1024]{2,1,0:T(8,128)(2,1)} %broadcast_in_dim.15), calls=%async_computation.1 | async-start | bytes 2097152 | tf_op jit(solution)/shard_map/gather_inputs/all_to_all | solution.py:44
  54.0 1.1 constant_dynamic-update-slice_fusion.1
  55.1 1.1 constant_dynamic-update-slice_fusion
  56.2 5.8 %all-to-all-done.1 = bf16[4,128,1024]{2,1,0:T(8,128)(2,1)S(1)} async-done(((bf16[4,128,1024]{2,1,0:T(8,128)(2,1)}), bf16[4,128,1024]{2,1,0:T(8,128)(2,1)S(1)}, u32[]{:S(2)}, u32[]{:S(2)}) %all-to-all-start.1) | async-done | bytes 1048608 | tf_op jit(solution)/shard_map/gather_inputs/all_to_all | solution.py:44
  62.2 2.9 %fusion = f32[2,2,128,1024]{3,2,1,0:T(8,128)S(1)} fusion(bf16[2,2,128,1024]{3,2,1,0:T(8,128)(2,1)S(1)} %bitcast.42, bf16[1024,1024]{1,0:T(8,128)(2,1)} %constant_dynamic-update-slice_fusion), kind=kOutput, calls=%fused_computation | convolution fusion | flops 1073741824 | bytes 5242880 | tf_op jit(solution)/shard_map/partial_gate_up/dot_general | solution.py:64
  65.2 8.9 %collective-permute-start.1 = (bf16[2,128,1024]{2,1,0:T(8,128)(2,1)S(1)}, bf16[2,128,1024]{2,1,0:T(8,128)(2,1)S(1)}, u32[]{:S(2)}, u32[]{:S(2)}) collective-permute-start(bf16[2,128,1024]{2,1,0:T(8,128)(2,1)S(1)} %fusion.3), channel_id=1, source_target_pairs={{0,32},{32,0},{1,33},{33,1},{2,34},{34,2},{3,35},{35,3},{4,36},{36... | collective-permute-start | bytes 1572872 | tf_op jit(solution)/shard_map/core_sum/ppermute | solution.py:23
  74.1 1.5 collective-permute-done.1
  75.6 0.2 fusion.2
  75.8 9.0 %collective-permute-start.2 = (bf16[128,1024]{1,0:T(8,128)(2,1)S(1)}, bf16[128,1024]{1,0:T(8,128)(2,1)S(1)}, u32[]{:S(2)}, u32[]{:S(2)}) collective-permute-start(bf16[128,1024]{1,0:T(8,128)(2,1)S(1)} %fusion.10), channel_id=1, source_target_pairs={{0,64},{64,0},{1,65},{65,1},{2,66},{66,2},{3,67},{67,3},{4,68},{68... | collective-permute-start | bytes 786440 | tf_op jit(solution)/shard_map/half_sum/ppermute | solution.py:23
  84.8 15.0 %collective-permute-done.2 = bf16[128,1024]{1,0:T(8,128)(2,1)S(1)} collective-permute-done((bf16[128,1024]{1,0:T(8,128)(2,1)S(1)}, bf16[128,1024]{1,0:T(8,128)(2,1)S(1)}, u32[]{:S(2)}, u32[]{:S(2)}) %collective-permute-start.2) | collective-permute-done | bytes 262176 | tf_op jit(solution)/shard_map/half_sum/ppermute | solution.py:23
  100.1 9.0 %collective-permute-start.3 = (bf16[128,1024]{1,0:T(8,128)(2,1)S(1)}, bf16[128,1024]{1,0:T(8,128)(2,1)S(1)}, u32[]{:S(2)}, u32[]{:S(2)}) collective-permute-start(bf16[128,1024]{1,0:T(8,128)(2,1)S(1)} %get-tuple-element.18), channel_id=1, source_target_pairs={{0,64},{64,0},{1,65},{65,1},{2,66},{66,2},{3,67},{67,3},{4,68},{68... | collective-permute-start | bytes 786440 | tf_op jit(solution)/shard_map/d_half/ppermute | solution.py:23
  109.1 15.1 %collective-permute-done.3 = bf16[128,1024]{1,0:T(8,128)(2,1)S(1)} collective-permute-done((bf16[128,1024]{1,0:T(8,128)(2,1)S(1)}, bf16[128,1024]{1,0:T(8,128)(2,1)S(1)}, u32[]{:S(2)}, u32[]{:S(2)}) %collective-permute-start.3) | collective-permute-done | bytes 262176 | tf_op jit(solution)/shard_map/d_half/ppermute | solution.py:23
  124.3 4.5 %collective-permute-start.4 = (bf16[2,128,1024]{2,1,0:T(8,128)(2,1)S(1)}, bf16[2,128,1024]{2,1,0:T(8,128)(2,1)S(1)}, u32[]{:S(2)}, u32[]{:S(2)}) collective-permute-start(bf16[2,128,1024]{2,1,0:T(8,128)(2,1)S(1)} %get-tuple-element.16), channel_id=1, source_target_pairs={{0,32},{32,0},{1,33},{33,1},{2,34},{34,2},{3,35},{35,3},{4,36},{36... | collective-permute-start | bytes 1572872 | tf_op jit(solution)/shard_map/d_core/ppermute | solution.py:23
  128.9 1.5 collective-permute-done.4
  130.6 2.6 %convolution_convert_fusion = bf16[1024,1024]{1,0:T(8,128)(2,1)} fusion(bf16[512,1024]{1,0:T(8,128)(2,1)S(1)} %bitcast.43, bf16[512,1024]{1,0:T(8,128)(2,1)S(1)} %bitcast.44), kind=kOutput, calls=%fused_computation.2 | convolution fusion | flops 1074790400 | bytes 4194304 | tf_op jit(solution)/shard_map/weight_grads/dot_general | solution.py:83
  133.2 2.9 %convolution_convert_fusion.1 = bf16[512,1024]{1,0:T(8,128)(2,1)S(1)} fusion(bf16[512,1024]{1,0:T(8,128)(2,1)S(1)} %bitcast.45, bf16[1024,1024]{1,0:T(8,128)(2,1)} %constant_dynamic-update-slice_fusion), kind=kOutput, calls=%fused_computation.3 | convolution fusion | flops 1074266112 | bytes 4194304 | tf_op jit(solution)/shard_map/d_input/dot_general | solution.py:86
  136.3 16.2 %all_to_all.21 = bf16[4,128,1024]{2,1,0:T(8,128)(2,1)S(1)} all-to-all(bf16[4,128,1024]{2,1,0:T(8,128)(2,1)S(1)} %pad_maximum_fusion.2), channel_id=1, replica_groups=mesh['x'=4,'zh'=2,'c'=2,'y'=4,'zl'=8] {'y'}, dimensions={0} | all-to-all | bytes 2097152 | tf_op jit(solution)/shard_map/d_input/all_to_all | solution.py:88
  152.5 0.2 reduce_sum.24
  152.7 0.2 copy.22
  152.9 0.2 copy.23
  153.1 32.4 %all_to_all.22 = bf16[8,128,128]{2,1,0:T(8,128)(2,1)S(1)} all-to-all(bf16[8,128,128]{2,1,0:T(8,128)(2,1)S(1)} %copy.23), channel_id=1, replica_groups=mesh['x'=4,'zh'=2,'c'=2,'y'=4,'zl'=8] {'zl'}, dimensions={0} | all-to-all | bytes 524288 | tf_op jit(solution)/shard_map/d_input/all_to_all | solution.py:90
  185.5 9.9 %collective-permute-start.5 = (bf16[128,128]{1,0:T(8,128)(2,1)S(1)}, bf16[128,128]{1,0:T(8,128)(2,1)S(1)}, u32[]{:S(2)}, u32[]{:S(2)}) collective-permute-start(bf16[128,128]{1,0:T(8,128)(2,1)S(1)} %reduce_sum.25), channel_id=1, source_target_pairs={{0,0},{8,32},{16,64},{24,96},{32,8},{40,40},{48,72},{56,104},{64,1... | collective-permute-start | bytes 98312 | tf_op jit(solution)/shard_map/d_input/ppermute | solution.py:23
  195.4 6.0 %collective-permute-done.5 = bf16[128,128]{1,0:T(8,128)(2,1)S(1)} collective-permute-done((bf16[128,128]{1,0:T(8,128)(2,1)S(1)}, bf16[128,128]{1,0:T(8,128)(2,1)S(1)}, u32[]{:S(2)}, u32[]{:S(2)}) %collective-permute-start.5) | collective-permute-done | bytes 32800 | tf_op jit(solution)/shard_map/d_input/ppermute | solution.py:23
  201.4 14.8 %all-reduce.2.cloned.1.call-done = bf16[1024,1024]{1,0:T(8,128)(2,1)} async-done(((bf16[1024,1024]{1,0:T(8,128)(2,1)}), bf16[1024,1024]{1,0:T(8,128)(2,1)}) %all-reduce.2.cloned.1.call-update) | async-done | bytes 2097168 | tf_op jit(solution)/shard_map/weight_grads/psum | solution.py:84
  216.2 3.0 %fusion.13 = (bf16[1024,512]{1,0:T(8,128)(2,1)}, bf16[1024,512]{1,0:T(8,128)(2,1)}) fusion(bf16[1024,1024]{1,0:T(8,128)(2,1)} %all-reduce.2.cloned.1.call-done), kind=kLoop, calls=%fused_computation.38 | loop fusion | bytes 4194304 | tf_op jit(solution)/shard_map/slice | solution.py:92
  219.2 0.6 copy.29
  (23 shorter events, 1.3 us)
Async XLA Ops:
  8.0 17.6 %collective-permute-start = (bf16[128,128]{1,0:T(8,128)(2,1)S(1)}, bf16[128,128]{1,0:T(8,128)(2,1)S(1)}, u32[]{:S(2)}, u32[]{:S(2)}) collective-permute-start(bf16[128,128]{1,0:T(8,128)(2,1)S(1)} %multiply_convert_fusion), channel_id=1, source_target_pairs={{0,0},{8,32},{16,64},{24,96},{32,8},{40,40},{48,72},{56,104},{64,1... | collective-permute-start | bytes 98312 | tf_op jit(solution)/shard_map/gather_inputs/ppermute | solution.py:23
  48.6 5.3 %copy-start = (bf16[1024,512]{1,0:T(8,128)(2,1)S(1)}, bf16[1024,512]{1,0:T(8,128)(2,1)}, u32[]{:S(2)}) copy-start(bf16[1024,512]{1,0:T(8,128)(2,1)} %param.8) | copy-start | bytes 3145732
  49.9 5.2 %copy-start.1 = (bf16[1024,512]{1,0:T(8,128)(2,1)S(1)}, bf16[1024,512]{1,0:T(8,128)(2,1)}, u32[]{:S(2)}) copy-start(bf16[1024,512]{1,0:T(8,128)(2,1)} %param.9) | copy-start | bytes 3145732
  49.9 12.1 %all-to-all-start.1 = ((bf16[4,128,1024]{2,1,0:T(8,128)(2,1)}), bf16[4,128,1024]{2,1,0:T(8,128)(2,1)S(1)}, u32[]{:S(2)}, u32[]{:S(2)}) async-start(bf16[4,128,1024]{2,1,0:T(8,128)(2,1)} %broadcast_in_dim.15), calls=%async_computation.1 | async-start | bytes 2097152 | tf_op jit(solution)/shard_map/gather_inputs/all_to_all | solution.py:44
  54.0 162.2 %all-reduce.2.cloned.1.call-start = ((), (), s32[]{:S(2)}) async-start(), calls=%async_computation.4 | async-start | bytes 4194304 | tf_op jit(solution)/shard_map/weight_grads/psum | solution.py:84
  65.2 34.7 %copy-start.2 = (bf16[128,512]{1,0:T(8,128)(2,1)S(1)}, bf16[128,512]{1,0:T(8,128)(2,1)}, u32[]{:S(2)}) copy-start(bf16[128,512]{1,0:T(8,128)(2,1)} %param.7) | copy-start | bytes 393220
  65.2 10.4 %collective-permute-start.1 = (bf16[2,128,1024]{2,1,0:T(8,128)(2,1)S(1)}, bf16[2,128,1024]{2,1,0:T(8,128)(2,1)S(1)}, u32[]{:S(2)}, u32[]{:S(2)}) collective-permute-start(bf16[2,128,1024]{2,1,0:T(8,128)(2,1)S(1)} %fusion.3), channel_id=1, source_target_pairs={{0,32},{32,0},{1,33},{33,1},{2,34},{34,2},{3,35},{35,3},{4,36},{36... | collective-permute-start | bytes 1572872 | tf_op jit(solution)/shard_map/core_sum/ppermute | solution.py:23
  75.8 24.0 %collective-permute-start.2 = (bf16[128,1024]{1,0:T(8,128)(2,1)S(1)}, bf16[128,1024]{1,0:T(8,128)(2,1)S(1)}, u32[]{:S(2)}, u32[]{:S(2)}) collective-permute-start(bf16[128,1024]{1,0:T(8,128)(2,1)S(1)} %fusion.10), channel_id=1, source_target_pairs={{0,64},{64,0},{1,65},{65,1},{2,66},{66,2},{3,67},{67,3},{4,68},{68... | collective-permute-start | bytes 786440 | tf_op jit(solution)/shard_map/half_sum/ppermute | solution.py:23
  100.1 24.2 %collective-permute-start.3 = (bf16[128,1024]{1,0:T(8,128)(2,1)S(1)}, bf16[128,1024]{1,0:T(8,128)(2,1)S(1)}, u32[]{:S(2)}, u32[]{:S(2)}) collective-permute-start(bf16[128,1024]{1,0:T(8,128)(2,1)S(1)} %get-tuple-element.18), channel_id=1, source_target_pairs={{0,64},{64,0},{1,65},{65,1},{2,66},{66,2},{3,67},{67,3},{4,68},{68... | collective-permute-start | bytes 786440 | tf_op jit(solution)/shard_map/d_half/ppermute | solution.py:23
  124.3 6.1 %collective-permute-start.4 = (bf16[2,128,1024]{2,1,0:T(8,128)(2,1)S(1)}, bf16[2,128,1024]{2,1,0:T(8,128)(2,1)S(1)}, u32[]{:S(2)}, u32[]{:S(2)}) collective-permute-start(bf16[2,128,1024]{2,1,0:T(8,128)(2,1)S(1)} %get-tuple-element.16), channel_id=1, source_target_pairs={{0,32},{32,0},{1,33},{33,1},{2,34},{34,2},{3,35},{35,3},{4,36},{36... | collective-permute-start | bytes 1572872 | tf_op jit(solution)/shard_map/d_core/ppermute | solution.py:23
  185.5 15.9 %collective-permute-start.5 = (bf16[128,128]{1,0:T(8,128)(2,1)S(1)}, bf16[128,128]{1,0:T(8,128)(2,1)S(1)}, u32[]{:S(2)}, u32[]{:S(2)}) collective-permute-start(bf16[128,128]{1,0:T(8,128)(2,1)S(1)} %reduce_sum.25), channel_id=1, source_target_pairs={{0,0},{8,32},{16,64},{24,96},{32,8},{40,40},{48,72},{56,104},{64,1... | collective-permute-start | bytes 98312 | tf_op jit(solution)/shard_map/d_input/ppermute | solution.py:23
Sparse Core Ops, SparseCore 0:
  133.3 82.8 all-reduce.1

commit v2 on v1

--- a/solution.py
+++ b/solution.py
@@ -45,8 +45,15 @@
 
 
 def relative(blocks):
-    s = lax.axis_index("zh") * 2 + lax.axis_index("c")
-    return jnp.stack([lax.dynamic_index_in_dim(blocks, s ^ r, 0, keepdims=False) for r in range(4)])
+    zh, c = lax.axis_index("zh"), lax.axis_index("c")
+    picks = [(zh ^ r_zh) * 2 + (c ^ r_c) for r_c in range(2) for r_zh in range(2)]
+    return jnp.stack([lax.dynamic_index_in_dim(blocks, p, 0, keepdims=False) for p in picks])
+
+
+def absolute(blocks):
+    zh, c = lax.axis_index("zh"), lax.axis_index("c")
+    picks = [(c ^ c_to) * 2 + (zh ^ zh_to) for zh_to in range(2) for c_to in range(2)]
+    return jnp.stack([lax.dynamic_index_in_dim(blocks, p, 0, keepdims=False) for p in picks])
 
 
 def shards(quantized, scales, d_hidden, w_gate, w_up):
@@ -54,42 +61,62 @@
     ff = w_gate.shape[1]
     rows = w_gate.shape[0]
     local = (quantized.astype(F32) * scales).astype(BF16)
+    with jax.named_scope("d_hidden_half"):
+        far_hidden = swap_half(d_hidden)
     with jax.named_scope("gather_inputs"):
         held = spread(swap_shard_y(local), "zl")
+        held, far_hidden = lax.optimization_barrier((held, far_hidden))
+        grad_out = jnp.stack([d_hidden, far_hidden]).astype(F32)
         held = held.transpose(1, 0, 2).reshape(count, rows)
         held = spread(held, "y")
         inputs = relative(held)
+    with jax.named_scope("all_inputs"):
+        all_inputs = lax.all_gather(inputs, "x", axis=0)
     with jax.named_scope("partial_gate_up"):
         w = jnp.concatenate([w_gate, w_up], axis=1)
         parts = jnp.dot(inputs.reshape(4 * count, rows), w, preferred_element_type=F32)
         parts = parts.reshape(2, 2, count, 2 * ff)
     with jax.named_scope("core_sum"):
-        parts = parts[:, 0] + swap_core(parts[:, 1].astype(BF16)).astype(F32)
+        parts = parts[0] + swap_core(parts[1].astype(BF16)).astype(F32)
     with jax.named_scope("half_sum"):
-        pre = parts[0] + swap_half(parts[1].astype(BF16)).astype(F32)
+        other = swap_half(parts.astype(BF16)).astype(F32)
+        pre = parts + other[::-1]
     with jax.named_scope("elementwise"):
-        gate, up = pre[:, :ff], pre[:, ff:]
+        gate, up = pre[..., :ff], pre[..., ff:]
         sig = jax.nn.sigmoid(gate)
-        grad_out = d_hidden.astype(F32)
         d_gate = (grad_out * up * sig * (1.0 + gate * (1.0 - sig))).astype(BF16)
         d_up = (grad_out * gate * sig).astype(BF16)
-        d = jnp.concatenate([d_gate, d_up], axis=1)
-    with jax.named_scope("d_half"):
-        d = jnp.stack([d, swap_half(d)])
+        d = jnp.concatenate([d_gate, d_up], axis=-1)
+    with jax.named_scope("d_over_x"):
+        d_sent, all_inputs = lax.optimization_barrier((d, all_inputs))
+        d_all = lax.all_gather(d_sent, "x", axis=0)
     with jax.named_scope("d_core"):
-        d = jnp.stack([d, swap_core(d)], axis=1)
-    d = d.reshape(4 * count, 2 * ff)
-    with jax.named_scope("weight_grads"):
-        dw = jnp.dot(inputs.reshape(4 * count, rows).T, d, preferred_element_type=F32).astype(BF16)
-        dw = lax.psum(dw, "x")
+        d_own = jnp.stack([d, swap_core(d)])
     with jax.named_scope("d_input"):
-        di = lax.dot_general(d, w, (((1,), (1,)), ((), ())), preferred_element_type=F32).astype(BF16)
-        di = relative(di.reshape(4, count, rows))
+        di = lax.dot_general(
+            d_own.reshape(4 * count, 2 * ff), w, (((1,), (1,)), ((), ())), preferred_element_type=F32
+        ).astype(BF16)
+        di = absolute(di.reshape(4, count, rows))
         di = jnp.sum(lax.all_to_all(di, "y", 0, 0).astype(F32), axis=0).astype(BF16)
+        di_y = di
         di = di.reshape(count, 8, width).transpose(1, 0, 2)
         di = jnp.sum(lax.all_to_all(di, "zl", 0, 0).astype(F32), axis=0).astype(BF16)
         di = swap_shard_y(di)
-    return di, dw[:, :ff], dw[:, ff:]
+    with jax.named_scope("weight_grads"):
+        d_all, _ = lax.optimization_barrier((d_all, di_y))
+        d_far = swap_core(d_all)
+        mine = all_inputs[:, :2].reshape(8 * count, rows)
+        theirs = all_inputs[:, 2:].reshape(8 * count, rows)
+        d_all = d_all.reshape(8 * count, 2 * ff)
+        d_far = d_far.reshape(8 * count, 2 * ff)
+        grads = [
+            (
+                jnp.dot(mine.T, d_all[:, k : k + ff], preferred_element_type=F32)
+                + jnp.dot(theirs.T, d_far[:, k : k + ff], preferred_element_type=F32)
+            ).astype(BF16)
+            for k in (0, ff)
+        ]
+    return di, grads[0], grads[1]
 
 
 def solution(mesh):

time: 228 us -> 248 us (1.088); the launches traced: 227 us -> 244 us
  waiting for transfers between devices: 61.2 us -> 99.5 us
  blocking collectives: 71.4 us -> 40.6 us
  starting transfers between devices: 61.5 us -> 67.6 us
    all_gather x0 -> x2, waiting for transfers between devices: none -> 35.4 us  [the longest x1 22.8 us: shards(): d_all = lax.all_gather(d_sent, 'x', axis=0)]
    all_to_all x1 -> x0, blocking collectives: 22.8 us -> none  [spread(): lax.all_to_all(jnp.broadcast_to(value[None], (n,) + value.shape), axis, 0...]
    ppermute x6 -> x7, waiting for transfers between devices: 40.6 us -> 56.1 us  [permute(): return lax.ppermute(value, axes if len(axes) > 1 else axes[0], pairs)]
    psum x1 -> x0, waiting for transfers between devices: 14.8 us -> none  [shards(): dw = lax.psum(dw, 'x')]
    all_to_all x1 -> x2, starting transfers between devices: 4.08 us -> 14.8 us  [spread(): lax.all_to_all(jnp.broadcast_to(value[None], (n,) + value.shape), axis, 0...]
    all_to_all x1, blocking collectives: 32.4 us -> 24.1 us  [shards(): lax.all_to_all(di, 'zl', 0, 0).astype(F32)]
    ppermute x6 -> x7, starting transfers between devices: 57.4 us -> 52.8 us  [permute(): return lax.ppermute(value, axes if len(axes) > 1 else axes[0], pairs)]
    dot_general x2 -> x5, matrix products: 5.49 us -> 8.41 us  [the longest x2 4.56 us: shards(): jnp.dot(theirs.T, d_far[:, k:k + ff], preferred_element_type=F32)]
  transfers between devices with their start and end apart: 8 -> 11, of which waited for: 8 -> 9; matrix products, arithmetic and copies ran while one was open for 3% -> 4% of each run, Pallas kernels for 0% -> 0%
where the time goes in v2:
time: 248 us; the launch traced here: 244 us
  waiting for transfers between devices  99.5 us (40%)
  starting transfers between devices  67.6 us (27%)
  blocking collectives  40.6 us (16%)
  between operations  14.3 us (6%)
  matrix products  9.66 us (4%)
  local copies, waits for them, and re-layouts  8.2 us (3%)
  other arithmetic  4.16 us (2%)
    ppermute x7, waiting for transfers between devices, permute(): return lax.ppermute(value, axes if len(axes) > 1 else axes[0], pairs)  56.1 us
    ppermute x7, starting transfers between devices, permute(): return lax.ppermute(value, axes if len(axes) > 1 else axes[0], pairs)  52.8 us
    all_to_all x1, blocking collectives, shards(): lax.all_to_all(di, 'zl', 0, 0).astype(F32)  24.1 us
    all_gather x1, waiting for transfers between devices, shards(): d_all = lax.all_gather(d_sent, 'x', axis=0)  22.8 us
    all_to_all x1, blocking collectives, shards(): di = jnp.sum(lax.all_to_all(di, 'y', 0, 0).astype(F32), axis=0).astype(BF16)  16.5 us
    all_to_all x2, starting transfers between devices, spread(): lax.all_to_all(jnp.broadcast_to(value[None], (n,) + value.shape), axis, 0...  14.8 us
    all_gather x1, waiting for transfers between devices, shards(): all_inputs = lax.all_gather(inputs, 'x', axis=0)  12.6 us
    all_to_all x2, waiting for transfers between devices, spread(): lax.all_to_all(jnp.broadcast_to(value[None], (n,) + value.shape), axis, 0...  7.96 us
  transfers between devices with their start and end apart: 11, of which 9 were waited for; matrix products, arithmetic and copies ran while one was open for 4% of the time, Pallas kernels for 0%

profile of v2, /device:TPU:25, one launch (start us, length us, event | category | flops | bytes accessed | tf_op | source)
XLA Modules:
  0.0 244.0 jit_solution(15888864338041099462)
XLA Ops:
  7.2 0.8 multiply_convert_fusion
  8.0 16.1 %collective-permute-start = (bf16[128,128]{1,0:T(8,128)(2,1)S(1)}, bf16[128,128]{1,0:T(8,128)(2,1)S(1)}, u32[]{:S(2)}, u32[]{:S(2)}) collective-permute-start(bf16[128,128]{1,0:T(8,128)(2,1)S(1)} %multiply_convert_fusion), channel_id=1, source_target_pairs={{0,0},{8,32},{16,64},{24,96},{32,8},{40,40},{48,72},{56,104},{64,1... | collective-permute-start | bytes 98312 | tf_op jit(solution)/shard_map/gather_inputs/ppermute | solution.py:23
  24.1 1.4 collective-permute-done
  25.7 0.7 broadcast_in_dim.6
  26.4 10.9 %all-to-all-start = ((bf16[8,128,128]{1,2,0:T(8,128)(2,1)}), bf16[8,128,128]{1,2,0:T(8,128)(2,1)S(1)}, u32[]{:S(2)}, u32[]{:S(2)}) async-start(bf16[8,128,128]{1,2,0:T(8,128)(2,1)} %broadcast_in_dim.6), calls=%async_computation | async-start | bytes 524288 | tf_op jit(solution)/shard_map/gather_inputs/all_to_all | solution.py:44
  37.3 1.9 collective-permute-start.1
  39.2 14.6 %collective-permute-done.1 = bf16[128,512]{1,0:T(8,128)(2,1)S(1)} collective-permute-done((bf16[128,512]{1,0:T(8,128)(2,1)}, bf16[128,512]{1,0:T(8,128)(2,1)S(1)}, u32[]{:S(2)}, u32[]{:S(2)}) %collective-permute-start.1) | collective-permute-done | bytes 131104 | tf_op jit(solution)/shard_map/d_hidden_half/ppermute | solution.py:23
  54.0 1.1 broadcast_in_dim.15
  55.1 3.9 %all-to-all-start.1 = ((bf16[4,128,1024]{2,1,0:T(8,128)(2,1)}), bf16[4,128,1024]{2,1,0:T(8,128)(2,1)S(1)}, u32[]{:S(2)}, u32[]{:S(2)}) async-start(bf16[4,128,1024]{2,1,0:T(8,128)(2,1)} %broadcast_in_dim.15), calls=%async_computation.1 | async-start | bytes 2097152 | tf_op jit(solution)/shard_map/gather_inputs/all_to_all | solution.py:44
  59.0 8.0 %all-to-all-done.1 = bf16[4,128,1024]{2,1,0:T(8,128)(2,1)S(1)} async-done(((bf16[4,128,1024]{2,1,0:T(8,128)(2,1)}), bf16[4,128,1024]{2,1,0:T(8,128)(2,1)S(1)}, u32[]{:S(2)}, u32[]{:S(2)}) %all-to-all-start.1) | async-done | bytes 1048608 | tf_op jit(solution)/shard_map/gather_inputs/all_to_all | solution.py:44
  67.1 1.1 pad_maximum_fusion
  69.8 1.2 fusion.14
  71.1 15.0 %collective-permute-start.2 = (bf16[2,128,1024]{2,1,0:T(8,128)(2,1)S(1)}, bf16[2,128,1024]{2,1,0:T(8,128)(2,1)S(1)}, u32[]{:S(2)}, u32[]{:S(2)}) collective-permute-start(bf16[2,128,1024]{2,1,0:T(8,128)(2,1)S(1)} %bitcast.43), channel_id=1, source_target_pairs={{0,32},{32,0},{1,33},{33,1},{2,34},{34,2},{3,35},{35,3},{4,36},{36... | collective-permute-start | bytes 1572872 | tf_op jit(solution)/shard_map/core_sum/ppermute | solution.py:23
  86.2 1.4 collective-permute-done.2
  87.8 7.8 %collective-permute-start.3 = (bf16[2,128,1024]{2,1,0:T(8,128)(2,1)S(1)}, bf16[2,128,1024]{2,1,0:T(8,128)(2,1)S(1)}, u32[]{:S(2)}, u32[]{:S(2)}) collective-permute-start(bf16[2,128,1024]{2,1,0:T(8,128)(2,1)S(1)} %fusion.6), channel_id=1, source_target_pairs={{0,64},{64,0},{1,65},{65,1},{2,66},{66,2},{3,67},{67,3},{4,68},{68... | collective-permute-start | bytes 1572872 | tf_op jit(solution)/shard_map/half_sum/ppermute | solution.py:23
  95.6 27.4 %collective-permute-done.3 = bf16[2,128,1024]{2,1,0:T(8,128)(2,1)S(1)} collective-permute-done((bf16[2,128,1024]{2,1,0:T(8,128)(2,1)S(1)}, bf16[2,128,1024]{2,1,0:T(8,128)(2,1)S(1)}, u32[]{:S(2)}, u32[]{:S(2)}) %collective-permute-start.3) | collective-permute-done | bytes 524320 | tf_op jit(solution)/shard_map/half_sum/ppermute | solution.py:23
  124.4 0.9 fusion.12
  125.3 12.6 %all-gather.5.cloned.1.call-done = bf16[16,128,1024]{2,1,0:T(8,128)(2,1)} async-done(((bf16[4,128,1024]{2,1,0:T(8,128)(2,1)}), bf16[16,128,1024]{2,1,0:T(8,128)(2,1)}) %all-gather.5.cloned.1.call-update) | async-done | bytes 4194320 | tf_op jit(solution)/shard_map/all_inputs/all_gather | solution.py:74
  137.9 2.6 %collective-permute-start.4 = (bf16[2,128,1024]{2,1,0:T(8,128)(2,1)}, bf16[2,128,1024]{2,1,0:T(8,128)(2,1)S(1)}, u32[]{:S(2)}, u32[]{:S(2)}) collective-permute-start(bf16[2,128,1024]{2,1,0:T(8,128)(2,1)} %get-tuple-element.11), channel_id=1, source_target_pairs={{0,32},{32,0},{1,33},{33,1},{2,34},{34,2},{3,35},{35,3},{4,36},{36... | collective-permute-start | bytes 1572872 | tf_op jit(solution)/shard_map/d_core/ppermute | solution.py:23
  140.5 1.7 collective-permute-done.4
  142.4 1.3 convolution_convert_fusion
  143.9 16.5 %all_to_all.20 = bf16[4,128,1024]{2,1,0:T(8,128)(2,1)S(1)} all-to-all(bf16[4,128,1024]{2,1,0:T(8,128)(2,1)S(1)} %pad_maximum_fusion.2), channel_id=1, replica_groups=mesh['x'=4,'zh'=2,'c'=2,'y'=4,'zl'=8] {'y'}, dimensions={0} | all-to-all | bytes 2097152 | tf_op jit(solution)/shard_map/d_input/all_to_all | solution.py:100
  160.5 22.8 %all-gather.7.cloned.1.call-done = bf16[8,128,1024]{2,1,0:T(8,128)(2,1)} async-done(((bf16[2,128,1024]{2,1,0:T(8,128)(2,1)}), bf16[8,128,1024]{2,1,0:T(8,128)(2,1)}) %all-gather.7.cloned.1.call-update) | async-done | bytes 2097168 | tf_op jit(solution)/shard_map/d_over_x/all_gather | solution.py:92
  183.3 2.6 %collective-permute-start.6 = (bf16[4,2,128,1024]{3,2,1,0:T(8,128)(2,1)}, bf16[4,2,128,1024]{3,2,1,0:T(8,128)(2,1)S(1)}, u32[]{:S(2)}, u32[]{:S(2)}) collective-permute-start(bf16[4,2,128,1024]{3,2,1,0:T(8,128)(2,1)} %bitcast.48), channel_id=1, source_target_pairs={{0,32},{32,0},{1,33},{33,1},{2,34},{34,2},{3,35},{35,3},{4,36},{36... | collective-permute-start | bytes 6291464 | tf_op jit(solution)/shard_map/weight_grads/ppermute | solution.py:23
  186.3 24.1 %all_to_all.21 = bf16[8,128,128]{2,1,0:T(8,128)(2,1)S(1)} all-to-all(bf16[8,128,128]{2,1,0:T(8,128)(2,1)S(1)} %copy.18), channel_id=1, replica_groups=mesh['x'=4,'zh'=2,'c'=2,'y'=4,'zl'=8] {'zl'}, dimensions={0} | all-to-all | bytes 524288 | tf_op jit(solution)/shard_map/d_input/all_to_all | solution.py:103
  210.4 6.8 %collective-permute-start.5 = (bf16[128,128]{1,0:T(8,128)(2,1)S(1)}, bf16[128,128]{1,0:T(8,128)(2,1)S(1)}, u32[]{:S(2)}, u32[]{:S(2)}) collective-permute-start(bf16[128,128]{1,0:T(8,128)(2,1)S(1)} %reduce_sum.25), channel_id=1, source_target_pairs={{0,0},{8,32},{16,64},{24,96},{32,8},{40,40},{48,72},{56,104},{64,1... | collective-permute-start | bytes 98312 | tf_op jit(solution)/shard_map/d_input/ppermute | solution.py:23
  217.2 9.5 %collective-permute-done.5 = bf16[128,128]{1,0:T(8,128)(2,1)S(1)} collective-permute-done((bf16[128,128]{1,0:T(8,128)(2,1)S(1)}, bf16[128,128]{1,0:T(8,128)(2,1)S(1)}, u32[]{:S(2)}, u32[]{:S(2)}) %collective-permute-start.5) | collective-permute-done | bytes 32800 | tf_op jit(solution)/shard_map/d_input/ppermute | solution.py:23
  226.7 2.7 %fusion.13 = (bf16[4,2,128,1024]{3,2,1,0:T(8,128)(2,1)S(1)}, bf16[4,2,128,1024]{3,2,1,0:T(8,128)(2,1)S(1)}) fusion(bf16[4,4,128,1024]{3,2,1,0:T(8,128)(2,1)} %bitcast.33), kind=kLoop, calls=%fused_computation.38 | loop fusion | bytes 8388608 | tf_op jit(solution)/shard_map/weight_grads/slice | solution.py:109
  229.5 1.3 fusion.1
  230.7 1.3 fusion.4
  232.0 2.3 add_convert_fusion
  234.3 2.3 add_convert_fusion.1
  (39 shorter events, 5.0 us)
Async XLA Ops:
  8.0 17.6 %collective-permute-start = (bf16[128,128]{1,0:T(8,128)(2,1)S(1)}, bf16[128,128]{1,0:T(8,128)(2,1)S(1)}, u32[]{:S(2)}, u32[]{:S(2)}) collective-permute-start(bf16[128,128]{1,0:T(8,128)(2,1)S(1)} %multiply_convert_fusion), channel_id=1, source_target_pairs={{0,0},{8,32},{16,64},{24,96},{32,8},{40,40},{48,72},{56,104},{64,1... | collective-permute-start | bytes 98312 | tf_op jit(solution)/shard_map/gather_inputs/ppermute | solution.py:23
  26.4 27.4 %all-to-all-start = ((bf16[8,128,128]{1,2,0:T(8,128)(2,1)}), bf16[8,128,128]{1,2,0:T(8,128)(2,1)S(1)}, u32[]{:S(2)}, u32[]{:S(2)}) async-start(bf16[8,128,128]{1,2,0:T(8,128)(2,1)} %broadcast_in_dim.6), calls=%async_computation | async-start | bytes 524288 | tf_op jit(solution)/shard_map/gather_inputs/all_to_all | solution.py:44
  37.3 16.5 %collective-permute-start.1 = (bf16[128,512]{1,0:T(8,128)(2,1)}, bf16[128,512]{1,0:T(8,128)(2,1)S(1)}, u32[]{:S(2)}, u32[]{:S(2)}) collective-permute-start(bf16[128,512]{1,0:T(8,128)(2,1)} %param.7), channel_id=1, source_target_pairs={{0,64},{64,0},{1,65},{65,1},{2,66},{66,2},{3,67},{67,3},{4,68},{68... | collective-permute-start | bytes 393224 | tf_op jit(solution)/shard_map/d_hidden_half/ppermute | solution.py:23
  55.1 11.9 %all-to-all-start.1 = ((bf16[4,128,1024]{2,1,0:T(8,128)(2,1)}), bf16[4,128,1024]{2,1,0:T(8,128)(2,1)S(1)}, u32[]{:S(2)}, u32[]{:S(2)}) async-start(bf16[4,128,1024]{2,1,0:T(8,128)(2,1)} %broadcast_in_dim.15), calls=%async_computation.1 | async-start | bytes 2097152 | tf_op jit(solution)/shard_map/gather_inputs/all_to_all | solution.py:44
  59.0 78.9 %all-gather.5.cloned.1.call-start = ((), (), s32[]{:S(2)}) async-start(), calls=%async_computation.4 | async-start | bytes 5242880 | tf_op jit(solution)/shard_map/all_inputs/all_gather | solution.py:74
  67.1 1.6 copy-start.1
  68.2 1.3 copy-start.2
  68.2 1.6 copy-start
  68.2 115.1 %all-gather.7.cloned.1.call-start = ((), (), s32[]{:S(2)}) async-start(), calls=%async_computation.5 | async-start | bytes 2621440 | tf_op jit(solution)/shard_map/d_over_x/all_gather | solution.py:92
  69.6 1.4 copy-start.3
  71.1 16.5 %collective-permute-start.2 = (bf16[2,128,1024]{2,1,0:T(8,128)(2,1)S(1)}, bf16[2,128,1024]{2,1,0:T(8,128)(2,1)S(1)}, u32[]{:S(2)}, u32[]{:S(2)}) collective-permute-start(bf16[2,128,1024]{2,1,0:T(8,128)(2,1)S(1)} %bitcast.43), channel_id=1, source_target_pairs={{0,32},{32,0},{1,33},{33,1},{2,34},{34,2},{3,35},{35,3},{4,36},{36... | collective-permute-start | bytes 1572872 | tf_op jit(solution)/shard_map/core_sum/ppermute | solution.py:23
  87.8 35.3 %collective-permute-start.3 = (bf16[2,128,1024]{2,1,0:T(8,128)(2,1)S(1)}, bf16[2,128,1024]{2,1,0:T(8,128)(2,1)S(1)}, u32[]{:S(2)}, u32[]{:S(2)}) collective-permute-start(bf16[2,128,1024]{2,1,0:T(8,128)(2,1)S(1)} %fusion.6), channel_id=1, source_target_pairs={{0,64},{64,0},{1,65},{65,1},{2,66},{66,2},{3,67},{67,3},{4,68},{68... | collective-permute-start | bytes 1572872 | tf_op jit(solution)/shard_map/half_sum/ppermute | solution.py:23
  123.2 0.9 copy-start.5
  124.4 18.0 %copy-start.4 = (bf16[1024,1024]{1,0:T(8,128)(2,1)S(1)}, bf16[1024,1024]{1,0:T(8,128)(2,1)}, u32[]{:S(2)}) copy-start(bf16[1024,1024]{1,0:T(8,128)(2,1)} %copy-done.3) | copy-start | bytes 6291460
  137.9 4.3 %collective-permute-start.4 = (bf16[2,128,1024]{2,1,0:T(8,128)(2,1)}, bf16[2,128,1024]{2,1,0:T(8,128)(2,1)S(1)}, u32[]{:S(2)}, u32[]{:S(2)}) collective-permute-start(bf16[2,128,1024]{2,1,0:T(8,128)(2,1)} %get-tuple-element.11), channel_id=1, source_target_pairs={{0,32},{32,0},{1,33},{33,1},{2,34},{34,2},{3,35},{35,3},{4,36},{36... | collective-permute-start | bytes 1572872 | tf_op jit(solution)/shard_map/d_core/ppermute | solution.py:23
  183.3 48.7 %collective-permute-start.6 = (bf16[4,2,128,1024]{3,2,1,0:T(8,128)(2,1)}, bf16[4,2,128,1024]{3,2,1,0:T(8,128)(2,1)S(1)}, u32[]{:S(2)}, u32[]{:S(2)}) collective-permute-start(bf16[4,2,128,1024]{3,2,1,0:T(8,128)(2,1)} %bitcast.48), channel_id=1, source_target_pairs={{0,32},{32,0},{1,33},{33,1},{2,34},{34,2},{3,35},{35,3},{4,36},{36... | collective-permute-start | bytes 6291464 | tf_op jit(solution)/shard_map/weight_grads/ppermute | solution.py:23
  210.4 19.0 %copy-start.6 = (bf16[8,128,1024]{2,1,0:T(8,128)(2,1)S(1)}, bf16[8,128,1024]{2,1,0:T(8,128)(2,1)}, u32[]{:S(2)}) copy-start(bf16[8,128,1024]{2,1,0:T(8,128)(2,1)} %all-gather.7.cloned.1.call-done) | copy-start | bytes 6291460
  210.4 16.3 %collective-permute-start.5 = (bf16[128,128]{1,0:T(8,128)(2,1)S(1)}, bf16[128,128]{1,0:T(8,128)(2,1)S(1)}, u32[]{:S(2)}, u32[]{:S(2)}) collective-permute-start(bf16[128,128]{1,0:T(8,128)(2,1)S(1)} %reduce_sum.25), channel_id=1, source_target_pairs={{0,0},{8,32},{16,64},{24,96},{32,8},{40,40},{48,72},{56,104},{64,1... | collective-permute-start | bytes 98312 | tf_op jit(solution)/shard_map/d_input/ppermute | solution.py:23
Sparse Core Ops, SparseCore 0:
  68.3 69.5 all-gather.4
  140.6 42.6 all-gather.6

commit v3 on v1

v3 whole, which is shorter than its diff:
```python
import jax
import jax.numpy as jnp
import numpy as np
from jax import lax
from jax.experimental import pallas as pl
from jax.experimental.pallas import tpu as pltpu
from jax.sharding import Mesh, PartitionSpec as P

AXES = ("x", "zh", "c", "y", "zl")
SIZES = {"x": 4, "zh": 2, "c": 2, "y": 4, "zl": 8}
ROWS = ("x", "zh", "c")
COLS = ("y", "zl")
SHARD = ("zh", "c")
F32 = jnp.float32
BF16 = jnp.bfloat16


def permute(value, axes, target):
    sizes = [SIZES[a] for a in axes]
    pairs = []
    for i in range(int(np.prod(sizes))):
        at = dict(zip(axes, map(int, np.unravel_index(i, sizes))))
        to = target(at)
        pairs.append((i, int(np.ravel_multi_index([to[a] for a in axes], sizes))))
    return lax.ppermute(value, axes if len(axes) > 1 else axes[0], pairs)


def swap_half_y(value):
    return permute(
        value, ("zh", "y"), lambda d: {"zh": d["y"] // 2, "y": d["zh"] * 2 + d["y"] % 2}
    )


def swap_core(value):
    return permute(value, ("c",), lambda d: {"c": 1 - d["c"]})


def swap_half(value):
    return permute(value, ("zh",), lambda d: {"zh": 1 - d["zh"]})


def step_outer(value, k):
    return permute(value, ("x",), lambda d: {"x": (d["x"] + k) % 4})


def spread(value, axis):
    n = SIZES[axis]
    return lax.all_to_all(jnp.broadcast_to(value[None], (n,) + value.shape), axis, 0, 0)


VMEM = pl.BlockSpec(memory_space=pltpu.VMEM)
SMEM = pl.BlockSpec(memory_space=pltpu.SMEM)
PARAMS = pltpu.CompilerParams(vmem_limit_bytes=32 * 1024 * 1024)


def partial_kernel(core_ref, x_ref, g0_ref, u0_ref, g1_ref, u1_ref, full_ref, send_ref):
    core = core_ref[0]
    ff = g0_ref.shape[1]
    for a in range(2):
        near, far = x_ref[2 * a + core], x_ref[2 * a + 1 - core]
        for k, (w0, w1) in enumerate(((g0_ref, g1_ref), (u0_ref, u1_ref))):
            total = jnp.dot(near, w0[...], preferred_element_type=F32)
            total = total + jnp.dot(far, w1[...], preferred_element_type=F32)
            full_ref[a, :, k * ff : (k + 1) * ff] = total
            send_ref[a, :, k * ff : (k + 1) * ff] = total.astype(BF16)


def partial_gate_up(core, x, weights):
    count, ff = x.shape[1], weights[0].shape[1]
    flops = 2 * 4 * count * x.shape[2] * 2 * ff
    return pl.pallas_call(
        partial_kernel,
        out_shape=(
            jax.ShapeDtypeStruct((2, count, 2 * ff), F32),
            jax.ShapeDtypeStruct((2, count, 2 * ff), BF16),
        ),
        in_specs=[SMEM] + [VMEM] * 5,
        out_specs=(VMEM, VMEM),
        compiler_params=PARAMS,
        cost_estimate=pl.CostEstimate(flops=flops, bytes_accessed=7 << 20, transcendentals=0),
        name="partial_gate_up",
    )(core, x, *weights)


def input_grad_kernel(core_ref, g_ref, u_ref, g0_ref, u0_ref, g1_ref, u1_ref, out_ref):
    core = core_ref[0]
    dims = (((1,), (1,)), ((), ()))
    for w_gate, w_up, b in ((g0_ref, u0_ref, core), (g1_ref, u1_ref, 1 - core)):
        for a in range(2):
            total = lax.dot_general(g_ref[a], w_gate[...], dims, preferred_element_type=F32)
            total = total + lax.dot_general(u_ref[a], w_up[...], dims, preferred_element_type=F32)
            out_ref[2 * a + b] = total.astype(BF16)


def input_grad(core, d_gate, d_up, weights):
    count, rows = d_gate.shape[1], weights[0].shape[0]
    flops = 2 * 4 * count * rows * 2 * d_gate.shape[2]
    return pl.pallas_call(
        input_grad_kernel,
        out_shape=jax.ShapeDtypeStruct((4, count, rows), BF16),
        in_specs=[SMEM] + [VMEM] * 6,
        out_specs=VMEM,
        compiler_params=PARAMS,
        cost_estimate=pl.CostEstimate(flops=flops, bytes_accessed=6 << 20, transcendentals=0),
        name="input_grad",
    )(core, d_gate, d_up, *weights)


def shards(quantized, scales, d_hidden, w_gate, w_up):
    count, width = quantized.shape
    rows, ff = w_gate.shape
    half, core = lax.axis_index("zh"), lax.axis_index("c")
    core_ref = core.astype(jnp.int32).reshape(1)
    with jax.named_scope("weights_of_chip"):
        weights = (w_gate, w_up, swap_core(w_gate), swap_core(w_up))
    local = (quantized.astype(F32) * scales).astype(BF16)
    with jax.named_scope("gather_inputs"):
        held = spread(swap_half_y(local), "zl")
        held = held.transpose(1, 0, 2).reshape(count, rows)
        inputs = spread(held, "y")
    with jax.named_scope("partial_gate_up"):
        parts, sent = partial_gate_up(core_ref, inputs, weights)
    with jax.named_scope("half_sum"):
        inputs, sent = lax.optimization_barrier((inputs, sent))
        other = swap_half(sent)
        far_hidden = swap_half(d_hidden)
    with jax.named_scope("all_inputs"):
        all_inputs = [inputs] + [step_outer(inputs, k) for k in (1, 2, 3)]
    with jax.named_scope("elementwise"):
        pre = parts + other.astype(F32)
        first = half == 0
        grad_out = jnp.stack(
            [jnp.where(first, d_hidden, far_hidden), jnp.where(first, far_hidden, d_hidden)]
        ).astype(F32)
        gate, up = pre[..., :ff], pre[..., ff:]
        sig = jax.nn.sigmoid(gate)
        d_gate = (grad_out * up * sig * (1.0 + gate * (1.0 - sig))).astype(BF16)
        d_up = (grad_out * gate * sig).astype(BF16)
    with jax.named_scope("d_input"):
        di = input_grad(core_ref, d_gate, d_up, weights)
        di_y = jnp.sum(lax.all_to_all(di, "y", 0, 0).astype(F32), axis=0).astype(BF16)
        di = di_y.reshape(count, 8, width).transpose(1, 0, 2)
        di_z = jnp.sum(lax.all_to_all(di, "zl", 0, 0).astype(F32), axis=0).astype(BF16)
        di = swap_half_y(di_z)
    with jax.named_scope("d_over_x"):
        d = jnp.concatenate([d_gate, d_up], axis=-1)
        d_all = lax.all_gather(d, "x", axis=0)
        d_all, all_inputs, _ = lax.optimization_barrier((d_all, all_inputs, di_z))
        outer = lax.axis_index("x")
        d_all = jnp.concatenate(
            [lax.dynamic_index_in_dim(d_all, (outer + 4 - k) % 4, 0, keepdims=False) for k in range(4)]
        ).reshape(8 * count, 2 * ff)
    with jax.named_scope("weight_grads"):

        def grad(b):
            picked = jnp.concatenate(
                [
                    lax.dynamic_index_in_dim(v.reshape(2, 2, count, rows), b, 1, keepdims=False)
                    for v in all_inputs
                ]
            )
            return jnp.dot(picked.reshape(8 * count, rows).T, d_all, preferred_element_type=F32)

        got = swap_core(grad(1 - core).astype(BF16))
        dw = grad(core) + got.astype(F32)
        dw = dw.astype(BF16)
    return di, dw[:, :ff], dw[:, ff:]


def solution(mesh):
    fine = Mesh(mesh.devices.reshape([SIZES[a] for a in AXES]), AXES)
    in_specs = (P(ROWS, COLS), P(ROWS, COLS), P(ROWS, COLS), P(SHARD, COLS), P(SHARD, COLS))
    out_specs = (P(ROWS, COLS), P(SHARD, COLS), P(SHARD, COLS))
    return jax.shard_map(shards, mesh=fine, in_specs=in_specs, out_specs=out_specs, check_vma=False)
```

time: 228 us -> 267 us (1.17)
  the two profiles are of different devices: /device:TPU:25 before, /device:TPU:112 now
where the time goes in v3:
time: 267 us; the launch traced here: 266 us
  waiting for transfers between devices  129 us (48%)
  starting transfers between devices  83.7 us (31%)
  local copies, waits for them, and re-layouts  17.4 us (7%)
  between operations  14.4 us (5%)
  Pallas kernels  8.95 us (3%)
  matrix products  8.12 us (3%)
  other arithmetic  3.71 us (1%)
    ppermute x10, waiting for transfers between devices, permute(): return lax.ppermute(value, axes if len(axes) > 1 else axes[0], pairs)  98.1 us
    ppermute x10, starting transfers between devices, permute(): return lax.ppermute(value, axes if len(axes) > 1 else axes[0], pairs)  51.4 us
    all_to_all x2, waiting for transfers between devices, spread(): lax.all_to_all(jnp.broadcast_to(value[None], (n,) + value.shape), axis, 0...  17.8 us
    all_to_all x2, starting transfers between devices, spread(): lax.all_to_all(jnp.broadcast_to(value[None], (n,) + value.shape), axis, 0...  16.4 us
    all_to_all x1, waiting for transfers between devices, shards(): lax.all_to_all(di, 'zl', 0, 0).astype(F32)  13.3 us
    all_to_all x1, starting transfers between devices, shards(): lax.all_to_all(di, 'zl', 0, 0).astype(F32)  9.53 us
    dot_general x2, matrix products, grad(): jnp.dot(picked.reshape(8 * count, rows).T, d_all, preferred_element_type=...  8.12 us
    dynamic_slice x10, local copies, waits for them, and re-layouts, grad(): lax.dynamic_index_in_dim(v.reshape(2, 2, count, rows), b, 1, keepdims=False)  7.6 us
  transfers between devices with their start and end apart: 15, of which 8 were waited for; matrix products, arithmetic and copies ran while one was open for 1% of the time, Pallas kernels for 2%

profile of v3, /device:TPU:112, one launch (start us, length us, event | category | flops | bytes accessed | tf_op | source)
XLA Modules:
  0.0 265.6 jit_solution(8567071054707342303)
XLA Ops:
  8.0 12.8 %collective-permute-start.1 = (bf16[128,128]{1,0:T(8,128)(2,1)S(1)}, bf16[128,128]{1,0:T(8,128)(2,1)S(1)}, u32[]{:S(2)}, u32[]{:S(2)}) collective-permute-start(bf16[128,128]{1,0:T(8,128)(2,1)S(1)} %multiply_convert_fusion), channel_id=1, source_target_pairs={{0,0},{8,8},{16,64},{24,72},{64,16},{72,24},{80,80},{88,88},{1,1},... | collective-permute-start | bytes 98312 | tf_op jit(solution)/shard_map/gather_inputs/ppermute | solution.py:25
  20.8 4.2 %collective-permute-done.1 = bf16[128,128]{1,0:T(8,128)(2,1)S(1)} collective-permute-done((bf16[128,128]{1,0:T(8,128)(2,1)S(1)}, bf16[128,128]{1,0:T(8,128)(2,1)S(1)}, u32[]{:S(2)}, u32[]{:S(2)}) %collective-permute-start.1) | collective-permute-done | bytes 32800 | tf_op jit(solution)/shard_map/gather_inputs/ppermute | solution.py:25
  25.8 11.6 %all-to-all-start = ((bf16[8,128,128]{2,1,0:T(8,128)(2,1)}), bf16[8,128,128]{2,1,0:T(8,128)(2,1)S(1)}, u32[]{:S(2)}, u32[]{:S(2)}) async-start(bf16[8,128,128]{2,1,0:T(8,128)(2,1)} %broadcast_in_dim.6), calls=%async_computation | async-start | bytes 524288 | tf_op jit(solution)/shard_map/gather_inputs/all_to_all | solution.py:48
  37.4 1.9 collective-permute-start.2
  39.3 2.4 collective-permute-start.3
  41.7 8.3 %all-to-all-done = bf16[8,128,128]{2,1,0:T(8,128)(2,1)S(1)} async-done(((bf16[8,128,128]{2,1,0:T(8,128)(2,1)}), bf16[8,128,128]{2,1,0:T(8,128)(2,1)S(1)}, u32[]{:S(2)}, u32[]{:S(2)}) %all-to-all-start) | async-done | bytes 262176 | tf_op jit(solution)/shard_map/gather_inputs/all_to_all | solution.py:48
  50.4 1.1 broadcast_in_dim.15
  51.5 4.8 %all-to-all-start.1 = ((bf16[4,128,1024]{2,1,0:T(8,128)(2,1)}), bf16[4,128,1024]{2,1,0:T(8,128)(2,1)S(1)}, u32[]{:S(2)}, u32[]{:S(2)}) async-start(bf16[4,128,1024]{2,1,0:T(8,128)(2,1)} %broadcast_in_dim.15), calls=%async_computation.1 | async-start | bytes 2097152 | tf_op jit(solution)/shard_map/gather_inputs/all_to_all | solution.py:48
  56.3 9.5 %all-to-all-done.1.x_ref = bf16[4,128,1024]{2,1,0:T(8,128)(2,1)S(1)} async-done(((bf16[4,128,1024]{2,1,0:T(8,128)(2,1)}), bf16[4,128,1024]{2,1,0:T(8,128)(2,1)S(1)}, u32[]{:S(2)}, u32[]{:S(2)}) %all-to-all-start.1) | async-done | bytes 1048608 | tf_op jit(solution)/shard_map/gather_inputs/all_to_all | solution.py:48
  65.8 3.6 %partial_gate_up.1 = (f32[2,128,1024]{2,1,0:T(8,128)S(1)}, bf16[2,128,1024]{2,1,0:T(8,128)(2,1)}) custom-call(s32[1]{0:T(128)} %bitcast.core_ref, bf16[4,128,1024]{2,1,0:T(8,128)(2,1)S(1)} %all-to-all-done.1.x_ref, bf16[1024,512]{1,0:T(8,128)(2,1)S(1)} %copy-done, bf16[1024,512]{1,0:T(8,128)(2,1)S(1)} %copy-done.1, ...), custom_call_target="tpu_custom_call" | custom-call | flops 1073741824 | bytes 7340032 | tf_op jit(solution)/shard_map/partial_gate_up/partial_gate_up/pallas_call | solution.py:71
  70.4 7.5 %collective-permute-start.4 = (bf16[2,128,1024]{2,1,0:T(8,128)(2,1)}, bf16[2,128,1024]{2,1,0:T(8,128)(2,1)}, u32[]{:S(2)}, u32[]{:S(2)}) collective-permute-start(bf16[2,128,1024]{2,1,0:T(8,128)(2,1)} %get-tuple-element.14), channel_id=1, source_target_pairs={{0,64},{64,0},{1,65},{65,1},{2,66},{66,2},{3,67},{67,3},{4,68},{68... | collective-permute-start | bytes 1572872 | tf_op jit(solution)/shard_map/half_sum/ppermute | solution.py:25
  78.0 7.0 %collective-permute-start = (bf16[128,512]{1,0:T(8,128)(2,1)S(1)}, bf16[128,512]{1,0:T(8,128)(2,1)S(1)}, u32[]{:S(2)}, u32[]{:S(2)}) collective-permute-start(bf16[128,512]{1,0:T(8,128)(2,1)S(1)} %copy-done.14), channel_id=1, source_target_pairs={{0,64},{64,0},{1,65},{65,1},{2,66},{66,2},{3,67},{67,3},{4,68},{68... | collective-permute-start | bytes 393224 | tf_op jit(solution)/shard_map/half_sum/ppermute | solution.py:25
  85.0 51.0 %collective-permute-done = bf16[128,512]{1,0:T(8,128)(2,1)S(1)} collective-permute-done((bf16[128,512]{1,0:T(8,128)(2,1)S(1)}, bf16[128,512]{1,0:T(8,128)(2,1)S(1)}, u32[]{:S(2)}, u32[]{:S(2)}) %collective-permute-start) | collective-permute-done | bytes 131104 | tf_op jit(solution)/shard_map/half_sum/ppermute | solution.py:25
  136.1 1.5 convert_add_fusion
  140.4 5.3 %input_grad.1 = bf16[4,128,1024]{2,1,0:T(8,128)(2,1)} custom-call(s32[1]{0:T(128)} %bitcast.core_ref, bf16[2,128,512]{2,1,0:T(8,128)(2,1)S(1)} %copy-done.3, bf16[2,128,512]{2,1,0:T(8,128)(2,1)S(1)} %get-tuple-element.27.u_ref, bf16[1024,512]{1,0:T(8,128)(2,1)S(1)} %copy-done, bf16[1024,512]{1,0:T(8,128)(2,1)S(1)} %copy-done.1, ...), custom_call_target="tpu_custom_call" | custom-call | flops 1073741824 | bytes 6291456 | tf_op jit(solution)/shard_map/d_input/input_grad/pallas_call | solution.py:98
  145.7 6.4 %all-to-all-start.2 = ((bf16[4,128,1024]{2,1,0:T(8,128)(2,1)}), bf16[4,128,1024]{2,1,0:T(8,128)(2,1)S(1)}, u32[]{:S(2)}, u32[]{:S(2)}) async-start(bf16[4,128,1024]{2,1,0:T(8,128)(2,1)} %input_grad.1), calls=%async_computation.2 | async-start | bytes 2097152 | tf_op jit(solution)/shard_map/d_input/all_to_all | solution.py:141
  152.1 4.7 %collective-permute-start.8 = (bf16[4,128,1024]{2,1,0:T(8,128)(2,1)S(1)}, bf16[4,128,1024]{2,1,0:T(8,128)(2,1)S(1)}, u32[]{:S(2)}, u32[]{:S(2)}) collective-permute-start(bf16[4,128,1024]{2,1,0:T(8,128)(2,1)S(1)} %all-to-all-done.1.x_ref), channel_id=1, source_target_pairs={{0,384},{128,0},{256,128},{384,256},{1,385},{129,1},{257,129},{385... | collective-permute-start | bytes 3145736 | tf_op jit(solution)/shard_map/all_inputs/ppermute | solution.py:25
  156.8 2.7 %collective-permute-start.7 = (bf16[4,128,1024]{2,1,0:T(8,128)(2,1)S(1)}, bf16[4,128,1024]{2,1,0:T(8,128)(2,1)}, u32[]{:S(2)}, u32[]{:S(2)}) collective-permute-start(bf16[4,128,1024]{2,1,0:T(8,128)(2,1)S(1)} %all-to-all-done.1.x_ref), channel_id=1, source_target_pairs={{0,256},{128,384},{256,0},{384,128},{1,257},{129,385},{257,1},{385... | collective-permute-start | bytes 3145736 | tf_op jit(solution)/shard_map/all_inputs/ppermute | solution.py:25
  159.5 2.8 %collective-permute-start.6 = (bf16[4,128,1024]{2,1,0:T(8,128)(2,1)S(1)}, bf16[4,128,1024]{2,1,0:T(8,128)(2,1)}, u32[]{:S(2)}, u32[]{:S(2)}) collective-permute-start(bf16[4,128,1024]{2,1,0:T(8,128)(2,1)S(1)} %all-to-all-done.1.x_ref), channel_id=1, source_target_pairs={{0,128},{128,256},{256,384},{384,0},{1,129},{129,257},{257,385},{3... | collective-permute-start | bytes 3145736 | tf_op jit(solution)/shard_map/all_inputs/ppermute | solution.py:25
  163.5 9.5 %all-to-all-start.3 = ((bf16[8,128,128]{2,1,0:T(8,128)(2,1)}), bf16[8,128,128]{2,1,0:T(8,128)(2,1)S(1)}, u32[]{:S(2)}, u32[]{:S(2)}) async-start(bf16[8,128,128]{2,1,0:T(8,128)(2,1)} %copy.38), calls=%async_computation.3 | async-start | bytes 524288 | tf_op jit(solution)/shard_map/d_input/all_to_all | solution.py:143
  173.0 13.3 %all-to-all-done.3 = bf16[8,128,128]{2,1,0:T(8,128)(2,1)S(1)} async-done(((bf16[8,128,128]{2,1,0:T(8,128)(2,1)}), bf16[8,128,128]{2,1,0:T(8,128)(2,1)S(1)}, u32[]{:S(2)}, u32[]{:S(2)}) %all-to-all-start.3) | async-done | bytes 262176 | tf_op jit(solution)/shard_map/d_input/all_to_all | solution.py:143
  186.4 10.1 %collective-permute-done.8 = bf16[4,128,1024]{2,1,0:T(8,128)(2,1)S(1)} collective-permute-done((bf16[4,128,1024]{2,1,0:T(8,128)(2,1)S(1)}, bf16[4,128,1024]{2,1,0:T(8,128)(2,1)S(1)}, u32[]{:S(2)}, u32[]{:S(2)}) %collective-permute-start.8) | collective-permute-done | bytes 1048608 | tf_op jit(solution)/shard_map/all_inputs/ppermute | solution.py:25
  196.5 23.4 %collective-permute-done.6 = bf16[4,128,1024]{2,1,0:T(8,128)(2,1)} collective-permute-done((bf16[4,128,1024]{2,1,0:T(8,128)(2,1)S(1)}, bf16[4,128,1024]{2,1,0:T(8,128)(2,1)}, u32[]{:S(2)}, u32[]{:S(2)}) %collective-permute-start.6) | collective-permute-done | bytes 1048608 | tf_op jit(solution)/shard_map/all_inputs/ppermute | solution.py:25
  220.0 1.5 constant_dynamic-slice_fusion.6
  223.5 1.8 constant_dynamic-slice_fusion.4
  226.5 1.8 dynamic-slice_bitcast_fusion.3
  228.5 3.7 %bitcast_convert_fusion = bf16[1024,1024]{1,0:T(8,128)(2,1)} fusion(bf16[2,128,1024]{1,2,0:T(8,128)(2,1)S(1)} %bitcast.48, bf16[2,128,1024]{1,2,0:T(8,128)(2,1)S(1)} %bitcast.49, bf16[2,128,1024]{1,2,0:T(8,128)(2,1)S(1)} %bitcast.44, bf16[2,128,1024]{1,2,0:T(8,128)(2,1)S(1)} %bitcast.45, bf16[2,128,1024]{2,1,0:T(8,128)(2,1)S(1)} %get-tuple-element.24, ...), kind=kOutput, calls=%fused_computation | convolution fusion | flops 2154823680 | bytes 6291456 | tf_op jit(solution)/shard_map/weight_grads/dot_general | solution.py:162
  232.2 1.9 collective-permute-start.9
  234.1 7.7 %collective-permute-start.5 = (bf16[128,128]{1,0:T(8,128)(2,1)S(1)}, bf16[128,128]{1,0:T(8,128)(2,1)S(1)}, u32[]{:S(2)}, u32[]{:S(2)}) collective-permute-start(bf16[128,128]{1,0:T(8,128)(2,1)S(1)} %reduce_sum.25), channel_id=1, source_target_pairs={{0,0},{8,8},{16,64},{24,72},{64,16},{72,24},{80,80},{88,88},{1,1},... | collective-permute-start | bytes 98312 | tf_op jit(solution)/shard_map/d_input/ppermute | solution.py:25
  241.8 9.3 %collective-permute-done.5 = bf16[128,128]{1,0:T(8,128)(2,1)S(1)} collective-permute-done((bf16[128,128]{1,0:T(8,128)(2,1)S(1)}, bf16[128,128]{1,0:T(8,128)(2,1)S(1)}, u32[]{:S(2)}, u32[]{:S(2)}) %collective-permute-start.5) | collective-permute-done | bytes 32800 | tf_op jit(solution)/shard_map/d_input/ppermute | solution.py:25
  252.2 4.4 %fusion = bf16[1024,1024]{1,0:T(8,128)(2,1)S(1)} fusion(bf16[1024,1024]{1,0:T(8,128)(2,1)} %collective-permute-done.9, bf16[2,128,1024]{1,2,0:T(8,128)(2,1)S(1)} %bitcast.46, bf16[2,128,1024]{1,2,0:T(8,128)(2,1)S(1)} %bitcast.51, bf16[2,128,1024]{1,2,0:T(8,128)(2,1)S(1)} %bitcast.47, bf16[2,128,1024]{1,2,0:T(8,128)(2,1)S(1)} %bitcast.50, ...), kind=kOutput, calls=%fused_computation.2 | convolution fusion | flops 2156920832 | bytes 8388608 | tf_op jit(solution)/shard_map/weight_grads/dot_general | solution.py:162
  256.6 1.5 fusion.22
  (59 shorter events, 12.0 us)
Async XLA Ops:
  8.0 17.0 %collective-permute-start.1 = (bf16[128,128]{1,0:T(8,128)(2,1)S(1)}, bf16[128,128]{1,0:T(8,128)(2,1)S(1)}, u32[]{:S(2)}, u32[]{:S(2)}) collective-permute-start(bf16[128,128]{1,0:T(8,128)(2,1)S(1)} %multiply_convert_fusion), channel_id=1, source_target_pairs={{0,0},{8,8},{16,64},{24,72},{64,16},{72,24},{80,80},{88,88},{1,1},... | collective-permute-start | bytes 98312 | tf_op jit(solution)/shard_map/gather_inputs/ppermute | solution.py:25
  25.8 24.2 %all-to-all-start = ((bf16[8,128,128]{2,1,0:T(8,128)(2,1)}), bf16[8,128,128]{2,1,0:T(8,128)(2,1)S(1)}, u32[]{:S(2)}, u32[]{:S(2)}) async-start(bf16[8,128,128]{2,1,0:T(8,128)(2,1)} %broadcast_in_dim.6), calls=%async_computation | async-start | bytes 524288 | tf_op jit(solution)/shard_map/gather_inputs/all_to_all | solution.py:48
  37.4 18.9 %collective-permute-start.2 = (bf16[1024,512]{1,0:T(8,128)(2,1)}, bf16[1024,512]{1,0:T(8,128)(2,1)}, u32[]{:S(2)}, u32[]{:S(2)}) collective-permute-start(bf16[1024,512]{1,0:T(8,128)(2,1)} %g0_ref.3), channel_id=1, source_target_pairs={{0,32},{32,0},{1,33},{33,1},{2,34},{34,2},{3,35},{35,3},{4,36},{36... | collective-permute-start | bytes 3145736 | tf_op jit(solution)/shard_map/weights_of_chip/ppermute | solution.py:25
  39.3 17.0 %collective-permute-start.3 = (bf16[1024,512]{1,0:T(8,128)(2,1)}, bf16[1024,512]{1,0:T(8,128)(2,1)}, u32[]{:S(2)}, u32[]{:S(2)}) collective-permute-start(bf16[1024,512]{1,0:T(8,128)(2,1)} %u0_ref.3), channel_id=1, source_target_pairs={{0,32},{32,0},{1,33},{33,1},{2,34},{34,2},{3,35},{35,3},{4,36},{36... | collective-permute-start | bytes 3145736 | tf_op jit(solution)/shard_map/weights_of_chip/ppermute | solution.py:25
  50.2 15.6 %copy-start = (bf16[1024,512]{1,0:T(8,128)(2,1)S(1)}, bf16[1024,512]{1,0:T(8,128)(2,1)}, u32[]{:S(2)}) copy-start(bf16[1024,512]{1,0:T(8,128)(2,1)} %g0_ref.3) | copy-start | bytes 3145732
  50.2 15.6 %copy-start.1 = (bf16[1024,512]{1,0:T(8,128)(2,1)S(1)}, bf16[1024,512]{1,0:T(8,128)(2,1)}, u32[]{:S(2)}) copy-start(bf16[1024,512]{1,0:T(8,128)(2,1)} %u0_ref.3) | copy-start | bytes 3145732
  51.5 14.3 %all-to-all-start.1 = ((bf16[4,128,1024]{2,1,0:T(8,128)(2,1)}), bf16[4,128,1024]{2,1,0:T(8,128)(2,1)S(1)}, u32[]{:S(2)}, u32[]{:S(2)}) async-start(bf16[4,128,1024]{2,1,0:T(8,128)(2,1)} %broadcast_in_dim.15), calls=%async_computation.1 | async-start | bytes 2097152 | tf_op jit(solution)/shard_map/gather_inputs/all_to_all | solution.py:48
  56.3 163.7 %all-gather.3.cloned.1.call-start = ((), (), s32[]{:S(2)}) async-start(), calls=%async_computation.4 | async-start | bytes 2621440 | tf_op jit(solution)/shard_map/d_over_x/all_gather | solution.py:147
  65.8 12.1 %copy-start.14 = (bf16[128,512]{1,0:T(8,128)(2,1)S(1)}, bf16[128,512]{1,0:T(8,128)(2,1)}, u32[]{:S(2)}) copy-start(bf16[128,512]{1,0:T(8,128)(2,1)} %param.7) | copy-start | bytes 393220
  69.5 1.0 copy-start.4
  70.4 65.6 %collective-permute-start.4 = (bf16[2,128,1024]{2,1,0:T(8,128)(2,1)}, bf16[2,128,1024]{2,1,0:T(8,128)(2,1)}, u32[]{:S(2)}, u32[]{:S(2)}) collective-permute-start(bf16[2,128,1024]{2,1,0:T(8,128)(2,1)} %get-tuple-element.14), channel_id=1, source_target_pairs={{0,64},{64,0},{1,65},{65,1},{2,66},{66,2},{3,67},{67,3},{4,68},{68... | collective-permute-start | bytes 1572872 | tf_op jit(solution)/shard_map/half_sum/ppermute | solution.py:25
  78.0 58.1 %collective-permute-start = (bf16[128,512]{1,0:T(8,128)(2,1)S(1)}, bf16[128,512]{1,0:T(8,128)(2,1)S(1)}, u32[]{:S(2)}, u32[]{:S(2)}) collective-permute-start(bf16[128,512]{1,0:T(8,128)(2,1)S(1)} %copy-done.14), channel_id=1, source_target_pairs={{0,64},{64,0},{1,65},{65,1},{2,66},{66,2},{3,67},{67,3},{4,68},{68... | collective-permute-start | bytes 393224 | tf_op jit(solution)/shard_map/half_sum/ppermute | solution.py:25
  138.7 0.7 copy-start.2
  139.4 1.0 copy-start.3
  145.7 16.6 %all-to-all-start.2 = ((bf16[4,128,1024]{2,1,0:T(8,128)(2,1)}), bf16[4,128,1024]{2,1,0:T(8,128)(2,1)S(1)}, u32[]{:S(2)}, u32[]{:S(2)}) async-start(bf16[4,128,1024]{2,1,0:T(8,128)(2,1)} %input_grad.1), calls=%async_computation.2 | async-start | bytes 2097152 | tf_op jit(solution)/shard_map/d_input/all_to_all | solution.py:141
  152.1 44.4 %collective-permute-start.8 = (bf16[4,128,1024]{2,1,0:T(8,128)(2,1)S(1)}, bf16[4,128,1024]{2,1,0:T(8,128)(2,1)S(1)}, u32[]{:S(2)}, u32[]{:S(2)}) collective-permute-start(bf16[4,128,1024]{2,1,0:T(8,128)(2,1)S(1)} %all-to-all-done.1.x_ref), channel_id=1, source_target_pairs={{0,384},{128,0},{256,128},{384,256},{1,385},{129,1},{257,129},{385... | collective-permute-start | bytes 3145736 | tf_op jit(solution)/shard_map/all_inputs/ppermute | solution.py:25
  156.8 39.8 %collective-permute-start.7 = (bf16[4,128,1024]{2,1,0:T(8,128)(2,1)S(1)}, bf16[4,128,1024]{2,1,0:T(8,128)(2,1)}, u32[]{:S(2)}, u32[]{:S(2)}) collective-permute-start(bf16[4,128,1024]{2,1,0:T(8,128)(2,1)S(1)} %all-to-all-done.1.x_ref), channel_id=1, source_target_pairs={{0,256},{128,384},{256,0},{384,128},{1,257},{129,385},{257,1},{385... | collective-permute-start | bytes 3145736 | tf_op jit(solution)/shard_map/all_inputs/ppermute | solution.py:25
  159.5 60.5 %collective-permute-start.6 = (bf16[4,128,1024]{2,1,0:T(8,128)(2,1)S(1)}, bf16[4,128,1024]{2,1,0:T(8,128)(2,1)}, u32[]{:S(2)}, u32[]{:S(2)}) collective-permute-start(bf16[4,128,1024]{2,1,0:T(8,128)(2,1)S(1)} %all-to-all-done.1.x_ref), channel_id=1, source_target_pairs={{0,128},{128,256},{256,384},{384,0},{1,129},{129,257},{257,385},{3... | collective-permute-start | bytes 3145736 | tf_op jit(solution)/shard_map/all_inputs/ppermute | solution.py:25
  163.5 22.8 %all-to-all-start.3 = ((bf16[8,128,128]{2,1,0:T(8,128)(2,1)}), bf16[8,128,128]{2,1,0:T(8,128)(2,1)S(1)}, u32[]{:S(2)}, u32[]{:S(2)}) async-start(bf16[8,128,128]{2,1,0:T(8,128)(2,1)} %copy.38), calls=%async_computation.3 | async-start | bytes 524288 | tf_op jit(solution)/shard_map/d_input/all_to_all | solution.py:143
  196.5 23.4 %copy-start.5 = (bf16[4,128,1024]{2,1,0:T(8,128)(2,1)}, bf16[4,128,1024]{2,1,0:T(8,128)(2,1)S(1)}, u32[]{:S(2)}) copy-start(bf16[4,128,1024]{2,1,0:T(8,128)(2,1)S(1)} %collective-permute-done.8) | copy-start | bytes 3145732
  226.5 1.9 copy-start.6
  226.5 1.9 copy-start.7
  226.5 2.0 copy-start.8
  228.4 3.8 %copy-start.9 = (bf16[2,128,1024]{2,1,0:T(8,128)(2,1)}, bf16[2,128,1024]{2,1,0:T(8,128)(2,1)S(1)}, u32[]{:S(2)}) copy-start(bf16[2,128,1024]{2,1,0:T(8,128)(2,1)S(1)} %get-tuple-element.23) | copy-start | bytes 1572868
  228.4 3.8 %copy-start.11 = (bf16[2,128,1024]{2,1,0:T(8,128)(2,1)}, bf16[2,128,1024]{2,1,0:T(8,128)(2,1)S(1)}, u32[]{:S(2)}) copy-start(bf16[2,128,1024]{2,1,0:T(8,128)(2,1)S(1)} %get-tuple-element.24) | copy-start | bytes 1572868
  228.4 3.8 %copy-start.12 = (bf16[2,128,1024]{2,1,0:T(8,128)(2,1)}, bf16[2,128,1024]{2,1,0:T(8,128)(2,1)S(1)}, u32[]{:S(2)}) copy-start(bf16[2,128,1024]{2,1,0:T(8,128)(2,1)S(1)} %get-tuple-element.25) | copy-start | bytes 1572868
  228.4 3.8 %copy-start.13 = (bf16[2,128,1024]{2,1,0:T(8,128)(2,1)}, bf16[2,128,1024]{2,1,0:T(8,128)(2,1)S(1)}, u32[]{:S(2)}) copy-start(bf16[2,128,1024]{2,1,0:T(8,128)(2,1)S(1)} %get-tuple-element.26) | copy-start | bytes 1572868
  232.2 20.0 %collective-permute-start.9 = (bf16[1024,1024]{1,0:T(8,128)(2,1)}, bf16[1024,1024]{1,0:T(8,128)(2,1)}, u32[]{:S(2)}, u32[]{:S(2)}) collective-permute-start(bf16[1024,1024]{1,0:T(8,128)(2,1)} %bitcast_convert_fusion), channel_id=1, source_target_pairs={{0,32},{32,0},{1,33},{33,1},{2,34},{34,2},{3,35},{35,3},{4,36},{36... | collective-permute-start | bytes 6291464 | tf_op jit(solution)/shard_map/weight_grads/ppermute | solution.py:25
  234.1 16.9 %collective-permute-start.5 = (bf16[128,128]{1,0:T(8,128)(2,1)S(1)}, bf16[128,128]{1,0:T(8,128)(2,1)S(1)}, u32[]{:S(2)}, u32[]{:S(2)}) collective-permute-start(bf16[128,128]{1,0:T(8,128)(2,1)S(1)} %reduce_sum.25), channel_id=1, source_target_pairs={{0,0},{8,8},{16,64},{24,72},{64,16},{72,24},{80,80},{88,88},{1,1},... | collective-permute-start | bytes 98312 | tf_op jit(solution)/shard_map/d_input/ppermute | solution.py:25
  251.1 1.1 copy-start.10
Sparse Core Ops, SparseCore 0:
  139.5 77.7 all-gather.2

commit v4 on v3

v4 whole, which is shorter than its diff:
```python
import jax
import jax.numpy as jnp
import numpy as np
from jax import lax
from jax.experimental import pallas as pl
from jax.experimental.pallas import tpu as pltpu
from jax.sharding import Mesh, PartitionSpec as P

AXES = ("x", "zh", "c", "y", "zl")
SIZES = {"x": 4, "zh": 2, "c": 2, "y": 4, "zl": 8}
ROWS = ("x", "zh", "c")
COLS = ("y", "zl")
SHARD = ("zh", "c")
F32 = jnp.float32
BF16 = jnp.bfloat16


def permute(value, axes, target):
    sizes = [SIZES[a] for a in axes]
    pairs = []
    for i in range(int(np.prod(sizes))):
        at = dict(zip(axes, map(int, np.unravel_index(i, sizes))))
        to = target(at)
        pairs.append((i, int(np.ravel_multi_index([to[a] for a in axes], sizes))))
    return lax.ppermute(value, axes if len(axes) > 1 else axes[0], pairs)


def swap_half_y(value):
    return permute(
        value, ("zh", "y"), lambda d: {"zh": d["y"] // 2, "y": d["zh"] * 2 + d["y"] % 2}
    )


def swap_core(value):
    return permute(value, ("c",), lambda d: {"c": 1 - d["c"]})


def swap_half(value):
    return permute(value, ("zh",), lambda d: {"zh": 1 - d["zh"]})


def step_outer(value, k):
    return permute(value, ("x",), lambda d: {"x": (d["x"] + k) % 4})


def spread(value, axis):
    n = SIZES[axis]
    return lax.all_to_all(jnp.broadcast_to(value[None], (n,) + value.shape), axis, 0, 0)


VMEM = pl.BlockSpec(memory_space=pltpu.VMEM)
SMEM = pl.BlockSpec(memory_space=pltpu.SMEM)
PARAMS = pltpu.CompilerParams(vmem_limit_bytes=32 * 1024 * 1024)


def partial_kernel(place_ref, x_ref, g0_ref, u0_ref, g1_ref, u1_ref, keep_ref, send_ref):
    half, core = place_ref[0], place_ref[1]
    count, ff = x_ref.shape[1], g0_ref.shape[1]

    def rows_of(b):
        return jnp.concatenate([x_ref[2 * (1 - half) + b], x_ref[2 * half + b]], axis=0)

    near, far = rows_of(core), rows_of(1 - core)
    for k, (w0, w1) in enumerate(((g0_ref, g1_ref), (u0_ref, u1_ref))):
        total = jnp.dot(near, w0[...], preferred_element_type=F32)
        total = total + jnp.dot(far, w1[...], preferred_element_type=F32)
        send_ref[:, k * ff : (k + 1) * ff] = total[:count].astype(BF16)
        keep_ref[:, k * ff : (k + 1) * ff] = total[count:]


def partial_gate_up(place, x, weights):
    count, ff = x.shape[1], weights[0].shape[1]
    flops = 2 * 4 * count * x.shape[2] * 2 * ff
    return pl.pallas_call(
        partial_kernel,
        out_shape=(
            jax.ShapeDtypeStruct((count, 2 * ff), F32),
            jax.ShapeDtypeStruct((count, 2 * ff), BF16),
        ),
        in_specs=[SMEM] + [VMEM] * 5,
        out_specs=(VMEM, VMEM),
        compiler_params=PARAMS,
        cost_estimate=pl.CostEstimate(flops=flops, bytes_accessed=6 << 20, transcendentals=0),
        name="partial_gate_up",
    )(place, x, *weights)


def hidden_grad_kernel(keep_ref, other_ref, grad_ref, out_ref):
    ff = grad_ref.shape[1]
    gate = keep_ref[:, :ff] + other_ref[:, :ff].astype(F32)
    up = keep_ref[:, ff:] + other_ref[:, ff:].astype(F32)
    grad_out = grad_ref[...].astype(F32)
    sig = jax.nn.sigmoid(gate)
    out_ref[:, :ff] = (grad_out * up * sig * (1.0 + gate * (1.0 - sig))).astype(BF16)
    out_ref[:, ff:] = (grad_out * gate * sig).astype(BF16)


def hidden_grad(keep, other, grad):
    return pl.pallas_call(
        hidden_grad_kernel,
        out_shape=jax.ShapeDtypeStruct(keep.shape, BF16),
        in_specs=[VMEM] * 3,
        out_specs=VMEM,
        compiler_params=PARAMS,
        cost_estimate=pl.CostEstimate(flops=1 << 20, bytes_accessed=1 << 20, transcendentals=1 << 16),
        name="hidden_grad",
    )(keep, other, grad)


def input_grad_kernel(place_ref, d0_ref, d1_ref, g0_ref, u0_ref, g1_ref, u1_ref, out_ref):
    half, core = place_ref[0], place_ref[1]
    count, ff = d0_ref.shape[0], g0_ref.shape[1]
    dims = (((1,), (1,)), ((), ()))
    d = jnp.concatenate([d0_ref[...], d1_ref[...]], axis=0)
    for w_gate, w_up, b in ((g0_ref, u0_ref, core), (g1_ref, u1_ref, 1 - core)):
        total = lax.dot_general(d[:, :ff], w_gate[...], dims, preferred_element_type=F32)
        total = total + lax.dot_general(d[:, ff:], w_up[...], dims, preferred_element_type=F32)
        out_ref[2 * half + b] = total[:count].astype(BF16)
        out_ref[2 * (1 - half) + b] = total[count:].astype(BF16)


def input_grad(place, d_own, d_other, weights):
    count, rows = d_own.shape[0], weights[0].shape[0]
    flops = 2 * 4 * count * rows * d_own.shape[1]
    return pl.pallas_call(
        input_grad_kernel,
        out_shape=jax.ShapeDtypeStruct((4, count, rows), BF16),
        in_specs=[SMEM] + [VMEM] * 6,
        out_specs=VMEM,
        compiler_params=PARAMS,
        cost_estimate=pl.CostEstimate(flops=flops, bytes_accessed=6 << 20, transcendentals=0),
        name="input_grad",
    )(place, d_own, d_other, *weights)


def weight_grad_kernel(other, place_ref, x_ref, d_ref, out_ref):
    half, core = place_ref[0], place_ref[1]
    b = 1 - core if other else core
    rows = x_ref.shape[2]
    step = 256
    d = jnp.concatenate([d_ref[k] for k in range(8)], axis=0)
    for i in range(0, rows, step):
        x = [x_ref[4 * k + 2 * a + b, :, i : i + step] for k in range(4) for a in (half, 1 - half)]
        total = lax.dot_general(
            jnp.concatenate(x, axis=0), d, (((0,), (0,)), ((), ())), preferred_element_type=F32
        )
        out_ref[i : i + step, :] = total.astype(out_ref.dtype)


def weight_grad(other, place, inputs, d, dtype):
    rows, cols = inputs.shape[2], d.shape[2]
    flops = 2 * 8 * d.shape[1] * rows * cols
    return pl.pallas_call(
        lambda *refs: weight_grad_kernel(other, *refs),
        out_shape=jax.ShapeDtypeStruct((rows, cols), dtype),
        in_specs=[SMEM] + [VMEM] * 2,
        out_specs=VMEM,
        compiler_params=PARAMS,
        cost_estimate=pl.CostEstimate(flops=flops, bytes_accessed=8 << 20, transcendentals=0),
        name="weight_grad_other" if other else "weight_grad_own",
    )(place, inputs, d)


def shards(quantized, scales, d_hidden, w_gate, w_up):
    count, width = quantized.shape
    rows, ff = w_gate.shape
    place = jnp.stack([lax.axis_index("zh"), lax.axis_index("c"), lax.axis_index("x")]).astype(jnp.int32)
    with jax.named_scope("weights_of_chip"):
        weights = (w_gate, w_up, swap_core(w_gate), swap_core(w_up))
    local = (quantized.astype(F32) * scales).astype(BF16)
    with jax.named_scope("gather_inputs"):
        held = spread(swap_half_y(local), "zl")
        held, weights = lax.optimization_barrier((held, weights))
        held = held.transpose(1, 0, 2).reshape(count, rows)
        inputs = spread(held, "y")
    with jax.named_scope("partial_gate_up"):
        keep, sent = partial_gate_up(place, inputs, weights)
    with jax.named_scope("all_inputs"):
        all_inputs = lax.all_gather(inputs, "x", axis=0, tiled=True)
    with jax.named_scope("half_sum"):
        other = swap_half(sent)
    with jax.named_scope("hidden_grad"):
        d_own = hidden_grad(keep, other, d_hidden)
    with jax.named_scope("d_far"):
        d_far = swap_half(d_own)
    with jax.named_scope("d_over_x"):
        d, all_inputs = lax.optimization_barrier((jnp.stack([d_own, d_far]), all_inputs))
        d_all = lax.all_gather(d, "x", axis=0, tiled=True)
    with jax.named_scope("d_input"):
        di = input_grad(place, d_own, d_far, weights)
        di = jnp.sum(lax.all_to_all(di, "y", 0, 0).astype(F32), axis=0).astype(BF16)
        di = di.reshape(count, 8, width).transpose(1, 0, 2)
        di_z = jnp.sum(lax.all_to_all(di, "zl", 0, 0).astype(F32), axis=0).astype(BF16)
        di = swap_half_y(di_z)
    with jax.named_scope("weight_grads"):
        d_all, all_inputs, _ = lax.optimization_barrier((d_all, all_inputs, di_z))
        got = swap_core(weight_grad(True, place, all_inputs, d_all, BF16))
        dw = weight_grad(False, place, all_inputs, d_all, F32)
        d_gate_weight, d_up_weight = (
            (dw[:, k : k + ff] + got[:, k : k + ff].astype(F32)).astype(BF16) for k in (0, ff)
        )
    return di, d_gate_weight, d_up_weight


def solution(mesh):
    fine = Mesh(mesh.devices.reshape([SIZES[a] for a in AXES]), AXES)
    in_specs = (P(ROWS, COLS), P(ROWS, COLS), P(ROWS, COLS), P(SHARD, COLS), P(SHARD, COLS))
    out_specs = (P(ROWS, COLS), P(SHARD, COLS), P(SHARD, COLS))
    return jax.shard_map(shards, mesh=fine, in_specs=in_specs, out_specs=out_specs, check_vma=False)
```

time: 267 us -> 218 us (0.82)
  the two profiles are of different devices: /device:TPU:112 before, /device:TPU:25 now
where the time goes in v4:
time: 218 us; the launch traced here: 216 us
  blocking collectives  76.9 us (35%)
  starting transfers between devices  50.7 us (23%)
  waiting for transfers between devices  49.2 us (23%)
  between operations  14.2 us (7%)
  local copies, waits for them, and re-layouts  11.5 us (5%)
  Pallas kernels  9.65 us (4%)
  other arithmetic  4.08 us (2%)
    ppermute x7, starting transfers between devices, permute(): return lax.ppermute(value, axes if len(axes) > 1 else axes[0], pairs)  50.6 us
    ppermute x7, waiting for transfers between devices, permute(): return lax.ppermute(value, axes if len(axes) > 1 else axes[0], pairs)  37.8 us
    all_to_all x2, blocking collectives, spread(): lax.all_to_all(jnp.broadcast_to(value[None], (n,) + value.shape), axis, 0...  34.4 us
    all_to_all x1, blocking collectives, shards(): lax.all_to_all(di, 'zl', 0, 0).astype(F32)  30.5 us
    all_to_all x1, blocking collectives, shards(): di = jnp.sum(lax.all_to_all(di, 'y', 0, 0).astype(F32), axis=0).astype(BF16)  12 us
    all_gather x1, waiting for transfers between devices, shards(): all_inputs = lax.all_gather(inputs, 'x', axis=0, tiled=True)  11.1 us
    unnamed x23, local copies, waits for them, and re-layouts  10.7 us
    pallas_call x2, Pallas kernels, weight_grad(): pl.pallas_call(lambda *refs: weight_grad_kernel(other, *refs), out_shape=...  5.86 us
  transfers between devices with their start and end apart: 9, of which 6 were waited for; matrix products, arithmetic and copies ran while one was open for 1% of the time, Pallas kernels for 3%

profile of v4, /device:TPU:25, one launch (start us, length us, event | category | flops | bytes accessed | tf_op | source)
XLA Modules:
  0.0 216.4 jit_solution(15378260514489643079)
XLA Ops:
  7.2 2.6 %collective-permute-start.1 = (bf16[1024,512]{1,0:T(8,128)(2,1)}, bf16[1024,512]{1,0:T(8,128)(2,1)S(1)}, u32[]{:S(2)}, u32[]{:S(2)}) collective-permute-start(bf16[1024,512]{1,0:T(8,128)(2,1)} %g0_ref.1), channel_id=1, source_target_pairs={{0,32},{32,0},{1,33},{33,1},{2,34},{34,2},{3,35},{35,3},{4,36},{36... | collective-permute-start | bytes 3145736 | tf_op jit(solution)/shard_map/weights_of_chip/ppermute | solution.py:25
  9.8 1.9 collective-permute-start.2
  11.7 0.8 multiply_convert_fusion
  12.6 16.1 %collective-permute-start = (bf16[128,128]{1,0:T(8,128)(2,1)S(1)}, bf16[128,128]{1,0:T(8,128)(2,1)S(1)}, u32[]{:S(2)}, u32[]{:S(2)}) collective-permute-start(bf16[128,128]{1,0:T(8,128)(2,1)S(1)} %multiply_convert_fusion), channel_id=1, source_target_pairs={{0,0},{8,8},{16,64},{24,72},{64,16},{72,24},{80,80},{88,88},{1,1},... | collective-permute-start | bytes 98312 | tf_op jit(solution)/shard_map/gather_inputs/ppermute | solution.py:25
  28.7 1.3 collective-permute-done
  30.1 22.3 %all_to_all.20 = bf16[8,128,128]{2,1,0:T(8,128)(2,1)S(1)} all-to-all(bf16[8,128,128]{2,1,0:T(8,128)(2,1)S(1)} %broadcast_in_dim.6), channel_id=1, replica_groups=mesh['x'=4,'zh'=2,'c'=2,'y'=4,'zl'=8] {'zl'}, dimensions={0} | all-to-all | bytes 524288 | tf_op jit(solution)/shard_map/gather_inputs/all_to_all | solution.py:48
  52.3 1.0 copy-done.5
  53.8 12.2 %all_to_all.21.x_ref = bf16[4,128,1024]{2,1,0:T(8,128)(2,1)} all-to-all(bf16[4,128,1024]{2,1,0:T(8,128)(2,1)S(1)} %broadcast_in_dim.15), channel_id=1, replica_groups=mesh['x'=4,'zh'=2,'c'=2,'y'=4,'zl'=8] {'y'}, dimensions={0} | all-to-all | bytes 2097152 | tf_op jit(solution)/shard_map/gather_inputs/all_to_all | solution.py:48
  66.1 1.2 copy-done.1
  67.4 1.2 copy-done.6
  68.6 1.8 partial_gate_up.1
  70.4 7.0 %collective-permute-start.3 = (bf16[128,1024]{1,0:T(8,128)(2,1)S(1)}, bf16[128,1024]{1,0:T(8,128)(2,1)S(1)}, u32[]{:S(2)}, u32[]{:S(2)}) collective-permute-start(bf16[128,1024]{1,0:T(8,128)(2,1)S(1)} %get-tuple-element.20), channel_id=1, source_target_pairs={{0,64},{64,0},{1,65},{65,1},{2,66},{66,2},{3,67},{67,3},{4,68},{68... | collective-permute-start | bytes 786440 | tf_op jit(solution)/shard_map/half_sum/ppermute | solution.py:25
  77.4 8.9 %collective-permute-done.3.other_ref = bf16[128,1024]{1,0:T(8,128)(2,1)S(1)} collective-permute-done((bf16[128,1024]{1,0:T(8,128)(2,1)S(1)}, bf16[128,1024]{1,0:T(8,128)(2,1)S(1)}, u32[]{:S(2)}, u32[]{:S(2)}) %collective-permute-start.3) | collective-permute-done | bytes 262176 | tf_op jit(solution)/shard_map/half_sum/ppermute | solution.py:25
  86.5 7.0 %collective-permute-start.4 = (bf16[128,1024]{1,0:T(8,128)(2,1)S(1)}, bf16[128,1024]{1,0:T(8,128)(2,1)S(1)}, u32[]{:S(2)}, u32[]{:S(2)}) collective-permute-start(bf16[128,1024]{1,0:T(8,128)(2,1)S(1)} %hidden_grad.1.d0_ref), channel_id=1, source_target_pairs={{0,64},{64,0},{1,65},{65,1},{2,66},{66,2},{3,67},{67,3},{4,68},{68... | collective-permute-start | bytes 786440 | tf_op jit(solution)/shard_map/d_far/ppermute | solution.py:25
  93.5 20.1 %collective-permute-done.4.d1_ref = bf16[128,1024]{1,0:T(8,128)(2,1)S(1)} collective-permute-done((bf16[128,1024]{1,0:T(8,128)(2,1)S(1)}, bf16[128,1024]{1,0:T(8,128)(2,1)S(1)}, u32[]{:S(2)}, u32[]{:S(2)}) %collective-permute-start.4) | collective-permute-done | bytes 262176 | tf_op jit(solution)/shard_map/d_far/ppermute | solution.py:25
  113.6 0.8 pad_maximum_fusion
  114.5 0.7 copy-done.8
  115.2 11.1 %all-gather.3.cloned.1.call-done.refs_1_ = bf16[16,128,1024]{2,1,0:T(8,128)(2,1)} async-done(((bf16[4,128,1024]{2,1,0:T(8,128)(2,1)}), bf16[16,128,1024]{2,1,0:T(8,128)(2,1)}) %all-gather.3.cloned.1.call-update) | async-done | bytes 4194320 | tf_op jit(solution)/shard_map/all_inputs/all_gather | solution.py:179
  126.3 1.2 copy-done.7
  127.5 0.9 copy-done.9
  128.5 1.8 input_grad.1
  130.3 12.0 %all_to_all.22 = bf16[4,128,1024]{2,1,0:T(8,128)(2,1)S(1)} all-to-all(bf16[4,128,1024]{2,1,0:T(8,128)(2,1)S(1)} %input_grad.1), channel_id=1, replica_groups=mesh['x'=4,'zh'=2,'c'=2,'y'=4,'zl'=8] {'y'}, dimensions={0} | all-to-all | bytes 2097152 | tf_op jit(solution)/shard_map/d_input/all_to_all | solution.py:191
  142.9 30.5 %all_to_all.23 = bf16[8,128,128]{2,1,0:T(8,128)(2,1)S(1)} all-to-all(bf16[8,128,128]{2,1,0:T(8,128)(2,1)S(1)} %copy.14), channel_id=1, replica_groups=mesh['x'=4,'zh'=2,'c'=2,'y'=4,'zl'=8] {'zl'}, dimensions={0} | all-to-all | bytes 524288 | tf_op jit(solution)/shard_map/d_input/all_to_all | solution.py:193
  173.7 2.2 %copy-done = bf16[16,128,1024]{2,1,0:T(8,128)(2,1)S(1)} copy-done((bf16[16,128,1024]{2,1,0:T(8,128)(2,1)S(1)}, bf16[16,128,1024]{2,1,0:T(8,128)(2,1)}, u32[]{:S(2)}) %copy-start) | copy-done | bytes 4194328
  175.9 1.6 copy-done.2
  177.5 2.9 %weight_grad_other.1 = bf16[1024,1024]{1,0:T(8,128)(2,1)S(1)} custom-call(s32[3]{0:T(128)S(1)} %pad_add_fusion.place_ref.refs_0_, bf16[16,128,1024]{2,1,0:T(8,128)(2,1)S(1)} %copy-done, bf16[8,128,1024]{2,1,0:T(8,128)(2,1)S(1)} %copy-done.2), custom_call_target="tpu_custom_call" | custom-call | flops 2147483648 | bytes 8388608 | tf_op jit(solution)/shard_map/weight_grads/weight_grad_other/pallas_call | solution.py:153
  180.4 7.7 %collective-permute-start.6 = (bf16[1024,1024]{1,0:T(8,128)(2,1)S(1)}, bf16[1024,1024]{1,0:T(8,128)(2,1)S(1)}, u32[]{:S(2)}, u32[]{:S(2)}) collective-permute-start(bf16[1024,1024]{1,0:T(8,128)(2,1)S(1)} %weight_grad_other.1), channel_id=1, source_target_pairs={{0,32},{32,0},{1,33},{33,1},{2,34},{34,2},{3,35},{35,3},{4,36},{36... | collective-permute-start | bytes 6291464 | tf_op jit(solution)/shard_map/weight_grads/ppermute | solution.py:25
  188.1 8.3 %collective-permute-start.5 = (bf16[128,128]{1,0:T(8,128)(2,1)S(1)}, bf16[128,128]{1,0:T(8,128)(2,1)S(1)}, u32[]{:S(2)}, u32[]{:S(2)}) collective-permute-start(bf16[128,128]{1,0:T(8,128)(2,1)S(1)} %reduce_sum.25), channel_id=1, source_target_pairs={{0,0},{8,8},{16,64},{24,72},{64,16},{72,24},{80,80},{88,88},{1,1},... | collective-permute-start | bytes 98312 | tf_op jit(solution)/shard_map/d_input/ppermute | solution.py:25
  196.4 7.5 %collective-permute-done.5 = bf16[128,128]{1,0:T(8,128)(2,1)S(1)} collective-permute-done((bf16[128,128]{1,0:T(8,128)(2,1)S(1)}, bf16[128,128]{1,0:T(8,128)(2,1)S(1)}, u32[]{:S(2)}, u32[]{:S(2)}) %collective-permute-start.5) | collective-permute-done | bytes 32800 | tf_op jit(solution)/shard_map/d_input/ppermute | solution.py:25
  203.9 2.9 %weight_grad_own.1 = f32[1024,1024]{1,0:T(8,128)S(1)} custom-call(s32[3]{0:T(128)S(1)} %pad_add_fusion.place_ref.refs_0_, bf16[16,128,1024]{2,1,0:T(8,128)(2,1)S(1)} %copy-done, bf16[8,128,1024]{2,1,0:T(8,128)(2,1)S(1)} %copy-done.2), custom_call_target="tpu_custom_call" | custom-call | flops 2147483648 | bytes 8388608 | tf_op jit(solution)/shard_map/weight_grads/weight_grad_own/pallas_call | solution.py:153
  206.8 2.1 fusion
  208.9 0.6 copy.16
  (32 shorter events, 1.7 us)
Async XLA Ops:
  7.2 119.1 %all-gather.3.cloned.1.call-start = ((), (), s32[]{:S(2)}) async-start(), calls=%async_computation.4 | async-start | bytes 5242880 | tf_op jit(solution)/shard_map/all_inputs/all_gather | solution.py:179
  7.2 45.1 %collective-permute-start.1 = (bf16[1024,512]{1,0:T(8,128)(2,1)}, bf16[1024,512]{1,0:T(8,128)(2,1)S(1)}, u32[]{:S(2)}, u32[]{:S(2)}) collective-permute-start(bf16[1024,512]{1,0:T(8,128)(2,1)} %g0_ref.1), channel_id=1, source_target_pairs={{0,32},{32,0},{1,33},{33,1},{2,34},{34,2},{3,35},{35,3},{4,36},{36... | collective-permute-start | bytes 3145736 | tf_op jit(solution)/shard_map/weights_of_chip/ppermute | solution.py:25
  9.8 42.5 %collective-permute-start.2 = (bf16[1024,512]{1,0:T(8,128)(2,1)}, bf16[1024,512]{1,0:T(8,128)(2,1)S(1)}, u32[]{:S(2)}, u32[]{:S(2)}) collective-permute-start(bf16[1024,512]{1,0:T(8,128)(2,1)} %u0_ref.1), channel_id=1, source_target_pairs={{0,32},{32,0},{1,33},{33,1},{2,34},{34,2},{3,35},{35,3},{4,36},{36... | collective-permute-start | bytes 3145736 | tf_op jit(solution)/shard_map/weights_of_chip/ppermute | solution.py:25
  12.6 17.4 %collective-permute-start = (bf16[128,128]{1,0:T(8,128)(2,1)S(1)}, bf16[128,128]{1,0:T(8,128)(2,1)S(1)}, u32[]{:S(2)}, u32[]{:S(2)}) collective-permute-start(bf16[128,128]{1,0:T(8,128)(2,1)S(1)} %multiply_convert_fusion), channel_id=1, source_target_pairs={{0,0},{8,8},{16,64},{24,72},{64,16},{72,24},{80,80},{88,88},{1,1},... | collective-permute-start | bytes 98312 | tf_op jit(solution)/shard_map/gather_inputs/ppermute | solution.py:25
  52.3 1.0 copy-start.5
  53.7 12.5 %copy-start.3 = (bf16[1024,512]{1,0:T(8,128)(2,1)S(1)}, bf16[1024,512]{1,0:T(8,128)(2,1)}, u32[]{:S(2)}) copy-start(bf16[1024,512]{1,0:T(8,128)(2,1)} %g0_ref.1) | copy-start | bytes 3145732
  53.7 12.5 %copy-start.4 = (bf16[1024,512]{1,0:T(8,128)(2,1)S(1)}, bf16[1024,512]{1,0:T(8,128)(2,1)}, u32[]{:S(2)}) copy-start(bf16[1024,512]{1,0:T(8,128)(2,1)} %u0_ref.1) | copy-start | bytes 3145732
  66.0 107.7 %all-gather.5.cloned.1.call-start = ((), (), s32[]{:S(2)}) async-start(), calls=%async_computation.5 | async-start | bytes 2621440 | tf_op jit(solution)/shard_map/d_over_x/all_gather | solution.py:188
  66.1 1.2 copy-start.1
  67.4 1.2 copy-start.6
  68.6 17.7 %copy-start.10 = (bf16[128,512]{1,0:T(8,128)(2,1)S(1)}, bf16[128,512]{1,0:T(8,128)(2,1)}, u32[]{:S(2)}) copy-start(bf16[128,512]{1,0:T(8,128)(2,1)} %grad_ref.1) | copy-start | bytes 393220
  70.4 15.9 %collective-permute-start.3 = (bf16[128,1024]{1,0:T(8,128)(2,1)S(1)}, bf16[128,1024]{1,0:T(8,128)(2,1)S(1)}, u32[]{:S(2)}, u32[]{:S(2)}) collective-permute-start(bf16[128,1024]{1,0:T(8,128)(2,1)S(1)} %get-tuple-element.20), channel_id=1, source_target_pairs={{0,64},{64,0},{1,65},{65,1},{2,66},{66,2},{3,67},{67,3},{4,68},{68... | collective-permute-start | bytes 786440 | tf_op jit(solution)/shard_map/half_sum/ppermute | solution.py:25
  86.5 27.1 %collective-permute-start.4 = (bf16[128,1024]{1,0:T(8,128)(2,1)S(1)}, bf16[128,1024]{1,0:T(8,128)(2,1)S(1)}, u32[]{:S(2)}, u32[]{:S(2)}) collective-permute-start(bf16[128,1024]{1,0:T(8,128)(2,1)S(1)} %hidden_grad.1.d0_ref), channel_id=1, source_target_pairs={{0,64},{64,0},{1,65},{65,1},{2,66},{66,2},{3,67},{67,3},{4,68},{68... | collective-permute-start | bytes 786440 | tf_op jit(solution)/shard_map/d_far/ppermute | solution.py:25
  114.5 0.7 copy-start.8
  126.3 1.2 copy-start.7
  127.5 0.9 copy-start.9
  173.7 2.2 %copy-start = (bf16[16,128,1024]{2,1,0:T(8,128)(2,1)S(1)}, bf16[16,128,1024]{2,1,0:T(8,128)(2,1)}, u32[]{:S(2)}) copy-start(bf16[16,128,1024]{2,1,0:T(8,128)(2,1)} %all-gather.3.cloned.1.call-done.refs_1_) | copy-start | bytes 12582916
  175.9 1.6 copy-start.2
  180.4 26.4 %collective-permute-start.6 = (bf16[1024,1024]{1,0:T(8,128)(2,1)S(1)}, bf16[1024,1024]{1,0:T(8,128)(2,1)S(1)}, u32[]{:S(2)}, u32[]{:S(2)}) collective-permute-start(bf16[1024,1024]{1,0:T(8,128)(2,1)S(1)} %weight_grad_other.1), channel_id=1, source_target_pairs={{0,32},{32,0},{1,33},{33,1},{2,34},{34,2},{3,35},{35,3},{4,36},{36... | collective-permute-start | bytes 6291464 | tf_op jit(solution)/shard_map/weight_grads/ppermute | solution.py:25
  188.1 15.8 %collective-permute-start.5 = (bf16[128,128]{1,0:T(8,128)(2,1)S(1)}, bf16[128,128]{1,0:T(8,128)(2,1)S(1)}, u32[]{:S(2)}, u32[]{:S(2)}) collective-permute-start(bf16[128,128]{1,0:T(8,128)(2,1)S(1)} %reduce_sum.25), channel_id=1, source_target_pairs={{0,0},{8,8},{16,64},{24,72},{64,16},{72,24},{80,80},{88,88},{1,1},... | collective-permute-start | bytes 98312 | tf_op jit(solution)/shard_map/d_input/ppermute | solution.py:25
Sparse Core Ops, SparseCore 0:
  66.1 60.1 all-gather.2
  129.0 44.6 all-gather.4

commit v5 on v4

v5 whole, which is shorter than its diff:
```python
import jax
import jax.numpy as jnp
import numpy as np
from jax import lax
from jax.experimental import pallas as pl
from jax.experimental.pallas import tpu as pltpu
from jax.sharding import Mesh, PartitionSpec as P

AXES = ("x", "zh", "c", "y", "zl")
SIZES = {"x": 4, "zh": 2, "c": 2, "y": 4, "zl": 8}
ROWS = ("x", "zh", "c")
COLS = ("y", "zl")
SHARD = ("zh", "c")
F32 = jnp.float32
BF16 = jnp.bfloat16


def permute(value, axes, target):
    sizes = [SIZES[a] for a in axes]
    pairs = []
    for i in range(int(np.prod(sizes))):
        at = dict(zip(axes, map(int, np.unravel_index(i, sizes))))
        to = target(at)
        pairs.append((i, int(np.ravel_multi_index([to[a] for a in axes], sizes))))
    return lax.ppermute(value, axes if len(axes) > 1 else axes[0], pairs)


def swap_half_y(value):
    return permute(
        value, ("zh", "y"), lambda d: {"zh": d["y"] // 2, "y": d["zh"] * 2 + d["y"] % 2}
    )


def swap_core(value):
    return permute(value, ("c",), lambda d: {"c": 1 - d["c"]})


def swap_half(value):
    return permute(value, ("zh",), lambda d: {"zh": 1 - d["zh"]})


def step_outer(value, k):
    return permute(value, ("x",), lambda d: {"x": (d["x"] + k) % 4})


def spread(value, axis):
    n = SIZES[axis]
    return lax.all_to_all(jnp.broadcast_to(value[None], (n,) + value.shape), axis, 0, 0)


VMEM = pl.BlockSpec(memory_space=pltpu.VMEM)
HBM = pl.BlockSpec(memory_space=pltpu.MemorySpace.HBM)
SMEM = pl.BlockSpec(memory_space=pltpu.SMEM)
PARAMS = pltpu.CompilerParams(vmem_limit_bytes=24 * 1024 * 1024)


def partial_kernel(place_ref, x_ref, g_ref, u_ref, keep_ref, send_ref):
    half = place_ref[0]
    count, ff = x_ref.shape[1], g_ref.shape[2]
    x = [jnp.concatenate([x_ref[2 * (1 - half) + b], x_ref[2 * half + b]], axis=0) for b in range(2)]
    for k, w in enumerate((g_ref, u_ref)):
        total = jnp.dot(x[0], w[0], preferred_element_type=F32)
        total = total + jnp.dot(x[1], w[1], preferred_element_type=F32)
        send_ref[:, k * ff : (k + 1) * ff] = total[:count].astype(BF16)
        keep_ref[:, k * ff : (k + 1) * ff] = total[count:]


def partial_gate_up(place, x, weights):
    count, ff = x.shape[1], weights[0].shape[2]
    flops = 2 * 4 * count * x.shape[2] * 2 * ff
    return pl.pallas_call(
        partial_kernel,
        out_shape=(
            jax.ShapeDtypeStruct((count, 2 * ff), F32),
            jax.ShapeDtypeStruct((count, 2 * ff), BF16),
        ),
        in_specs=[SMEM] + [VMEM] * 3,
        out_specs=(VMEM, VMEM),
        compiler_params=PARAMS,
        cost_estimate=pl.CostEstimate(flops=flops, bytes_accessed=6 << 20, transcendentals=0),
        name="partial_gate_up",
    )(place, x, *weights)


def hidden_grad_kernel(keep_ref, other_ref, grad_ref, out_ref):
    ff = grad_ref.shape[1]
    gate = keep_ref[:, :ff] + other_ref[:, :ff].astype(F32)
    up = keep_ref[:, ff:] + other_ref[:, ff:].astype(F32)
    grad_out = grad_ref[...].astype(F32)
    sig = jax.nn.sigmoid(gate)
    out_ref[:, :ff] = (grad_out * up * sig * (1.0 + gate * (1.0 - sig))).astype(BF16)
    out_ref[:, ff:] = (grad_out * gate * sig).astype(BF16)


def hidden_grad(keep, other, grad):
    return pl.pallas_call(
        hidden_grad_kernel,
        out_shape=jax.ShapeDtypeStruct(keep.shape, BF16),
        in_specs=[VMEM] * 3,
        out_specs=VMEM,
        compiler_params=PARAMS,
        cost_estimate=pl.CostEstimate(flops=1 << 20, bytes_accessed=1 << 20, transcendentals=1 << 16),
        name="hidden_grad",
    )(keep, other, grad)


def input_grad_kernel(place_ref, d0_ref, d1_ref, g_ref, u_ref, out_ref, both_ref):
    half = place_ref[0]
    count, ff = d0_ref.shape[0], g_ref.shape[2]
    dims = (((1,), (1,)), ((), ()))
    both_ref[0], both_ref[1] = d0_ref[...], d1_ref[...]
    d = jnp.concatenate([d0_ref[...], d1_ref[...]], axis=0)
    for b in range(2):
        total = lax.dot_general(d[:, :ff], g_ref[b], dims, preferred_element_type=F32)
        total = total + lax.dot_general(d[:, ff:], u_ref[b], dims, preferred_element_type=F32)
        out_ref[2 * half + b] = total[:count].astype(BF16)
        out_ref[2 * (1 - half) + b] = total[count:].astype(BF16)


def input_grad(place, d_own, d_other, weights):
    (count, cols), rows = d_own.shape, weights[0].shape[1]
    flops = 2 * 4 * count * rows * cols
    return pl.pallas_call(
        input_grad_kernel,
        out_shape=(
            jax.ShapeDtypeStruct((4, count, rows), BF16),
            jax.ShapeDtypeStruct((2, count, cols), BF16),
        ),
        in_specs=[SMEM] + [VMEM] * 4,
        out_specs=(VMEM, VMEM),
        compiler_params=PARAMS,
        cost_estimate=pl.CostEstimate(flops=flops, bytes_accessed=6 << 20, transcendentals=0),
        name="input_grad",
    )(place, d_own, d_other, *weights)


STEP = 256


def weight_grad_rows(place_ref, x_ref, d_ref, x_held, d_held, x_sem, d_sem, other):
    half, core = place_ref[0], place_ref[1]
    b = 1 - core if other else core
    tiles = x_ref.shape[3] // STEP

    def columns(i):
        return pltpu.make_async_copy(
            x_ref.at[:, b, :, pl.ds(i * STEP, STEP)], x_held.at[i], x_sem.at[i]
        )

    def tokens(a):
        r = half if a == 0 else 1 - half
        return pltpu.make_async_copy(d_ref.at[:, r], d_held.at[:, a], d_sem.at[a])

    copies = [tokens(0), tokens(1)] + [columns(i) for i in range(tiles)]
    for copy in copies:
        copy.start()
    copies[0].wait()
    copies[1].wait()
    d = d_held[...].reshape(-1, d_held.shape[3])
    for i in range(tiles):
        copies[2 + i].wait()
        x = x_held[i].reshape(-1, STEP)
        yield slice(i * STEP, (i + 1) * STEP), lax.dot_general(
            x, d, (((0,), (0,)), ((), ())), preferred_element_type=F32
        )


def weight_grad_other_kernel(place_ref, x_ref, d_ref, out_ref, *scratch):
    for at, total in weight_grad_rows(place_ref, x_ref, d_ref, *scratch, True):
        out_ref[at, :] = total.astype(BF16)


def weight_grad_own_kernel(place_ref, x_ref, d_ref, got_ref, gate_ref, up_ref, *scratch):
    ff = gate_ref.shape[1]
    *scratch, got_held, got_sem = scratch
    copy = pltpu.make_async_copy(got_ref, got_held, got_sem.at[0])
    copy.start()
    for at, total in weight_grad_rows(place_ref, x_ref, d_ref, *scratch, False):
        if at.start == 0:
            copy.wait()
        total = (total + got_held[at, :].astype(F32)).astype(BF16)
        gate_ref[at, :] = total[:, :ff]
        up_ref[at, :] = total[:, ff:]


def weight_grad(kernel, name, place, inputs, d, got, shapes):
    pairs, _, count, rows = inputs.shape
    cols = d.shape[3]
    flops = 2 * pairs * count * rows * cols
    return pl.pallas_call(
        kernel,
        out_shape=[jax.ShapeDtypeStruct(v, BF16) for v in shapes],
        in_specs=[SMEM, HBM, HBM] + [HBM] * len(got),
        out_specs=[VMEM] * len(shapes),
        scratch_shapes=[
            pltpu.VMEM((rows // STEP, pairs, count, STEP), BF16),
            pltpu.VMEM((pairs // 2, 2, count, cols), BF16),
            pltpu.SemaphoreType.DMA((rows // STEP,)),
            pltpu.SemaphoreType.DMA((2,)),
        ]
        + [v for g in got for v in (pltpu.VMEM(g.shape, BF16), pltpu.SemaphoreType.DMA((1,)))],
        compiler_params=pltpu.CompilerParams(vmem_limit_bytes=58 * 1024 * 1024),
        cost_estimate=pl.CostEstimate(flops=flops, bytes_accessed=8 << 20, transcendentals=0),
        name=name,
    )(place, inputs, d, *got)


def shards(quantized, scales, d_hidden, w_gate, w_up):
    count, width = quantized.shape
    rows, ff = w_gate.shape
    place = jnp.stack([lax.axis_index("zh"), lax.axis_index("c"), lax.axis_index("x")]).astype(jnp.int32)
    with jax.named_scope("weights_of_chip"):
        weights = tuple(lax.all_gather(w, "c", axis=0) for w in (w_gate, w_up))
    local = (quantized.astype(F32) * scales).astype(BF16)
    with jax.named_scope("gather_inputs"):
        held = spread(swap_half_y(local), "zl")
        held, weights = lax.optimization_barrier((held, weights))
        held = held.transpose(1, 0, 2).reshape(count, rows)
        inputs = spread(held, "y")
    with jax.named_scope("partial_gate_up"):
        keep, sent = partial_gate_up(place, inputs, weights)
    with jax.named_scope("all_inputs"):
        all_inputs = lax.all_gather(inputs, "x", axis=0, tiled=True)
    with jax.named_scope("half_sum"):
        other = swap_half(sent)
    with jax.named_scope("hidden_grad"):
        d_own = hidden_grad(keep, other, d_hidden)
    with jax.named_scope("d_far"):
        d_far = swap_half(d_own)
    with jax.named_scope("d_input"):
        di, d_both = input_grad(place, d_own, d_far, weights)
        di = jnp.sum(lax.all_to_all(di, "y", 0, 0).astype(F32), axis=0).astype(BF16)
        di = di.reshape(count, 8, width).transpose(1, 0, 2)
        di_z = jnp.sum(lax.all_to_all(di, "zl", 0, 0).astype(F32), axis=0).astype(BF16)
        di = swap_half_y(di_z)
    with jax.named_scope("d_over_x"):
        d_both, all_inputs = lax.optimization_barrier((d_both, all_inputs))
        d_all = lax.all_gather(d_both, "x", axis=0, tiled=True)
    with jax.named_scope("weight_grads"):
        d_all, _ = lax.optimization_barrier((d_all, di_z))
        d_all = d_all.reshape(4, 2, count, 2 * ff)
        all_inputs = all_inputs.reshape(8, 2, count, rows)
        (sent,) = weight_grad(
            weight_grad_other_kernel, "weight_grad_other", place, all_inputs, d_all, (), [(rows, 2 * ff)]
        )
        d_gate_weight, d_up_weight = weight_grad(
            weight_grad_own_kernel,
            "weight_grad_own",
            place,
            all_inputs,
            d_all,
            (swap_core(sent),),
            [(rows, ff)] * 2,
        )
    return lax.optimization_barrier((di, d_gate_weight, d_up_weight))


def solution(mesh):
    fine = Mesh(mesh.devices.reshape([SIZES[a] for a in AXES]), AXES)
    in_specs = (P(ROWS, COLS), P(ROWS, COLS), P(ROWS, COLS), P(SHARD, COLS), P(SHARD, COLS))
    out_specs = (P(ROWS, COLS), P(SHARD, COLS), P(SHARD, COLS))
    return jax.shard_map(shards, mesh=fine, in_specs=in_specs, out_specs=out_specs, check_vma=False)
```

time: 218 us -> 226 us (1.037)
  blocking collectives: 76.9 us -> 90.6 us
  waiting for transfers between devices: 49.2 us -> 40 us
  Pallas kernels: 9.65 us -> 17.7 us
  starting transfers between devices: 50.7 us -> 56 us
  local copies, waits for them, and re-layouts: 11.5 us -> 6.44 us
  other arithmetic: 4.08 us -> 0.39 us
    ppermute x7 -> x5, waiting for transfers between devices: 37.8 us -> 21.6 us  [permute(): return lax.ppermute(value, axes if len(axes) > 1 else axes[0], pairs)]
    all_gather x1 -> x3, waiting for transfers between devices: 0.25 us -> 11.8 us  [the longest x2 11.7 us: shards(): weights = tuple((lax.all_gather(w, 'c', axis=0) for w in (w_gate, w_up)))]
    pallas_call x3, Pallas kernels: 7.69 us -> 15.7 us  [the longest x2 13.9 us: weight_grad(): pl.pallas_call(kernel, out_shape=[jax.ShapeDtypeStruct(v, BF16) for v in...]
    all_gather x1, waiting for transfers between devices: 11.1 us -> 5.26 us  [shards(): all_inputs = lax.all_gather(inputs, 'x', axis=0, tiled=True)]
    all_to_all x2, blocking collectives: 34.4 us -> 39.9 us  [spread(): lax.all_to_all(jnp.broadcast_to(value[None], (n,) + value.shape), axis, 0...]
    ppermute x7 -> x5, starting transfers between devices: 50.6 us -> 55.8 us  [permute(): return lax.ppermute(value, axes if len(axes) > 1 else axes[0], pairs)]
    unnamed x23 -> x21, local copies, waits for them, and re-layouts: 10.7 us -> 5.61 us
    all_to_all x1, blocking collectives: 12 us -> 16.4 us  [shards(): di = jnp.sum(lax.all_to_all(di, 'y', 0, 0).astype(F32), axis=0).astype(BF16)]
  transfers between devices with their start and end apart: 9 -> 9, of which waited for: 6 -> 5; matrix products, arithmetic and copies ran while one was open for 1% -> 0% of each run, Pallas kernels for 3% -> 5%
where the time goes in v5:
time: 226 us; the launch traced here: 225 us
  blocking collectives  90.6 us (40%)
  starting transfers between devices  56 us (25%)
  waiting for transfers between devices  40 us (18%)
  Pallas kernels  17.7 us (8%)
  between operations  14 us (6%)
  local copies, waits for them, and re-layouts  6.44 us (3%)
    ppermute x5, starting transfers between devices, permute(): return lax.ppermute(value, axes if len(axes) > 1 else axes[0], pairs)  55.8 us
    all_to_all x2, blocking collectives, spread(): lax.all_to_all(jnp.broadcast_to(value[None], (n,) + value.shape), axis, 0...  39.9 us
    all_to_all x1, blocking collectives, shards(): lax.all_to_all(di, 'zl', 0, 0).astype(F32)  34.2 us
    ppermute x5, waiting for transfers between devices, permute(): return lax.ppermute(value, axes if len(axes) > 1 else axes[0], pairs)  21.6 us
    all_to_all x1, blocking collectives, shards(): di = jnp.sum(lax.all_to_all(di, 'y', 0, 0).astype(F32), axis=0).astype(BF16)  16.4 us
    pallas_call x2, Pallas kernels, weight_grad(): pl.pallas_call(kernel, out_shape=[jax.ShapeDtypeStruct(v, BF16) for v in...  13.9 us
    all_gather x2, waiting for transfers between devices, shards(): weights = tuple((lax.all_gather(w, 'c', axis=0) for w in (w_gate, w_up)))  11.7 us
    unnamed x21, local copies, waits for them, and re-layouts  5.61 us
  transfers between devices with their start and end apart: 9, of which 5 were waited for; matrix products, arithmetic and copies ran while one was open for 0% of the time, Pallas kernels for 5%

profile of v5, /device:TPU:25, one launch (start us, length us, event | category | flops | bytes accessed | tf_op | source)
XLA Modules:
  0.0 225.1 jit_solution(18003570076907975691)
XLA Ops:
  7.2 0.7 all-gather.11.cloned.1.call-update
  8.0 0.7 all-gather.13.cloned.1.call-update
  8.8 16.1 %collective-permute-start = (bf16[128,128]{1,0:T(8,128)(2,1)S(1)}, bf16[128,128]{1,0:T(8,128)(2,1)S(1)}, u32[]{:S(2)}, u32[]{:S(2)}) collective-permute-start(bf16[128,128]{1,0:T(8,128)(2,1)S(1)} %multiply_convert_fusion), channel_id=1, source_target_pairs={{0,0},{8,8},{16,64},{24,72},{64,16},{72,24},{80,80},{88,88},{1,1},... | collective-permute-start | bytes 98312 | tf_op jit(solution)/shard_map/gather_inputs/ppermute | solution.py:25
  24.9 1.3 collective-permute-done
  26.3 22.3 %all_to_all.20 = bf16[8,128,128]{2,1,0:T(8,128)(2,1)S(1)} all-to-all(bf16[8,128,128]{2,1,0:T(8,128)(2,1)S(1)} %broadcast_in_dim.6), channel_id=1, replica_groups=mesh['x'=4,'zh'=2,'c'=2,'y'=4,'zl'=8] {'zl'}, dimensions={0} | all-to-all | bytes 524288 | tf_op jit(solution)/shard_map/gather_inputs/all_to_all | solution.py:48
  48.6 11.7 %all-gather.13.cloned.1.call-done = bf16[2048,512]{1,0:T(8,128)(2,1)} async-done(((bf16[1024,512]{1,0:T(8,128)(2,1)}), bf16[2048,512]{1,0:T(8,128)(2,1)}) %all-gather.13.cloned.1.call-update) | async-done | bytes 2097168 | tf_op jit(solution)/shard_map/weights_of_chip/all_gather | solution.py:213
  60.3 0.2 copy.11
  60.5 0.1 copy.12
  60.7 0.1 broadcast_in_dim.15
  60.8 17.6 %all_to_all.21.x_ref = bf16[4,128,1024]{2,1,0:T(8,128)(2,1)} all-to-all(bf16[4,128,1024]{2,1,0:T(8,128)(2,1)S(1)} %broadcast_in_dim.15), channel_id=1, replica_groups=mesh['x'=4,'zh'=2,'c'=2,'y'=4,'zl'=8] {'y'}, dimensions={0} | all-to-all | bytes 2097152 | tf_op jit(solution)/shard_map/gather_inputs/all_to_all | solution.py:48
  78.6 1.2 copy-done
  79.8 1.6 copy-done.2
  81.4 1.8 partial_gate_up.1
  83.2 12.1 %collective-permute-start.1 = (bf16[128,1024]{1,0:T(8,128)(2,1)S(1)}, bf16[128,1024]{1,0:T(8,128)(2,1)S(1)}, u32[]{:S(2)}, u32[]{:S(2)}) collective-permute-start(bf16[128,1024]{1,0:T(8,128)(2,1)S(1)} %get-tuple-element.19), channel_id=1, source_target_pairs={{0,64},{64,0},{1,65},{65,1},{2,66},{66,2},{3,67},{67,3},{4,68},{68... | collective-permute-start | bytes 786440 | tf_op jit(solution)/shard_map/half_sum/ppermute | solution.py:25
  95.3 11.6 %collective-permute-done.1.other_ref = bf16[128,1024]{1,0:T(8,128)(2,1)S(1)} collective-permute-done((bf16[128,1024]{1,0:T(8,128)(2,1)S(1)}, bf16[128,1024]{1,0:T(8,128)(2,1)S(1)}, u32[]{:S(2)}, u32[]{:S(2)}) %collective-permute-start.1) | collective-permute-done | bytes 262176 | tf_op jit(solution)/shard_map/half_sum/ppermute | solution.py:25
  107.0 0.2 hidden_grad.1.d0_ref
  107.1 12.1 %collective-permute-start.2 = (bf16[128,1024]{1,0:T(8,128)(2,1)S(1)}, bf16[128,1024]{1,0:T(8,128)(2,1)S(1)}, u32[]{:S(2)}, u32[]{:S(2)}) collective-permute-start(bf16[128,1024]{1,0:T(8,128)(2,1)S(1)} %hidden_grad.1.d0_ref), channel_id=1, source_target_pairs={{0,64},{64,0},{1,65},{65,1},{2,66},{66,2},{3,67},{67,3},{4,68},{68... | collective-permute-start | bytes 786440 | tf_op jit(solution)/shard_map/d_far/ppermute | solution.py:25
  119.3 8.6 %collective-permute-done.2.d1_ref = bf16[128,1024]{1,0:T(8,128)(2,1)S(1)} collective-permute-done((bf16[128,1024]{1,0:T(8,128)(2,1)S(1)}, bf16[128,1024]{1,0:T(8,128)(2,1)S(1)}, u32[]{:S(2)}, u32[]{:S(2)}) %collective-permute-start.2) | collective-permute-done | bytes 262176 | tf_op jit(solution)/shard_map/d_far/ppermute | solution.py:25
  127.9 1.9 input_grad.1
  129.8 0.8 copy-done.4
  130.6 5.3 %all-gather.7.cloned.1.call-done = bf16[16,128,1024]{2,1,0:T(8,128)(2,1)} async-done(((bf16[4,128,1024]{2,1,0:T(8,128)(2,1)}), bf16[16,128,1024]{2,1,0:T(8,128)(2,1)}) %all-gather.7.cloned.1.call-update) | async-done | bytes 4194320 | tf_op jit(solution)/shard_map/all_inputs/all_gather | solution.py:223
  135.8 16.4 %all_to_all.22 = bf16[4,128,1024]{2,1,0:T(8,128)(2,1)S(1)} all-to-all(bf16[4,128,1024]{2,1,0:T(8,128)(2,1)S(1)} %get-tuple-element.20), channel_id=1, replica_groups=mesh['x'=4,'zh'=2,'c'=2,'y'=4,'zl'=8] {'y'}, dimensions={0} | all-to-all | bytes 2097152 | tf_op jit(solution)/shard_map/d_input/all_to_all | solution.py:232
  152.3 0.2 reduce_sum.24
  152.5 0.2 copy.13
  152.6 0.2 copy.14
  152.8 34.2 %all_to_all.23 = bf16[8,128,128]{2,1,0:T(8,128)(2,1)S(1)} all-to-all(bf16[8,128,128]{2,1,0:T(8,128)(2,1)S(1)} %copy.14), channel_id=1, replica_groups=mesh['x'=4,'zh'=2,'c'=2,'y'=4,'zl'=8] {'zl'}, dimensions={0} | all-to-all | bytes 524288 | tf_op jit(solution)/shard_map/d_input/all_to_all | solution.py:234
  187.1 6.8 %weight_grad_other.1 = bf16[1024,1024]{1,0:T(8,128)(2,1)} custom-call(s32[3]{0:T(128)} %copy-done.6, bf16[8,2,128,1024]{3,2,1,0:T(8,128)(2,1)} %bitcast.18, bf16[4,2,128,1024]{3,2,1,0:T(8,128)(2,1)} %bitcast.20), custom_call_target="tpu_custom_call" | custom-call | flops 2147483648 | bytes 8388608 | tf_op jit(solution)/shard_map/weight_grads/weight_grad_other/pallas_call | solution.py:190
  193.9 8.0 %collective-permute-start.4 = (bf16[1024,1024]{1,0:T(8,128)(2,1)}, bf16[1024,1024]{1,0:T(8,128)(2,1)S(1)}, u32[]{:S(2)}, u32[]{:S(2)}) collective-permute-start(bf16[1024,1024]{1,0:T(8,128)(2,1)} %weight_grad_other.1), channel_id=1, source_target_pairs={{0,32},{32,0},{1,33},{33,1},{2,34},{34,2},{3,35},{35,3},{4,36},{36... | collective-permute-start | bytes 6291464 | tf_op jit(solution)/shard_map/weight_grads/ppermute | solution.py:25
  201.9 7.5 %collective-permute-start.3 = (bf16[128,128]{1,0:T(8,128)(2,1)S(1)}, bf16[128,128]{1,0:T(8,128)(2,1)S(1)}, u32[]{:S(2)}, u32[]{:S(2)}) collective-permute-start(bf16[128,128]{1,0:T(8,128)(2,1)S(1)} %reduce_sum.25), channel_id=1, source_target_pairs={{0,0},{8,8},{16,64},{24,72},{64,16},{72,24},{80,80},{88,88},{1,1},... | collective-permute-start | bytes 98312 | tf_op jit(solution)/shard_map/d_input/ppermute | solution.py:25
  209.4 1.4 copy-done.7
  210.8 7.1 %weight_grad_own.1 = (bf16[1024,512]{1,0:T(8,128)(2,1)}, bf16[1024,512]{1,0:T(8,128)(2,1)}) custom-call(s32[3]{0:T(128)} %copy-done.6, bf16[8,2,128,1024]{3,2,1,0:T(8,128)(2,1)} %bitcast.19, bf16[4,2,128,1024]{3,2,1,0:T(8,128)(2,1)} %bitcast.21, bf16[1024,1024]{1,0:T(8,128)(2,1)} %copy-done.7), custom_call_target="tpu_custom_call" | custom-call | flops 2147483648 | bytes 8388608 | tf_op jit(solution)/shard_map/weight_grads/weight_grad_own/pallas_call | solution.py:190
  217.9 0.6 copy.16
  (30 shorter events, 0.5 us)
Async XLA Ops:
  7.2 1.6 copy-start.9
  7.2 1.6 copy-start.8
  7.2 41.4 %all-gather.11.cloned.1.call-start = ((), (), s32[]{:S(2)}) async-start(), calls=%async_computation.6 | async-start | bytes 3145728 | tf_op jit(solution)/shard_map/weights_of_chip/all_gather | solution.py:213
  7.9 52.4 %all-gather.13.cloned.1.call-start = ((), (), s32[]{:S(2)}) async-start(), calls=%async_computation.7 | async-start | bytes 3145728 | tf_op jit(solution)/shard_map/weights_of_chip/all_gather | solution.py:213
  8.7 127.2 %all-gather.7.cloned.1.call-start = ((), (), s32[]{:S(2)}) async-start(), calls=%async_computation.4 | async-start | bytes 5242880 | tf_op jit(solution)/shard_map/all_inputs/all_gather | solution.py:223
  8.8 17.4 %collective-permute-start = (bf16[128,128]{1,0:T(8,128)(2,1)S(1)}, bf16[128,128]{1,0:T(8,128)(2,1)S(1)}, u32[]{:S(2)}, u32[]{:S(2)}) collective-permute-start(bf16[128,128]{1,0:T(8,128)(2,1)S(1)} %multiply_convert_fusion), channel_id=1, source_target_pairs={{0,0},{8,8},{16,64},{24,72},{64,16},{72,24},{80,80},{88,88},{1,1},... | collective-permute-start | bytes 98312 | tf_op jit(solution)/shard_map/gather_inputs/ppermute | solution.py:25
  60.7 17.9 %copy-start.1 = (bf16[2048,512]{1,0:T(8,128)(2,1)S(1)}, bf16[2048,512]{1,0:T(8,128)(2,1)}, u32[]{:S(2)}) copy-start(bf16[2048,512]{1,0:T(8,128)(2,1)} %all-gather.11.cloned.1.call-done) | copy-start | bytes 6291460
  78.5 108.7 %all-gather.9.cloned.1.call-start = ((), (), s32[]{:S(2)}) async-start(), calls=%async_computation.5 | async-start | bytes 2621440 | tf_op jit(solution)/shard_map/d_over_x/all_gather | solution.py:238
  78.6 1.2 copy-start
  79.8 1.6 copy-start.2
  81.4 46.5 %copy-start.6 = (s32[3]{0:T(128)}, s32[3]{0:T(128)S(1)}, u32[]{:S(2)}) copy-start(s32[3]{0:T(128)S(1)} %pad_add_fusion.place_ref) | copy-start | bytes 40
  81.4 25.6 %copy-start.5 = (bf16[128,512]{1,0:T(8,128)(2,1)S(1)}, bf16[128,512]{1,0:T(8,128)(2,1)}, u32[]{:S(2)}) copy-start(bf16[128,512]{1,0:T(8,128)(2,1)} %grad_ref.1) | copy-start | bytes 393220
  81.4 46.5 %copy-start.3 = (bf16[2048,512]{1,0:T(8,128)(2,1)S(1)}, bf16[2048,512]{1,0:T(8,128)(2,1)}, u32[]{:S(2)}) copy-start(bf16[2048,512]{1,0:T(8,128)(2,1)} %all-gather.13.cloned.1.call-done) | copy-start | bytes 6291460
  83.2 23.7 %collective-permute-start.1 = (bf16[128,1024]{1,0:T(8,128)(2,1)S(1)}, bf16[128,1024]{1,0:T(8,128)(2,1)S(1)}, u32[]{:S(2)}, u32[]{:S(2)}) collective-permute-start(bf16[128,1024]{1,0:T(8,128)(2,1)S(1)} %get-tuple-element.19), channel_id=1, source_target_pairs={{0,64},{64,0},{1,65},{65,1},{2,66},{66,2},{3,67},{67,3},{4,68},{68... | collective-permute-start | bytes 786440 | tf_op jit(solution)/shard_map/half_sum/ppermute | solution.py:25
  107.1 20.8 %collective-permute-start.2 = (bf16[128,1024]{1,0:T(8,128)(2,1)S(1)}, bf16[128,1024]{1,0:T(8,128)(2,1)S(1)}, u32[]{:S(2)}, u32[]{:S(2)}) collective-permute-start(bf16[128,1024]{1,0:T(8,128)(2,1)S(1)} %hidden_grad.1.d0_ref), channel_id=1, source_target_pairs={{0,64},{64,0},{1,65},{65,1},{2,66},{66,2},{3,67},{67,3},{4,68},{68... | collective-permute-start | bytes 786440 | tf_op jit(solution)/shard_map/d_far/ppermute | solution.py:25
  129.8 0.8 copy-start.4
  193.9 15.5 %collective-permute-start.4 = (bf16[1024,1024]{1,0:T(8,128)(2,1)}, bf16[1024,1024]{1,0:T(8,128)(2,1)S(1)}, u32[]{:S(2)}, u32[]{:S(2)}) collective-permute-start(bf16[1024,1024]{1,0:T(8,128)(2,1)} %weight_grad_other.1), channel_id=1, source_target_pairs={{0,32},{32,0},{1,33},{33,1},{2,34},{34,2},{3,35},{35,3},{4,36},{36... | collective-permute-start | bytes 6291464 | tf_op jit(solution)/shard_map/weight_grads/ppermute | solution.py:25
  201.9 16.0 %collective-permute-start.3 = (bf16[128,128]{1,0:T(8,128)(2,1)S(1)}, bf16[128,128]{1,0:T(8,128)(2,1)S(1)}, u32[]{:S(2)}, u32[]{:S(2)}) collective-permute-start(bf16[128,128]{1,0:T(8,128)(2,1)S(1)} %reduce_sum.25), channel_id=1, source_target_pairs={{0,0},{8,8},{16,64},{24,72},{64,16},{72,24},{80,80},{88,88},{1,1},... | collective-permute-start | bytes 98312 | tf_op jit(solution)/shard_map/d_input/ppermute | solution.py:25
  209.4 1.4 copy-start.7
Sparse Core Ops, SparseCore 0:
  10.1 25.6 all-gather.10
  37.9 22.3 all-gather.12
  78.6 57.1 all-gather.6
  138.4 47.1 all-gather.8

commit v6 on v4

--- a/solution.py
+++ b/solution.py
@@ -50,7 +50,7 @@
 
 VMEM = pl.BlockSpec(memory_space=pltpu.VMEM)
 SMEM = pl.BlockSpec(memory_space=pltpu.SMEM)
-PARAMS = pltpu.CompilerParams(vmem_limit_bytes=32 * 1024 * 1024)
+PARAMS = pltpu.CompilerParams(vmem_limit_bytes=12 * 1024 * 1024)
 
 
 def partial_kernel(place_ref, x_ref, g0_ref, u0_ref, g1_ref, u1_ref, keep_ref, send_ref):
@@ -120,8 +120,8 @@
 
 
 def input_grad(place, d_own, d_other, weights):
-    count, rows = d_own.shape[0], weights[0].shape[0]
-    flops = 2 * 4 * count * rows * d_own.shape[1]
+    (count, cols), rows = d_own.shape, weights[0].shape[0]
+    flops = 2 * 4 * count * rows * cols
     return pl.pallas_call(
         input_grad_kernel,
         out_shape=jax.ShapeDtypeStruct((4, count, rows), BF16),
@@ -133,44 +133,55 @@
     )(place, d_own, d_other, *weights)
 
 
-def weight_grad_kernel(other, place_ref, x_ref, d_ref, out_ref):
+def weight_grad_rows(place_ref, x_ref, d_ref, other):
     half, core = place_ref[0], place_ref[1]
     b = 1 - core if other else core
-    rows = x_ref.shape[2]
     step = 256
     d = jnp.concatenate([d_ref[k] for k in range(8)], axis=0)
-    for i in range(0, rows, step):
+    for i in range(0, x_ref.shape[2], step):
         x = [x_ref[4 * k + 2 * a + b, :, i : i + step] for k in range(4) for a in (half, 1 - half)]
-        total = lax.dot_general(
+        yield slice(i, i + step), lax.dot_general(
             jnp.concatenate(x, axis=0), d, (((0,), (0,)), ((), ())), preferred_element_type=F32
         )
-        out_ref[i : i + step, :] = total.astype(out_ref.dtype)
-
-
-def weight_grad(other, place, inputs, d, dtype):
-    rows, cols = inputs.shape[2], d.shape[2]
-    flops = 2 * 8 * d.shape[1] * rows * cols
-    return pl.pallas_call(
-        lambda *refs: weight_grad_kernel(other, *refs),
-        out_shape=jax.ShapeDtypeStruct((rows, cols), dtype),
-        in_specs=[SMEM] + [VMEM] * 2,
-        out_specs=VMEM,
+
+
+def weight_grad_other_kernel(place_ref, x_ref, d_ref, out_ref):
+    for at, total in weight_grad_rows(place_ref, x_ref, d_ref, True):
+        out_ref[at, :] = total.astype(BF16)
+
+
+def weight_grad_own_kernel(place_ref, x_ref, d_ref, got_ref, gate_ref, up_ref):
+    ff = gate_ref.shape[1]
+    for at, total in weight_grad_rows(place_ref, x_ref, d_ref, False):
+        total = (total + got_ref[at, :].astype(F32)).astype(BF16)
+        gate_ref[at, :] = total[:, :ff]
+        up_ref[at, :] = total[:, ff:]
+
+
+def weight_grad(kernel, name, place, inputs, d, got, shapes):
+    flops = 2 * 8 * d.shape[1] * inputs.shape[2] * d.shape[2]
+    return pl.pallas_call(
+        kernel,
+        out_shape=[jax.ShapeDtypeStruct(v, BF16) for v in shapes],
+        in_specs=[SMEM] + [VMEM] * (2 + len(got)),
+        out_specs=[VMEM] * len(shapes),
         compiler_params=PARAMS,
         cost_estimate=pl.CostEstimate(flops=flops, bytes_accessed=8 << 20, transcendentals=0),
-        name="weight_grad_other" if other else "weight_grad_own",
-    )(place, inputs, d)
+        name=name,
+    )(place, inputs, d, *got)
 
 
 def shards(quantized, scales, d_hidden, w_gate, w_up):
     count, width = quantized.shape
     rows, ff = w_gate.shape
     place = jnp.stack([lax.axis_index("zh"), lax.axis_index("c"), lax.axis_index("x")]).astype(jnp.int32)
-    with jax.named_scope("weights_of_chip"):
-        weights = (w_gate, w_up, swap_core(w_gate), swap_core(w_up))
     local = (quantized.astype(F32) * scales).astype(BF16)
     with jax.named_scope("gather_inputs"):
-        held = spread(swap_half_y(local), "zl")
-        held, weights = lax.optimization_barrier((held, weights))
+        held, gate_sent, up_sent = lax.optimization_barrier((swap_half_y(local), w_gate, w_up))
+        others = swap_core(gate_sent), swap_core(up_sent)
+        held = spread(held, "zl")
+        held, *others = lax.optimization_barrier((held, *others))
+        weights = (w_gate, w_up, *others)
         held = held.transpose(1, 0, 2).reshape(count, rows)
         inputs = spread(held, "y")
     with jax.named_scope("partial_gate_up"):
@@ -183,23 +194,31 @@
         d_own = hidden_grad(keep, other, d_hidden)
     with jax.named_scope("d_far"):
         d_far = swap_half(d_own)
-    with jax.named_scope("d_over_x"):
-        d, all_inputs = lax.optimization_barrier((jnp.stack([d_own, d_far]), all_inputs))
-        d_all = lax.all_gather(d, "x", axis=0, tiled=True)
     with jax.named_scope("d_input"):
         di = input_grad(place, d_own, d_far, weights)
+        di, d_own, d_far = lax.optimization_barrier((di, d_own, d_far))
         di = jnp.sum(lax.all_to_all(di, "y", 0, 0).astype(F32), axis=0).astype(BF16)
         di = di.reshape(count, 8, width).transpose(1, 0, 2)
         di_z = jnp.sum(lax.all_to_all(di, "zl", 0, 0).astype(F32), axis=0).astype(BF16)
         di = swap_half_y(di_z)
+    with jax.named_scope("d_over_x"):
+        d_both, all_inputs = lax.optimization_barrier((jnp.stack([d_own, d_far]), all_inputs))
+        d_all = lax.all_gather(d_both, "x", axis=0, tiled=True)
     with jax.named_scope("weight_grads"):
-        d_all, all_inputs, _ = lax.optimization_barrier((d_all, all_inputs, di_z))
-        got = swap_core(weight_grad(True, place, all_inputs, d_all, BF16))
-        dw = weight_grad(False, place, all_inputs, d_all, F32)
-        d_gate_weight, d_up_weight = (
-            (dw[:, k : k + ff] + got[:, k : k + ff].astype(F32)).astype(BF16) for k in (0, ff)
+        d_all, _ = lax.optimization_barrier((d_all, di_z))
+        (sent,) = weight_grad(
+            weight_grad_other_kernel, "weight_grad_other", place, all_inputs, d_all, (), [(rows, 2 * ff)]
         )
-    return di, d_gate_weight, d_up_weight
+        d_gate_weight, d_up_weight = weight_grad(
+            weight_grad_own_kernel,
+            "weight_grad_own",
+            place,
+            all_inputs,
+            d_all,
+            (swap_core(sent),),
+            [(rows, ff)] * 2,
+        )
+    return lax.optimization_barrier((di, d_gate_weight, d_up_weight))
 
 
 def solution(mesh):

time: 218 us -> 216 us (level)
  waiting for transfers between devices: 49.2 us -> 42.6 us
  blocking collectives: 76.9 us -> 83.4 us
    all_to_all x1, blocking collectives: 30.5 us -> 36.4 us  [shards(): lax.all_to_all(di, 'zl', 0, 0).astype(F32)]
    ppermute x7, waiting for transfers between devices: 37.8 us -> 33.1 us  [permute(): return lax.ppermute(value, axes if len(axes) > 1 else axes[0], pairs)]
    all_gather x1, waiting for transfers between devices: 11.1 us -> 8.77 us  [shards(): all_inputs = lax.all_gather(inputs, 'x', axis=0, tiled=True)]
  transfers between devices with their start and end apart: 9 -> 9, of which waited for: 6 -> 6; matrix products, arithmetic and copies ran while one was open for 1% -> 1% of each run, Pallas kernels for 3% -> 4%
where the time goes in v6:
time: 216 us; the launch traced here: 214 us
  blocking collectives  83.4 us (39%)
  starting transfers between devices  51.6 us (24%)
  waiting for transfers between devices  42.6 us (20%)
  between operations  14.2 us (7%)
  Pallas kernels  10.7 us (5%)
  local copies, waits for them, and re-layouts  9.91 us (5%)
    ppermute x7, starting transfers between devices, permute(): return lax.ppermute(value, axes if len(axes) > 1 else axes[0], pairs)  51.5 us
    all_to_all x1, blocking collectives, shards(): lax.all_to_all(di, 'zl', 0, 0).astype(F32)  36.4 us
    all_to_all x2, blocking collectives, spread(): lax.all_to_all(jnp.broadcast_to(value[None], (n,) + value.shape), axis, 0...  35 us
    ppermute x7, waiting for transfers between devices, permute(): return lax.ppermute(value, axes if len(axes) > 1 else axes[0], pairs)  33.1 us
    all_to_all x1, blocking collectives, shards(): di = jnp.sum(lax.all_to_all(di, 'y', 0, 0).astype(F32), axis=0).astype(BF16)  12 us
    unnamed x23, local copies, waits for them, and re-layouts  9.08 us
    all_gather x1, waiting for transfers between devices, shards(): all_inputs = lax.all_gather(inputs, 'x', axis=0, tiled=True)  8.77 us
    pallas_call x2, Pallas kernels, weight_grad(): pl.pallas_call(kernel, out_shape=[jax.ShapeDtypeStruct(v, BF16) for v in...  6.95 us
  transfers between devices with their start and end apart: 9, of which 6 were waited for; matrix products, arithmetic and copies ran while one was open for 1% of the time, Pallas kernels for 4%

profile of v6, /device:TPU:25, one launch (start us, length us, event | category | flops | bytes accessed | tf_op | source)
XLA Modules:
  0.0 214.5 jit_solution(1489665286626715141)
XLA Ops:
  7.2 0.8 multiply_convert_fusion
  8.1 16.1 %collective-permute-start = (bf16[128,128]{1,0:T(8,128)(2,1)S(1)}, bf16[128,128]{1,0:T(8,128)(2,1)S(1)}, u32[]{:S(2)}, u32[]{:S(2)}) collective-permute-start(bf16[128,128]{1,0:T(8,128)(2,1)S(1)} %multiply_convert_fusion), channel_id=1, source_target_pairs={{0,0},{8,8},{16,64},{24,72},{64,16},{72,24},{80,80},{88,88},{1,1},... | collective-permute-start | bytes 98312 | tf_op jit(solution)/shard_map/gather_inputs/ppermute | solution.py:25
  24.2 1.3 collective-permute-done
  25.5 3.4 %collective-permute-start.1 = (bf16[1024,512]{1,0:T(8,128)(2,1)}, bf16[1024,512]{1,0:T(8,128)(2,1)S(1)}, u32[]{:S(2)}, u32[]{:S(2)}) collective-permute-start(bf16[1024,512]{1,0:T(8,128)(2,1)} %g0_ref.3), channel_id=1, source_target_pairs={{0,32},{32,0},{1,33},{33,1},{2,34},{34,2},{3,35},{35,3},{4,36},{36... | collective-permute-start | bytes 3145736 | tf_op jit(solution)/shard_map/gather_inputs/ppermute | solution.py:25
  28.9 1.9 collective-permute-start.2
  30.9 22.8 %all_to_all.20 = bf16[8,128,128]{2,1,0:T(8,128)(2,1)S(1)} all-to-all(bf16[8,128,128]{2,1,0:T(8,128)(2,1)S(1)} %broadcast_in_dim.6), channel_id=1, replica_groups=mesh['x'=4,'zh'=2,'c'=2,'y'=4,'zl'=8] {'zl'}, dimensions={0} | all-to-all | bytes 524288 | tf_op jit(solution)/shard_map/gather_inputs/all_to_all | solution.py:48
  53.8 1.0 copy-done.7
  55.2 12.2 %all_to_all.21.x_ref = bf16[4,128,1024]{2,1,0:T(8,128)(2,1)} all-to-all(bf16[4,128,1024]{2,1,0:T(8,128)(2,1)S(1)} %broadcast_in_dim.15), channel_id=1, replica_groups=mesh['x'=4,'zh'=2,'c'=2,'y'=4,'zl'=8] {'y'}, dimensions={0} | all-to-all | bytes 2097152 | tf_op jit(solution)/shard_map/gather_inputs/all_to_all | solution.py:48
  67.6 1.2 copy-done.1
  68.8 1.2 copy-done.8
  70.0 1.8 partial_gate_up.1
  71.8 7.0 %collective-permute-start.3 = (bf16[128,1024]{1,0:T(8,128)(2,1)S(1)}, bf16[128,1024]{1,0:T(8,128)(2,1)S(1)}, u32[]{:S(2)}, u32[]{:S(2)}) collective-permute-start(bf16[128,1024]{1,0:T(8,128)(2,1)S(1)} %get-tuple-element.26), channel_id=1, source_target_pairs={{0,64},{64,0},{1,65},{65,1},{2,66},{66,2},{3,67},{67,3},{4,68},{68... | collective-permute-start | bytes 786440 | tf_op jit(solution)/shard_map/half_sum/ppermute | solution.py:25
  78.9 8.9 %collective-permute-done.3.other_ref = bf16[128,1024]{1,0:T(8,128)(2,1)S(1)} collective-permute-done((bf16[128,1024]{1,0:T(8,128)(2,1)S(1)}, bf16[128,1024]{1,0:T(8,128)(2,1)S(1)}, u32[]{:S(2)}, u32[]{:S(2)}) %collective-permute-start.3) | collective-permute-done | bytes 262176 | tf_op jit(solution)/shard_map/half_sum/ppermute | solution.py:25
  87.9 7.0 %collective-permute-start.4 = (bf16[128,1024]{1,0:T(8,128)(2,1)S(1)}, bf16[128,1024]{1,0:T(8,128)(2,1)S(1)}, u32[]{:S(2)}, u32[]{:S(2)}) collective-permute-start(bf16[128,1024]{1,0:T(8,128)(2,1)S(1)} %hidden_grad.1.d0_ref), channel_id=1, source_target_pairs={{0,64},{64,0},{1,65},{65,1},{2,66},{66,2},{3,67},{67,3},{4,68},{68... | collective-permute-start | bytes 786440 | tf_op jit(solution)/shard_map/d_far/ppermute | solution.py:25
  95.0 19.8 %collective-permute-done.4.d1_ref = bf16[128,1024]{1,0:T(8,128)(2,1)S(1)} collective-permute-done((bf16[128,1024]{1,0:T(8,128)(2,1)S(1)}, bf16[128,1024]{1,0:T(8,128)(2,1)S(1)}, u32[]{:S(2)}, u32[]{:S(2)}) %collective-permute-start.4) | collective-permute-done | bytes 262176 | tf_op jit(solution)/shard_map/d_far/ppermute | solution.py:25
  114.8 1.2 copy-done.6
  116.0 1.8 input_grad.1
  117.9 0.8 pad_maximum_fusion
  118.7 8.8 %all-gather.3.cloned.1.call-done.x_ref = bf16[16,128,1024]{2,1,0:T(8,128)(2,1)} async-done(((bf16[4,128,1024]{2,1,0:T(8,128)(2,1)}), bf16[16,128,1024]{2,1,0:T(8,128)(2,1)}) %all-gather.3.cloned.1.call-update) | async-done | bytes 4194320 | tf_op jit(solution)/shard_map/all_inputs/all_gather | solution.py:190
  127.5 12.0 %all_to_all.22 = bf16[4,128,1024]{2,1,0:T(8,128)(2,1)S(1)} all-to-all(bf16[4,128,1024]{2,1,0:T(8,128)(2,1)S(1)} %input_grad.1), channel_id=1, replica_groups=mesh['x'=4,'zh'=2,'c'=2,'y'=4,'zl'=8] {'y'}, dimensions={0} | all-to-all | bytes 2097152 | tf_op jit(solution)/shard_map/d_input/all_to_all | solution.py:200
  139.5 0.2 reduce_sum.24
  139.9 0.2 copy.14
  140.0 36.4 %all_to_all.23 = bf16[8,128,128]{2,1,0:T(8,128)(2,1)S(1)} all-to-all(bf16[8,128,128]{2,1,0:T(8,128)(2,1)S(1)} %copy.14), channel_id=1, replica_groups=mesh['x'=4,'zh'=2,'c'=2,'y'=4,'zl'=8] {'zl'}, dimensions={0} | all-to-all | bytes 524288 | tf_op jit(solution)/shard_map/d_input/all_to_all | solution.py:202
  176.5 0.7 all-gather.5.cloned.1.call-done.d_ref
  177.2 2.2 %copy-done = bf16[16,128,1024]{2,1,0:T(8,128)(2,1)S(1)} copy-done((bf16[16,128,1024]{2,1,0:T(8,128)(2,1)S(1)}, bf16[16,128,1024]{2,1,0:T(8,128)(2,1)}, u32[]{:S(2)}) %copy-start) | copy-done | bytes 4194328
  179.4 1.6 copy-done.2
  181.0 2.9 %weight_grad_other.1 = bf16[1024,1024]{1,0:T(8,128)(2,1)S(1)} custom-call(s32[3]{0:T(128)S(1)} %pad_add_fusion.place_ref, bf16[16,128,1024]{2,1,0:T(8,128)(2,1)S(1)} %copy-done, bf16[8,128,1024]{2,1,0:T(8,128)(2,1)S(1)} %copy-done.2), custom_call_target="tpu_custom_call" | custom-call | flops 2147483648 | bytes 8388608 | tf_op jit(solution)/shard_map/weight_grads/weight_grad_other/pallas_call | solution.py:163
  183.9 7.3 %collective-permute-start.6 = (bf16[1024,1024]{1,0:T(8,128)(2,1)S(1)}, bf16[1024,1024]{1,0:T(8,128)(2,1)S(1)}, u32[]{:S(2)}, u32[]{:S(2)}) collective-permute-start(bf16[1024,1024]{1,0:T(8,128)(2,1)S(1)} %weight_grad_other.1), channel_id=1, source_target_pairs={{0,32},{32,0},{1,33},{33,1},{2,34},{34,2},{3,35},{35,3},{4,36},{36... | collective-permute-start | bytes 6291464 | tf_op jit(solution)/shard_map/weight_grads/ppermute | solution.py:25
  191.2 8.7 %collective-permute-start.5 = (bf16[128,128]{1,0:T(8,128)(2,1)S(1)}, bf16[128,128]{1,0:T(8,128)(2,1)S(1)}, u32[]{:S(2)}, u32[]{:S(2)}) collective-permute-start(bf16[128,128]{1,0:T(8,128)(2,1)S(1)} %reduce_sum.25), channel_id=1, source_target_pairs={{0,0},{8,8},{16,64},{24,72},{64,16},{72,24},{80,80},{88,88},{1,1},... | collective-permute-start | bytes 98312 | tf_op jit(solution)/shard_map/d_input/ppermute | solution.py:25
  199.9 4.0 %weight_grad_own.1 = (bf16[1024,512]{1,0:T(8,128)(2,1)}, bf16[1024,512]{1,0:T(8,128)(2,1)}) custom-call(s32[3]{0:T(128)S(1)} %pad_add_fusion.place_ref, bf16[16,128,1024]{2,1,0:T(8,128)(2,1)S(1)} %copy-done, bf16[8,128,1024]{2,1,0:T(8,128)(2,1)S(1)} %copy-done.2, bf16[1024,1024]{1,0:T(8,128)(2,1)S(1)} %collective-permute-done.6.got_ref), custom_call_target="tpu_custom_call" | custom-call | flops 2147483648 | bytes 8388608 | tf_op jit(solution)/shard_map/weight_grads/weight_grad_own/pallas_call | solution.py:163
  203.9 3.1 %collective-permute-done.5 = bf16[128,128]{1,0:T(8,128)(2,1)S(1)} collective-permute-done((bf16[128,128]{1,0:T(8,128)(2,1)S(1)}, bf16[128,128]{1,0:T(8,128)(2,1)S(1)}, u32[]{:S(2)}, u32[]{:S(2)}) %collective-permute-start.5) | collective-permute-done | bytes 32800 | tf_op jit(solution)/shard_map/d_input/ppermute | solution.py:25
  207.0 0.6 copy.16
  (31 shorter events, 1.1 us)
Async XLA Ops:
  7.2 120.3 %all-gather.3.cloned.1.call-start = ((), (), s32[]{:S(2)}) async-start(), calls=%async_computation.4 | async-start | bytes 5242880 | tf_op jit(solution)/shard_map/all_inputs/all_gather | solution.py:190
  8.1 17.4 %collective-permute-start = (bf16[128,128]{1,0:T(8,128)(2,1)S(1)}, bf16[128,128]{1,0:T(8,128)(2,1)S(1)}, u32[]{:S(2)}, u32[]{:S(2)}) collective-permute-start(bf16[128,128]{1,0:T(8,128)(2,1)S(1)} %multiply_convert_fusion), channel_id=1, source_target_pairs={{0,0},{8,8},{16,64},{24,72},{64,16},{72,24},{80,80},{88,88},{1,1},... | collective-permute-start | bytes 98312 | tf_op jit(solution)/shard_map/gather_inputs/ppermute | solution.py:25
  25.5 28.3 %collective-permute-start.1 = (bf16[1024,512]{1,0:T(8,128)(2,1)}, bf16[1024,512]{1,0:T(8,128)(2,1)S(1)}, u32[]{:S(2)}, u32[]{:S(2)}) collective-permute-start(bf16[1024,512]{1,0:T(8,128)(2,1)} %g0_ref.3), channel_id=1, source_target_pairs={{0,32},{32,0},{1,33},{33,1},{2,34},{34,2},{3,35},{35,3},{4,36},{36... | collective-permute-start | bytes 3145736 | tf_op jit(solution)/shard_map/gather_inputs/ppermute | solution.py:25
  28.9 24.8 %collective-permute-start.2 = (bf16[1024,512]{1,0:T(8,128)(2,1)}, bf16[1024,512]{1,0:T(8,128)(2,1)S(1)}, u32[]{:S(2)}, u32[]{:S(2)}) collective-permute-start(bf16[1024,512]{1,0:T(8,128)(2,1)} %u0_ref.3), channel_id=1, source_target_pairs={{0,32},{32,0},{1,33},{33,1},{2,34},{34,2},{3,35},{35,3},{4,36},{36... | collective-permute-start | bytes 3145736 | tf_op jit(solution)/shard_map/gather_inputs/ppermute | solution.py:25
  53.8 13.8 %copy-start.5 = (bf16[1024,512]{1,0:T(8,128)(2,1)}, bf16[1024,512]{1,0:T(8,128)(2,1)S(1)}, u32[]{:S(2)}) copy-start(bf16[1024,512]{1,0:T(8,128)(2,1)S(1)} %collective-permute-done.1.g1_ref) | copy-start | bytes 3145732
  53.8 1.0 copy-start.7
  55.1 12.5 %copy-start.3 = (bf16[1024,512]{1,0:T(8,128)(2,1)S(1)}, bf16[1024,512]{1,0:T(8,128)(2,1)}, u32[]{:S(2)}) copy-start(bf16[1024,512]{1,0:T(8,128)(2,1)} %g0_ref.3) | copy-start | bytes 3145732
  55.1 12.5 %copy-start.4 = (bf16[1024,512]{1,0:T(8,128)(2,1)S(1)}, bf16[1024,512]{1,0:T(8,128)(2,1)}, u32[]{:S(2)}) copy-start(bf16[1024,512]{1,0:T(8,128)(2,1)} %u0_ref.3) | copy-start | bytes 3145732
  67.4 109.8 %all-gather.5.cloned.1.call-start = ((), (), s32[]{:S(2)}) async-start(), calls=%async_computation.5 | async-start | bytes 2621440 | tf_op jit(solution)/shard_map/d_over_x/all_gather | solution.py:206
  67.6 1.2 copy-start.1
  68.8 1.2 copy-start.8
  70.0 17.7 %copy-start.10 = (bf16[128,512]{1,0:T(8,128)(2,1)S(1)}, bf16[128,512]{1,0:T(8,128)(2,1)}, u32[]{:S(2)}) copy-start(bf16[128,512]{1,0:T(8,128)(2,1)} %grad_ref.1) | copy-start | bytes 393220
  70.0 44.8 %copy-start.9 = (bf16[1024,512]{1,0:T(8,128)(2,1)S(1)}, bf16[1024,512]{1,0:T(8,128)(2,1)}, u32[]{:S(2)}) copy-start(bf16[1024,512]{1,0:T(8,128)(2,1)} %copy-done.7) | copy-start | bytes 3145732
  71.8 15.9 %collective-permute-start.3 = (bf16[128,1024]{1,0:T(8,128)(2,1)S(1)}, bf16[128,1024]{1,0:T(8,128)(2,1)S(1)}, u32[]{:S(2)}, u32[]{:S(2)}) collective-permute-start(bf16[128,1024]{1,0:T(8,128)(2,1)S(1)} %get-tuple-element.26), channel_id=1, source_target_pairs={{0,64},{64,0},{1,65},{65,1},{2,66},{66,2},{3,67},{67,3},{4,68},{68... | collective-permute-start | bytes 786440 | tf_op jit(solution)/shard_map/half_sum/ppermute | solution.py:25
  87.9 26.9 %collective-permute-start.4 = (bf16[128,1024]{1,0:T(8,128)(2,1)S(1)}, bf16[128,1024]{1,0:T(8,128)(2,1)S(1)}, u32[]{:S(2)}, u32[]{:S(2)}) collective-permute-start(bf16[128,1024]{1,0:T(8,128)(2,1)S(1)} %hidden_grad.1.d0_ref), channel_id=1, source_target_pairs={{0,64},{64,0},{1,65},{65,1},{2,66},{66,2},{3,67},{67,3},{4,68},{68... | collective-permute-start | bytes 786440 | tf_op jit(solution)/shard_map/d_far/ppermute | solution.py:25
  114.8 1.2 copy-start.6
  177.2 2.2 %copy-start = (bf16[16,128,1024]{2,1,0:T(8,128)(2,1)S(1)}, bf16[16,128,1024]{2,1,0:T(8,128)(2,1)}, u32[]{:S(2)}) copy-start(bf16[16,128,1024]{2,1,0:T(8,128)(2,1)} %all-gather.3.cloned.1.call-done.x_ref) | copy-start | bytes 12582916
  179.4 1.6 copy-start.2
  183.9 16.0 %collective-permute-start.6 = (bf16[1024,1024]{1,0:T(8,128)(2,1)S(1)}, bf16[1024,1024]{1,0:T(8,128)(2,1)S(1)}, u32[]{:S(2)}, u32[]{:S(2)}) collective-permute-start(bf16[1024,1024]{1,0:T(8,128)(2,1)S(1)} %weight_grad_other.1), channel_id=1, source_target_pairs={{0,32},{32,0},{1,33},{33,1},{2,34},{34,2},{3,35},{35,3},{4,36},{36... | collective-permute-start | bytes 6291464 | tf_op jit(solution)/shard_map/weight_grads/ppermute | solution.py:25
  191.2 15.8 %collective-permute-start.5 = (bf16[128,128]{1,0:T(8,128)(2,1)S(1)}, bf16[128,128]{1,0:T(8,128)(2,1)S(1)}, u32[]{:S(2)}, u32[]{:S(2)}) collective-permute-start(bf16[128,128]{1,0:T(8,128)(2,1)S(1)} %reduce_sum.25), channel_id=1, source_target_pairs={{0,0},{8,8},{16,64},{24,72},{64,16},{72,24},{80,80},{88,88},{1,1},... | collective-permute-start | bytes 98312 | tf_op jit(solution)/shard_map/d_input/ppermute | solution.py:25
Sparse Core Ops, SparseCore 0:
  67.6 59.8 all-gather.2
  130.2 46.9 all-gather.4

commit v7 on v6

--- a/solution.py
+++ b/solution.py
@@ -177,15 +177,14 @@
     place = jnp.stack([lax.axis_index("zh"), lax.axis_index("c"), lax.axis_index("x")]).astype(jnp.int32)
     local = (quantized.astype(F32) * scales).astype(BF16)
     with jax.named_scope("gather_inputs"):
-        held, gate_sent, up_sent = lax.optimization_barrier((swap_half_y(local), w_gate, w_up))
-        others = swap_core(gate_sent), swap_core(up_sent)
-        held = spread(held, "zl")
-        held, *others = lax.optimization_barrier((held, *others))
-        weights = (w_gate, w_up, *others)
+        held = spread(swap_half_y(local), "zl")
         held = held.transpose(1, 0, 2).reshape(count, rows)
         inputs = spread(held, "y")
+        inputs, *others = lax.optimization_barrier((inputs, swap_core(w_gate), swap_core(w_up)))
+        weights = (w_gate, w_up, *others)
     with jax.named_scope("partial_gate_up"):
         keep, sent = partial_gate_up(place, inputs, weights)
+        inputs, sent = lax.optimization_barrier((inputs, sent))
     with jax.named_scope("all_inputs"):
         all_inputs = lax.all_gather(inputs, "x", axis=0, tiled=True)
     with jax.named_scope("half_sum"):
@@ -199,16 +198,15 @@
         di, d_own, d_far = lax.optimization_barrier((di, d_own, d_far))
         di = jnp.sum(lax.all_to_all(di, "y", 0, 0).astype(F32), axis=0).astype(BF16)
         di = di.reshape(count, 8, width).transpose(1, 0, 2)
-        di_z = jnp.sum(lax.all_to_all(di, "zl", 0, 0).astype(F32), axis=0).astype(BF16)
-        di = swap_half_y(di_z)
+        di = lax.all_to_all(di, "zl", 0, 0)
     with jax.named_scope("d_over_x"):
         d_both, all_inputs = lax.optimization_barrier((jnp.stack([d_own, d_far]), all_inputs))
         d_all = lax.all_gather(d_both, "x", axis=0, tiled=True)
     with jax.named_scope("weight_grads"):
-        d_all, _ = lax.optimization_barrier((d_all, di_z))
         (sent,) = weight_grad(
             weight_grad_other_kernel, "weight_grad_other", place, all_inputs, d_all, (), [(rows, 2 * ff)]
         )
+        di, sent = lax.optimization_barrier((di, sent))
         d_gate_weight, d_up_weight = weight_grad(
             weight_grad_own_kernel,
             "weight_grad_own",
@@ -218,6 +216,8 @@
             (swap_core(sent),),
             [(rows, ff)] * 2,
         )
+    with jax.named_scope("d_input"):
+        di = swap_half_y(jnp.sum(di.astype(F32), axis=0).astype(BF16))
     return lax.optimization_barrier((di, d_gate_weight, d_up_weight))
 
 

time: 216 us -> 212 us (0.981)
  blocking collectives: 83.4 us -> 12 us
  starting transfers between devices: 51.6 us -> 85.8 us
  waiting for transfers between devices: 42.6 us -> 69.4 us
  Pallas kernels: 10.7 us -> 14.2 us
  local copies, waits for them, and re-layouts: 9.91 us -> 13 us
    all_to_all x3 -> x0, blocking collectives: 71.4 us -> none  [the longest x1 36.4 us: shards(): lax.all_to_all(di, 'zl', 0, 0).astype(F32)]
    all_to_all x0 -> x3, starting transfers between devices: none -> 33.2 us  [the longest x1 18.5 us: shards(): di = lax.all_to_all(di, 'zl', 0, 0)]
    all_to_all x0 -> x3, waiting for transfers between devices: none -> 13.9 us  [the longest x2 13.9 us: spread(): lax.all_to_all(jnp.broadcast_to(value[None], (n,) + value.shape), axis, 0...]
    all_gather x1, waiting for transfers between devices: 0.68 us -> 13.4 us  [shards(): d_all = lax.all_gather(d_both, 'x', axis=0, tiled=True)]
    all_gather x1, waiting for transfers between devices: 8.77 us -> 13.3 us  [shards(): all_inputs = lax.all_gather(inputs, 'x', axis=0, tiled=True)]
    ppermute x7, waiting for transfers between devices: 33.1 us -> 28.7 us  [permute(): return lax.ppermute(value, axes if len(axes) > 1 else axes[0], pairs)]
  transfers between devices with their start and end apart: 9 -> 12, of which waited for: 6 -> 7; matrix products, arithmetic and copies ran while one was open for 1% -> 2% of each run, Pallas kernels for 4% -> 5%
where the time goes in v7:
time: 212 us; the launch traced here: 211 us
  starting transfers between devices  85.8 us (40%)
  waiting for transfers between devices  69.4 us (33%)
  Pallas kernels  14.2 us (7%)
  between operations  14.2 us (7%)
  local copies, waits for them, and re-layouts  13 us (6%)
  blocking collectives  12 us (6%)
    ppermute x7, starting transfers between devices, permute(): return lax.ppermute(value, axes if len(axes) > 1 else axes[0], pairs)  52.6 us
    ppermute x7, waiting for transfers between devices, permute(): return lax.ppermute(value, axes if len(axes) > 1 else axes[0], pairs)  28.7 us
    all_to_all x1, starting transfers between devices, shards(): di = lax.all_to_all(di, 'zl', 0, 0)  18.5 us
    all_to_all x2, starting transfers between devices, spread(): lax.all_to_all(jnp.broadcast_to(value[None], (n,) + value.shape), axis, 0...  14.7 us
    all_to_all x2, waiting for transfers between devices, spread(): lax.all_to_all(jnp.broadcast_to(value[None], (n,) + value.shape), axis, 0...  13.9 us
    all_gather x1, waiting for transfers between devices, shards(): d_all = lax.all_gather(d_both, 'x', axis=0, tiled=True)  13.4 us
    all_gather x1, waiting for transfers between devices, shards(): all_inputs = lax.all_gather(inputs, 'x', axis=0, tiled=True)  13.3 us
    all_to_all x1, blocking collectives, shards(): di = jnp.sum(lax.all_to_all(di, 'y', 0, 0).astype(F32), axis=0).astype(BF16)  12 us
  transfers between devices with their start and end apart: 12, of which 7 were waited for; matrix products, arithmetic and copies ran while one was open for 2% of the time, Pallas kernels for 5%

profile of v7, /device:TPU:25, one launch (start us, length us, event | category | flops | bytes accessed | tf_op | source)
XLA Modules:
  0.0 210.6 jit_solution(8348452178834399114)
XLA Ops:
  7.2 0.8 multiply_convert_fusion
  8.0 16.1 %collective-permute-start = (bf16[128,128]{1,0:T(8,128)(2,1)S(1)}, bf16[128,128]{1,0:T(8,128)(2,1)S(1)}, u32[]{:S(2)}, u32[]{:S(2)}) collective-permute-start(bf16[128,128]{1,0:T(8,128)(2,1)S(1)} %multiply_convert_fusion), channel_id=1, source_target_pairs={{0,0},{8,8},{16,64},{24,72},{64,16},{72,24},{80,80},{88,88},{1,1},... | collective-permute-start | bytes 98312 | tf_op jit(solution)/shard_map/gather_inputs/ppermute | solution.py:25
  24.1 1.3 collective-permute-done
  26.2 10.6 %all-to-all-start = ((bf16[8,128,128]{2,1,0:T(8,128)(2,1)}), bf16[8,128,128]{2,1,0:T(8,128)(2,1)S(1)}, u32[]{:S(2)}, u32[]{:S(2)}) async-start(bf16[8,128,128]{2,1,0:T(8,128)(2,1)} %broadcast_in_dim.6), calls=%async_computation | async-start | bytes 524288 | tf_op jit(solution)/shard_map/gather_inputs/all_to_all | solution.py:48
  36.8 4.0 %collective-permute-start.1 = (bf16[1024,512]{1,0:T(8,128)(2,1)}, bf16[1024,512]{1,0:T(8,128)(2,1)}, u32[]{:S(2)}, u32[]{:S(2)}) collective-permute-start(bf16[1024,512]{1,0:T(8,128)(2,1)} %g0_ref.3), channel_id=1, source_target_pairs={{0,32},{32,0},{1,33},{33,1},{2,34},{34,2},{3,35},{35,3},{4,36},{36... | collective-permute-start | bytes 3145736 | tf_op jit(solution)/shard_map/gather_inputs/ppermute | solution.py:25
  40.8 1.9 collective-permute-start.2
  42.7 6.0 %all-to-all-done = bf16[8,128,128]{2,1,0:T(8,128)(2,1)S(1)} async-done(((bf16[8,128,128]{2,1,0:T(8,128)(2,1)}), bf16[8,128,128]{2,1,0:T(8,128)(2,1)S(1)}, u32[]{:S(2)}, u32[]{:S(2)}) %all-to-all-start) | async-done | bytes 262176 | tf_op jit(solution)/shard_map/gather_inputs/all_to_all | solution.py:48
  49.1 1.1 broadcast_in_dim.15
  50.2 4.1 %all-to-all-start.1 = ((bf16[4,128,1024]{2,1,0:T(8,128)(2,1)}), bf16[4,128,1024]{2,1,0:T(8,128)(2,1)S(1)}, u32[]{:S(2)}, u32[]{:S(2)}) async-start(bf16[4,128,1024]{2,1,0:T(8,128)(2,1)} %broadcast_in_dim.15), calls=%async_computation.1 | async-start | bytes 2097152 | tf_op jit(solution)/shard_map/gather_inputs/all_to_all | solution.py:48
  54.4 7.9 %all-to-all-done.1.x_ref = bf16[4,128,1024]{2,1,0:T(8,128)(2,1)S(1)} async-done(((bf16[4,128,1024]{2,1,0:T(8,128)(2,1)}), bf16[4,128,1024]{2,1,0:T(8,128)(2,1)S(1)}, u32[]{:S(2)}, u32[]{:S(2)}) %all-to-all-start.1) | async-done | bytes 1048608 | tf_op jit(solution)/shard_map/gather_inputs/all_to_all | solution.py:48
  62.3 3.2 %partial_gate_up.1 = (f32[128,1024]{1,0:T(8,128)S(1)}, bf16[128,1024]{1,0:T(8,128)(2,1)S(1)}) custom-call(s32[3]{0:T(128)S(1)} %pad_add_fusion.place_ref, bf16[4,128,1024]{2,1,0:T(8,128)(2,1)S(1)} %all-to-all-done.1.x_ref, bf16[1024,512]{1,0:T(8,128)(2,1)S(1)} %copy-done.5, bf16[1024,512]{1,0:T(8,128)(2,1)S(1)} %copy-done.6, ...), custom_call_target="tpu_custom_call" | custom-call | flops 1073741824 | bytes 6291456 | tf_op jit(solution)/shard_map/partial_gate_up/partial_gate_up/pallas_call | solution.py:74
  65.6 0.8 copy-done.8
  66.4 7.3 %collective-permute-start.3 = (bf16[128,1024]{1,0:T(8,128)(2,1)S(1)}, bf16[128,1024]{1,0:T(8,128)(2,1)S(1)}, u32[]{:S(2)}, u32[]{:S(2)}) collective-permute-start(bf16[128,1024]{1,0:T(8,128)(2,1)S(1)} %get-tuple-element.24), channel_id=1, source_target_pairs={{0,64},{64,0},{1,65},{65,1},{2,66},{66,2},{3,67},{67,3},{4,68},{68... | collective-permute-start | bytes 786440 | tf_op jit(solution)/shard_map/half_sum/ppermute | solution.py:25
  73.7 8.6 %collective-permute-done.3.other_ref = bf16[128,1024]{1,0:T(8,128)(2,1)S(1)} collective-permute-done((bf16[128,1024]{1,0:T(8,128)(2,1)S(1)}, bf16[128,1024]{1,0:T(8,128)(2,1)S(1)}, u32[]{:S(2)}, u32[]{:S(2)}) %collective-permute-start.3) | collective-permute-done | bytes 262176 | tf_op jit(solution)/shard_map/half_sum/ppermute | solution.py:25
  82.4 1.0 copy-done.9
  83.6 7.3 %collective-permute-start.4 = (bf16[128,1024]{1,0:T(8,128)(2,1)S(1)}, bf16[128,1024]{1,0:T(8,128)(2,1)S(1)}, u32[]{:S(2)}, u32[]{:S(2)}) collective-permute-start(bf16[128,1024]{1,0:T(8,128)(2,1)S(1)} %hidden_grad.1.d0_ref), channel_id=1, source_target_pairs={{0,64},{64,0},{1,65},{65,1},{2,66},{66,2},{3,67},{67,3},{4,68},{68... | collective-permute-start | bytes 786440 | tf_op jit(solution)/shard_map/d_far/ppermute | solution.py:25
  90.8 18.7 %collective-permute-done.4.d1_ref = bf16[128,1024]{1,0:T(8,128)(2,1)S(1)} collective-permute-done((bf16[128,1024]{1,0:T(8,128)(2,1)S(1)}, bf16[128,1024]{1,0:T(8,128)(2,1)S(1)}, u32[]{:S(2)}, u32[]{:S(2)}) %collective-permute-start.4) | collective-permute-done | bytes 262176 | tf_op jit(solution)/shard_map/d_far/ppermute | solution.py:25
  109.6 2.9 %input_grad.1 = bf16[4,128,1024]{2,1,0:T(8,128)(2,1)S(1)} custom-call(s32[3]{0:T(128)S(1)} %pad_add_fusion.place_ref, bf16[128,1024]{1,0:T(8,128)(2,1)S(1)} %hidden_grad.1.d0_ref, bf16[128,1024]{1,0:T(8,128)(2,1)S(1)} %collective-permute-done.4.d1_ref, bf16[1024,512]{1,0:T(8,128)(2,1)S(1)} %copy-done.5, bf16[1024,512]{1,0:T(8,128)(2,1)S(1)} %copy-done.6, ...), custom_call_target="tpu_custom_call" | custom-call | flops 1073741824 | bytes 6291456 | tf_op jit(solution)/shard_map/d_input/input_grad/pallas_call | solution.py:125
  112.5 0.8 pad_maximum_fusion
  113.3 13.3 %all-gather.3.cloned.1.call-done.x_ref = bf16[16,128,1024]{2,1,0:T(8,128)(2,1)} async-done(((bf16[4,128,1024]{2,1,0:T(8,128)(2,1)}), bf16[16,128,1024]{2,1,0:T(8,128)(2,1)}) %all-gather.3.cloned.1.call-update) | async-done | bytes 4194320 | tf_op jit(solution)/shard_map/all_inputs/all_gather | solution.py:189
  126.6 12.0 %all_to_all.20 = bf16[4,128,1024]{2,1,0:T(8,128)(2,1)S(1)} all-to-all(bf16[4,128,1024]{2,1,0:T(8,128)(2,1)S(1)} %input_grad.1), channel_id=1, replica_groups=mesh['x'=4,'zh'=2,'c'=2,'y'=4,'zl'=8] {'y'}, dimensions={0} | all-to-all | bytes 2097152 | tf_op jit(solution)/shard_map/d_input/all_to_all | solution.py:199
  139.0 0.9 copy.14
  139.8 18.5 %all-to-all-start.3 = ((bf16[8,128,128]{2,1,0:T(8,128)(2,1)}), bf16[8,128,128]{2,1,0:T(8,128)(2,1)S(1)}, u32[]{:S(2)}, u32[]{:S(2)}) async-start(bf16[8,128,128]{2,1,0:T(8,128)(2,1)} %copy.14), calls=%async_computation.3 | async-start | bytes 524288 | tf_op jit(solution)/shard_map/d_input/all_to_all | solution.py:201
  158.3 13.4 %all-gather.5.cloned.1.call-done.d_ref = bf16[8,128,1024]{2,1,0:T(8,128)(2,1)} async-done(((bf16[2,128,1024]{2,1,0:T(8,128)(2,1)}), bf16[8,128,1024]{2,1,0:T(8,128)(2,1)}) %all-gather.5.cloned.1.call-update) | async-done | bytes 2097168 | tf_op jit(solution)/shard_map/d_over_x/all_gather | solution.py:204
  171.8 2.2 %copy-done = bf16[16,128,1024]{2,1,0:T(8,128)(2,1)S(1)} copy-done((bf16[16,128,1024]{2,1,0:T(8,128)(2,1)S(1)}, bf16[16,128,1024]{2,1,0:T(8,128)(2,1)}, u32[]{:S(2)}) %copy-start) | copy-done | bytes 4194328
  174.0 1.6 copy-done.3
  175.5 2.9 %weight_grad_other.1 = bf16[1024,1024]{1,0:T(8,128)(2,1)S(1)} custom-call(s32[3]{0:T(128)S(1)} %pad_add_fusion.place_ref, bf16[16,128,1024]{2,1,0:T(8,128)(2,1)S(1)} %copy-done, bf16[8,128,1024]{2,1,0:T(8,128)(2,1)S(1)} %copy-done.3), custom_call_target="tpu_custom_call" | custom-call | flops 2147483648 | bytes 8388608 | tf_op jit(solution)/shard_map/weight_grads/weight_grad_other/pallas_call | solution.py:163
  178.5 1.4 copy-done.7
  179.9 2.6 %collective-permute-start.6 = (bf16[1024,1024]{1,0:T(8,128)(2,1)}, bf16[1024,1024]{1,0:T(8,128)(2,1)}, u32[]{:S(2)}, u32[]{:S(2)}) collective-permute-start(bf16[1024,1024]{1,0:T(8,128)(2,1)} %copy-done.7), channel_id=1, source_target_pairs={{0,32},{32,0},{1,33},{33,1},{2,34},{34,2},{3,35},{35,3},{4,36},{36... | collective-permute-start | bytes 6291464 | tf_op jit(solution)/shard_map/weight_grads/ppermute | solution.py:25
  182.5 13.4 %collective-permute-start.5 = (bf16[128,128]{1,0:T(8,128)(2,1)S(1)}, bf16[128,128]{1,0:T(8,128)(2,1)S(1)}, u32[]{:S(2)}, u32[]{:S(2)}) collective-permute-start(bf16[128,128]{1,0:T(8,128)(2,1)S(1)} %reduce_sum.25), channel_id=1, source_target_pairs={{0,0},{8,8},{16,64},{24,72},{64,16},{72,24},{80,80},{88,88},{1,1},... | collective-permute-start | bytes 98312 | tf_op jit(solution)/shard_map/d_input/ppermute | solution.py:25
  195.9 2.2 %copy-done.1 = bf16[16,128,1024]{2,1,0:T(8,128)(2,1)S(1)} copy-done((bf16[16,128,1024]{2,1,0:T(8,128)(2,1)S(1)}, bf16[16,128,1024]{2,1,0:T(8,128)(2,1)}, u32[]{:S(2)}) %copy-start.1) | copy-done | bytes 4194328
  198.1 5.0 %weight_grad_own.1 = (bf16[1024,512]{1,0:T(8,128)(2,1)}, bf16[1024,512]{1,0:T(8,128)(2,1)}) custom-call(s32[3]{0:T(128)S(1)} %pad_add_fusion.place_ref, bf16[16,128,1024]{2,1,0:T(8,128)(2,1)S(1)} %copy-done.1, bf16[8,128,1024]{2,1,0:T(8,128)(2,1)S(1)} %copy-done.4, bf16[1024,1024]{1,0:T(8,128)(2,1)} %collective-permute-done.6.got_ref), custom_call_target="tpu_custom_call" | custom-call | flops 2147483648 | bytes 8388608 | tf_op jit(solution)/shard_map/weight_grads/weight_grad_own/pallas_call | solution.py:163
  (34 shorter events, 2.5 us)
Async XLA Ops:
  8.0 17.4 %collective-permute-start = (bf16[128,128]{1,0:T(8,128)(2,1)S(1)}, bf16[128,128]{1,0:T(8,128)(2,1)S(1)}, u32[]{:S(2)}, u32[]{:S(2)}) collective-permute-start(bf16[128,128]{1,0:T(8,128)(2,1)S(1)} %multiply_convert_fusion), channel_id=1, source_target_pairs={{0,0},{8,8},{16,64},{24,72},{64,16},{72,24},{80,80},{88,88},{1,1},... | collective-permute-start | bytes 98312 | tf_op jit(solution)/shard_map/gather_inputs/ppermute | solution.py:25
  26.2 22.5 %all-to-all-start = ((bf16[8,128,128]{2,1,0:T(8,128)(2,1)}), bf16[8,128,128]{2,1,0:T(8,128)(2,1)S(1)}, u32[]{:S(2)}, u32[]{:S(2)}) async-start(bf16[8,128,128]{2,1,0:T(8,128)(2,1)} %broadcast_in_dim.6), calls=%async_computation | async-start | bytes 524288 | tf_op jit(solution)/shard_map/gather_inputs/all_to_all | solution.py:48
  36.8 17.6 %collective-permute-start.1 = (bf16[1024,512]{1,0:T(8,128)(2,1)}, bf16[1024,512]{1,0:T(8,128)(2,1)}, u32[]{:S(2)}, u32[]{:S(2)}) collective-permute-start(bf16[1024,512]{1,0:T(8,128)(2,1)} %g0_ref.3), channel_id=1, source_target_pairs={{0,32},{32,0},{1,33},{33,1},{2,34},{34,2},{3,35},{35,3},{4,36},{36... | collective-permute-start | bytes 3145736 | tf_op jit(solution)/shard_map/gather_inputs/ppermute | solution.py:25
  40.8 13.6 %collective-permute-start.2 = (bf16[1024,512]{1,0:T(8,128)(2,1)}, bf16[1024,512]{1,0:T(8,128)(2,1)}, u32[]{:S(2)}, u32[]{:S(2)}) collective-permute-start(bf16[1024,512]{1,0:T(8,128)(2,1)} %u0_ref.3), channel_id=1, source_target_pairs={{0,32},{32,0},{1,33},{33,1},{2,34},{34,2},{3,35},{35,3},{4,36},{36... | collective-permute-start | bytes 3145736 | tf_op jit(solution)/shard_map/gather_inputs/ppermute | solution.py:25
  48.9 13.4 %copy-start.5 = (bf16[1024,512]{1,0:T(8,128)(2,1)S(1)}, bf16[1024,512]{1,0:T(8,128)(2,1)}, u32[]{:S(2)}) copy-start(bf16[1024,512]{1,0:T(8,128)(2,1)} %g0_ref.3) | copy-start | bytes 3145732
  48.9 13.4 %copy-start.6 = (bf16[1024,512]{1,0:T(8,128)(2,1)S(1)}, bf16[1024,512]{1,0:T(8,128)(2,1)}, u32[]{:S(2)}) copy-start(bf16[1024,512]{1,0:T(8,128)(2,1)} %u0_ref.3) | copy-start | bytes 3145732
  50.2 12.1 %all-to-all-start.1 = ((bf16[4,128,1024]{2,1,0:T(8,128)(2,1)}), bf16[4,128,1024]{2,1,0:T(8,128)(2,1)S(1)}, u32[]{:S(2)}, u32[]{:S(2)}) async-start(bf16[4,128,1024]{2,1,0:T(8,128)(2,1)} %broadcast_in_dim.15), calls=%async_computation.1 | async-start | bytes 2097152 | tf_op jit(solution)/shard_map/gather_inputs/all_to_all | solution.py:48
  54.3 72.3 %all-gather.3.cloned.1.call-start = ((), (), s32[]{:S(2)}) async-start(), calls=%async_computation.4 | async-start | bytes 5242880 | tf_op jit(solution)/shard_map/all_inputs/all_gather | solution.py:189
  62.3 3.2 %copy-start.2 = (bf16[4,128,1024]{2,1,0:T(8,128)(2,1)}, bf16[4,128,1024]{2,1,0:T(8,128)(2,1)S(1)}, u32[]{:S(2)}) copy-start(bf16[4,128,1024]{2,1,0:T(8,128)(2,1)S(1)} %all-to-all-done.1.x_ref) | copy-start | bytes 3145732
  62.3 20.0 %copy-start.10 = (bf16[128,512]{1,0:T(8,128)(2,1)S(1)}, bf16[128,512]{1,0:T(8,128)(2,1)}, u32[]{:S(2)}) copy-start(bf16[128,512]{1,0:T(8,128)(2,1)} %grad_ref.1) | copy-start | bytes 393220
  65.6 0.8 copy-start.8
  66.4 105.4 %all-gather.5.cloned.1.call-start = ((), (), s32[]{:S(2)}) async-start(), calls=%async_computation.5 | async-start | bytes 2621440 | tf_op jit(solution)/shard_map/d_over_x/all_gather | solution.py:204
  66.4 15.9 %collective-permute-start.3 = (bf16[128,1024]{1,0:T(8,128)(2,1)S(1)}, bf16[128,1024]{1,0:T(8,128)(2,1)S(1)}, u32[]{:S(2)}, u32[]{:S(2)}) collective-permute-start(bf16[128,1024]{1,0:T(8,128)(2,1)S(1)} %get-tuple-element.24), channel_id=1, source_target_pairs={{0,64},{64,0},{1,65},{65,1},{2,66},{66,2},{3,67},{67,3},{4,68},{68... | collective-permute-start | bytes 786440 | tf_op jit(solution)/shard_map/half_sum/ppermute | solution.py:25
  82.4 1.0 copy-start.9
  83.6 26.0 %collective-permute-start.4 = (bf16[128,1024]{1,0:T(8,128)(2,1)S(1)}, bf16[128,1024]{1,0:T(8,128)(2,1)S(1)}, u32[]{:S(2)}, u32[]{:S(2)}) collective-permute-start(bf16[128,1024]{1,0:T(8,128)(2,1)S(1)} %hidden_grad.1.d0_ref), channel_id=1, source_target_pairs={{0,64},{64,0},{1,65},{65,1},{2,66},{66,2},{3,67},{67,3},{4,68},{68... | collective-permute-start | bytes 786440 | tf_op jit(solution)/shard_map/d_far/ppermute | solution.py:25
  139.8 40.1 %all-to-all-start.3 = ((bf16[8,128,128]{2,1,0:T(8,128)(2,1)}), bf16[8,128,128]{2,1,0:T(8,128)(2,1)S(1)}, u32[]{:S(2)}, u32[]{:S(2)}) async-start(bf16[8,128,128]{2,1,0:T(8,128)(2,1)} %copy.14), calls=%async_computation.3 | async-start | bytes 524288 | tf_op jit(solution)/shard_map/d_input/all_to_all | solution.py:201
  171.8 2.2 %copy-start = (bf16[16,128,1024]{2,1,0:T(8,128)(2,1)S(1)}, bf16[16,128,1024]{2,1,0:T(8,128)(2,1)}, u32[]{:S(2)}) copy-start(bf16[16,128,1024]{2,1,0:T(8,128)(2,1)} %all-gather.3.cloned.1.call-done.x_ref) | copy-start | bytes 12582916
  174.0 1.6 copy-start.3
  175.5 20.4 %copy-start.4 = (bf16[8,128,1024]{2,1,0:T(8,128)(2,1)S(1)}, bf16[8,128,1024]{2,1,0:T(8,128)(2,1)}, u32[]{:S(2)}) copy-start(bf16[8,128,1024]{2,1,0:T(8,128)(2,1)} %all-gather.5.cloned.1.call-done.d_ref) | copy-start | bytes 6291460
  178.5 1.4 copy-start.7
  179.9 16.0 %collective-permute-start.6 = (bf16[1024,1024]{1,0:T(8,128)(2,1)}, bf16[1024,1024]{1,0:T(8,128)(2,1)}, u32[]{:S(2)}, u32[]{:S(2)}) collective-permute-start(bf16[1024,1024]{1,0:T(8,128)(2,1)} %copy-done.7), channel_id=1, source_target_pairs={{0,32},{32,0},{1,33},{33,1},{2,34},{34,2},{3,35},{35,3},{4,36},{36... | collective-permute-start | bytes 6291464 | tf_op jit(solution)/shard_map/weight_grads/ppermute | solution.py:25
  182.5 20.6 %collective-permute-start.5 = (bf16[128,128]{1,0:T(8,128)(2,1)S(1)}, bf16[128,128]{1,0:T(8,128)(2,1)S(1)}, u32[]{:S(2)}, u32[]{:S(2)}) collective-permute-start(bf16[128,128]{1,0:T(8,128)(2,1)S(1)} %reduce_sum.25), channel_id=1, source_target_pairs={{0,0},{8,8},{16,64},{24,72},{64,16},{72,24},{80,80},{88,88},{1,1},... | collective-permute-start | bytes 98312 | tf_op jit(solution)/shard_map/d_input/ppermute | solution.py:25
  195.9 2.2 %copy-start.1 = (bf16[16,128,1024]{2,1,0:T(8,128)(2,1)S(1)}, bf16[16,128,1024]{2,1,0:T(8,128)(2,1)}, u32[]{:S(2)}) copy-start(bf16[16,128,1024]{2,1,0:T(8,128)(2,1)} %all-gather.3.cloned.1.call-done.x_ref) | copy-start | bytes 12582916
Sparse Core Ops, SparseCore 0:
  66.5 60.0 all-gather.2
  129.3 42.4 all-gather.4

commit v8 on v7

--- a/solution.py
+++ b/solution.py
@@ -49,6 +49,7 @@
 
 
 VMEM = pl.BlockSpec(memory_space=pltpu.VMEM)
+HBM = pl.BlockSpec(memory_space=pltpu.MemorySpace.HBM)
 SMEM = pl.BlockSpec(memory_space=pltpu.SMEM)
 PARAMS = pltpu.CompilerParams(vmem_limit_bytes=12 * 1024 * 1024)
 
@@ -65,7 +66,7 @@
         total = jnp.dot(near, w0[...], preferred_element_type=F32)
         total = total + jnp.dot(far, w1[...], preferred_element_type=F32)
         send_ref[:, k * ff : (k + 1) * ff] = total[:count].astype(BF16)
-        keep_ref[:, k * ff : (k + 1) * ff] = total[count:]
+        keep_ref[:, k * ff : (k + 1) * ff] = total[count:].astype(BF16)
 
 
 def partial_gate_up(place, x, weights):
@@ -74,7 +75,7 @@
     return pl.pallas_call(
         partial_kernel,
         out_shape=(
-            jax.ShapeDtypeStruct((count, 2 * ff), F32),
+            jax.ShapeDtypeStruct((count, 2 * ff), BF16),
             jax.ShapeDtypeStruct((count, 2 * ff), BF16),
         ),
         in_specs=[SMEM] + [VMEM] * 5,
@@ -87,8 +88,8 @@
 
 def hidden_grad_kernel(keep_ref, other_ref, grad_ref, out_ref):
     ff = grad_ref.shape[1]
-    gate = keep_ref[:, :ff] + other_ref[:, :ff].astype(F32)
-    up = keep_ref[:, ff:] + other_ref[:, ff:].astype(F32)
+    gate = keep_ref[:, :ff].astype(F32) + other_ref[:, :ff].astype(F32)
+    up = keep_ref[:, ff:].astype(F32) + other_ref[:, ff:].astype(F32)
     grad_out = grad_ref[...].astype(F32)
     sig = jax.nn.sigmoid(gate)
     out_ref[:, :ff] = (grad_out * up * sig * (1.0 + gate * (1.0 - sig))).astype(BF16)
@@ -133,39 +134,66 @@
     )(place, d_own, d_other, *weights)
 
 
-def weight_grad_rows(place_ref, x_ref, d_ref, other):
+def weight_grad_rows(place_ref, x_ref, d_ref, x_held, d_held, x_sem, d_sem, other):
     half, core = place_ref[0], place_ref[1]
     b = 1 - core if other else core
+    pairs = d_ref.shape[0]
     step = 256
-    d = jnp.concatenate([d_ref[k] for k in range(8)], axis=0)
-    for i in range(0, x_ref.shape[2], step):
-        x = [x_ref[4 * k + 2 * a + b, :, i : i + step] for k in range(4) for a in (half, 1 - half)]
-        yield slice(i, i + step), lax.dot_general(
-            jnp.concatenate(x, axis=0), d, (((0,), (0,)), ((), ())), preferred_element_type=F32
-        )
-
-
-def weight_grad_other_kernel(place_ref, x_ref, d_ref, out_ref):
-    for at, total in weight_grad_rows(place_ref, x_ref, d_ref, True):
+    copies = [pltpu.make_async_copy(d_ref, d_held, d_sem.at[0])]
+    for n in range(pairs):
+        a = half if n % 2 == 0 else 1 - half
+        copies.append(
+            pltpu.make_async_copy(x_ref.at[4 * (n // 2) + 2 * a + b], x_held.at[n], x_sem.at[n])
+        )
+    for copy in copies:
+        copy.start()
+    for copy in copies:
+        copy.wait()
+    for i in range(0, x_held.shape[2], step):
+        at = slice(i, i + step)
+        yield at, lax.dot_general(
+            x_held[:, :, at].reshape(-1, step),
+            d_held[...].reshape(-1, d_held.shape[2]),
+            (((0,), (0,)), ((), ())),
+            preferred_element_type=F32,
+        )
+
+
+def weight_grad_other_kernel(place_ref, x_ref, d_ref, out_ref, *scratch):
+    for at, total in weight_grad_rows(place_ref, x_ref, d_ref, *scratch, True):
         out_ref[at, :] = total.astype(BF16)
 
 
-def weight_grad_own_kernel(place_ref, x_ref, d_ref, got_ref, gate_ref, up_ref):
+def weight_grad_own_kernel(place_ref, x_ref, d_ref, got_ref, gate_ref, up_ref, *scratch):
     ff = gate_ref.shape[1]
-    for at, total in weight_grad_rows(place_ref, x_ref, d_ref, False):
-        total = (total + got_ref[at, :].astype(F32)).astype(BF16)
+    *scratch, got_held, got_sem = scratch
+    copy = pltpu.make_async_copy(got_ref, got_held, got_sem.at[0])
+    copy.start()
+    for at, total in weight_grad_rows(place_ref, x_ref, d_ref, *scratch, False):
+        if at.start == 0:
+            copy.wait()
+        total = (total + got_held[at, :].astype(F32)).astype(BF16)
         gate_ref[at, :] = total[:, :ff]
         up_ref[at, :] = total[:, ff:]
 
 
 def weight_grad(kernel, name, place, inputs, d, got, shapes):
-    flops = 2 * 8 * d.shape[1] * inputs.shape[2] * d.shape[2]
+    pairs, count, cols = d.shape
+    rows = inputs.shape[2]
+    flops = 2 * pairs * count * rows * cols
     return pl.pallas_call(
         kernel,
         out_shape=[jax.ShapeDtypeStruct(v, BF16) for v in shapes],
-        in_specs=[SMEM] + [VMEM] * (2 + len(got)),
+        in_specs=[SMEM, HBM, HBM] + [HBM] * len(got),
         out_specs=[VMEM] * len(shapes),
-        compiler_params=PARAMS,
+        scratch_shapes=[
+            pltpu.VMEM((pairs, count, rows), BF16),
+            pltpu.VMEM((pairs, count, cols), BF16),
+            pltpu.SemaphoreType.DMA((pairs,)),
+            pltpu.SemaphoreType.DMA((1,)),
+        ]
+        + [v for g in got for v in (pltpu.VMEM(g.shape, BF16), pltpu.SemaphoreType.DMA((1,)))],
+        compiler_params=pltpu.CompilerParams(vmem_limit_bytes=62 * 1024 * 1024),
         cost_estimate=pl.CostEstimate(flops=flops, bytes_accessed=8 << 20, transcendentals=0),
         name=name,
     )(place, inputs, d, *got)

time: 212 us -> 210 us (level)
  local copies, waits for them, and re-layouts: 13 us -> 4.52 us
  Pallas kernels: 14.2 us -> 20.1 us
  waiting for transfers between devices: 69.4 us -> 72 us
    unnamed x23 -> x13, local copies, waits for them, and re-layouts: 9.82 us -> 1.34 us
    pallas_call x2, Pallas kernels: 7.96 us -> 13.9 us  [weight_grad(): pl.pallas_call(kernel, out_shape=[jax.ShapeDtypeStruct(v, BF16) for v in...]
  transfers between devices with their start and end apart: 12 -> 12, of which waited for: 7 -> 7; matrix products, arithmetic and copies ran while one was open for 2% -> 2% of each run, Pallas kernels for 5% -> 8%
where the time goes in v8:
time: 210 us; the launch traced here: 209 us
  starting transfers between devices  84.4 us (40%)
  waiting for transfers between devices  72 us (34%)
  Pallas kernels  20.1 us (10%)
  between operations  14.2 us (7%)
  blocking collectives  12 us (6%)
  local copies, waits for them, and re-layouts  4.52 us (2%)
    ppermute x7, starting transfers between devices, permute(): return lax.ppermute(value, axes if len(axes) > 1 else axes[0], pairs)  52.6 us
    ppermute x7, waiting for transfers between devices, permute(): return lax.ppermute(value, axes if len(axes) > 1 else axes[0], pairs)  29.9 us
    all_to_all x1, starting transfers between devices, shards(): di = lax.all_to_all(di, 'zl', 0, 0)  17.1 us
    all_gather x1, waiting for transfers between devices, shards(): d_all = lax.all_gather(d_both, 'x', axis=0, tiled=True)  15.1 us
    all_to_all x2, starting transfers between devices, spread(): lax.all_to_all(jnp.broadcast_to(value[None], (n,) + value.shape), axis, 0...  14.7 us
    all_to_all x2, waiting for transfers between devices, spread(): lax.all_to_all(jnp.broadcast_to(value[None], (n,) + value.shape), axis, 0...  13.9 us
    pallas_call x2, Pallas kernels, weight_grad(): pl.pallas_call(kernel, out_shape=[jax.ShapeDtypeStruct(v, BF16) for v in...  13.9 us
    all_gather x1, waiting for transfers between devices, shards(): all_inputs = lax.all_gather(inputs, 'x', axis=0, tiled=True)  13 us
  transfers between devices with their start and end apart: 12, of which 7 were waited for; matrix products, arithmetic and copies ran while one was open for 2% of the time, Pallas kernels for 8%

profile of v8, /device:TPU:25, one launch (start us, length us, event | category | flops | bytes accessed | tf_op | source)
XLA Modules:
  0.0 209.3 jit_solution(95604811282812494)
XLA Ops:
  7.2 0.8 multiply_convert_fusion
  8.0 16.1 %collective-permute-start = (bf16[128,128]{1,0:T(8,128)(2,1)S(1)}, bf16[128,128]{1,0:T(8,128)(2,1)S(1)}, u32[]{:S(2)}, u32[]{:S(2)}) collective-permute-start(bf16[128,128]{1,0:T(8,128)(2,1)S(1)} %multiply_convert_fusion), channel_id=1, source_target_pairs={{0,0},{8,8},{16,64},{24,72},{64,16},{72,24},{80,80},{88,88},{1,1},... | collective-permute-start | bytes 98312 | tf_op jit(solution)/shard_map/gather_inputs/ppermute | solution.py:25
  24.1 1.3 collective-permute-done
  25.4 0.7 broadcast_in_dim.6
  26.2 10.6 %all-to-all-start = ((bf16[8,128,128]{2,1,0:T(8,128)(2,1)}), bf16[8,128,128]{2,1,0:T(8,128)(2,1)S(1)}, u32[]{:S(2)}, u32[]{:S(2)}) async-start(bf16[8,128,128]{2,1,0:T(8,128)(2,1)} %broadcast_in_dim.6), calls=%async_computation | async-start | bytes 524288 | tf_op jit(solution)/shard_map/gather_inputs/all_to_all | solution.py:48
  36.8 4.0 %collective-permute-start.1 = (bf16[1024,512]{1,0:T(8,128)(2,1)}, bf16[1024,512]{1,0:T(8,128)(2,1)}, u32[]{:S(2)}, u32[]{:S(2)}) collective-permute-start(bf16[1024,512]{1,0:T(8,128)(2,1)} %g0_ref.3), channel_id=1, source_target_pairs={{0,32},{32,0},{1,33},{33,1},{2,34},{34,2},{3,35},{35,3},{4,36},{36... | collective-permute-start | bytes 3145736 | tf_op jit(solution)/shard_map/gather_inputs/ppermute | solution.py:25
  40.8 1.9 collective-permute-start.2
  42.7 6.0 %all-to-all-done = bf16[8,128,128]{2,1,0:T(8,128)(2,1)S(1)} async-done(((bf16[8,128,128]{2,1,0:T(8,128)(2,1)}), bf16[8,128,128]{2,1,0:T(8,128)(2,1)S(1)}, u32[]{:S(2)}, u32[]{:S(2)}) %all-to-all-start) | async-done | bytes 262176 | tf_op jit(solution)/shard_map/gather_inputs/all_to_all | solution.py:48
  48.7 0.2 copy.11
  49.1 1.1 broadcast_in_dim.15
  50.2 4.1 %all-to-all-start.1 = ((bf16[4,128,1024]{2,1,0:T(8,128)(2,1)}), bf16[4,128,1024]{2,1,0:T(8,128)(2,1)S(1)}, u32[]{:S(2)}, u32[]{:S(2)}) async-start(bf16[4,128,1024]{2,1,0:T(8,128)(2,1)} %broadcast_in_dim.15), calls=%async_computation.1 | async-start | bytes 2097152 | tf_op jit(solution)/shard_map/gather_inputs/all_to_all | solution.py:48
  54.4 7.9 %all-to-all-done.1.x_ref = bf16[4,128,1024]{2,1,0:T(8,128)(2,1)S(1)} async-done(((bf16[4,128,1024]{2,1,0:T(8,128)(2,1)}), bf16[4,128,1024]{2,1,0:T(8,128)(2,1)S(1)}, u32[]{:S(2)}, u32[]{:S(2)}) %all-to-all-start.1) | async-done | bytes 1048608 | tf_op jit(solution)/shard_map/gather_inputs/all_to_all | solution.py:48
  62.3 3.2 %partial_gate_up.1 = (bf16[128,1024]{1,0:T(8,128)(2,1)S(1)}, bf16[128,1024]{1,0:T(8,128)(2,1)S(1)}) custom-call(s32[3]{0:T(128)S(1)} %pad_add_fusion.place_ref, bf16[4,128,1024]{2,1,0:T(8,128)(2,1)S(1)} %all-to-all-done.1.x_ref, bf16[1024,512]{1,0:T(8,128)(2,1)S(1)} %copy-done.1, bf16[1024,512]{1,0:T(8,128)(2,1)S(1)} %copy-done.2, ...), custom_call_target="tpu_custom_call" | custom-call | flops 1073741824 | bytes 6291456 | tf_op jit(solution)/shard_map/partial_gate_up/partial_gate_up/pallas_call | solution.py:75
  65.5 0.7 copy-done.5
  66.3 7.3 %collective-permute-start.3 = (bf16[128,1024]{1,0:T(8,128)(2,1)}, bf16[128,1024]{1,0:T(8,128)(2,1)S(1)}, u32[]{:S(2)}, u32[]{:S(2)}) collective-permute-start(bf16[128,1024]{1,0:T(8,128)(2,1)} %copy-done.5), channel_id=1, source_target_pairs={{0,64},{64,0},{1,65},{65,1},{2,66},{66,2},{3,67},{67,3},{4,68},{68... | collective-permute-start | bytes 786440 | tf_op jit(solution)/shard_map/half_sum/ppermute | solution.py:25
  73.6 8.9 %collective-permute-done.3.other_ref = bf16[128,1024]{1,0:T(8,128)(2,1)S(1)} collective-permute-done((bf16[128,1024]{1,0:T(8,128)(2,1)}, bf16[128,1024]{1,0:T(8,128)(2,1)S(1)}, u32[]{:S(2)}, u32[]{:S(2)}) %collective-permute-start.3) | collective-permute-done | bytes 262176 | tf_op jit(solution)/shard_map/half_sum/ppermute | solution.py:25
  82.4 0.2 hidden_grad.1.d0_ref
  82.6 7.3 %collective-permute-start.4 = (bf16[128,1024]{1,0:T(8,128)(2,1)S(1)}, bf16[128,1024]{1,0:T(8,128)(2,1)S(1)}, u32[]{:S(2)}, u32[]{:S(2)}) collective-permute-start(bf16[128,1024]{1,0:T(8,128)(2,1)S(1)} %hidden_grad.1.d0_ref), channel_id=1, source_target_pairs={{0,64},{64,0},{1,65},{65,1},{2,66},{66,2},{3,67},{67,3},{4,68},{68... | collective-permute-start | bytes 786440 | tf_op jit(solution)/shard_map/d_far/ppermute | solution.py:25
  89.9 19.8 %collective-permute-done.4.d1_ref = bf16[128,1024]{1,0:T(8,128)(2,1)S(1)} collective-permute-done((bf16[128,1024]{1,0:T(8,128)(2,1)S(1)}, bf16[128,1024]{1,0:T(8,128)(2,1)S(1)}, u32[]{:S(2)}, u32[]{:S(2)}) %collective-permute-start.4) | collective-permute-done | bytes 262176 | tf_op jit(solution)/shard_map/d_far/ppermute | solution.py:25
  109.7 2.9 %input_grad.1 = bf16[4,128,1024]{2,1,0:T(8,128)(2,1)S(1)} custom-call(s32[3]{0:T(128)S(1)} %pad_add_fusion.place_ref, bf16[128,1024]{1,0:T(8,128)(2,1)S(1)} %hidden_grad.1.d0_ref, bf16[128,1024]{1,0:T(8,128)(2,1)S(1)} %collective-permute-done.4.d1_ref, bf16[1024,512]{1,0:T(8,128)(2,1)S(1)} %copy-done.1, bf16[1024,512]{1,0:T(8,128)(2,1)S(1)} %copy-done.2, ...), custom_call_target="tpu_custom_call" | custom-call | flops 1073741824 | bytes 6291456 | tf_op jit(solution)/shard_map/d_input/input_grad/pallas_call | solution.py:126
  112.6 0.8 pad_maximum_fusion
  113.4 13.0 %all-gather.3.cloned.1.call-done.x_ref = bf16[16,128,1024]{2,1,0:T(8,128)(2,1)} async-done(((bf16[4,128,1024]{2,1,0:T(8,128)(2,1)}), bf16[16,128,1024]{2,1,0:T(8,128)(2,1)}) %all-gather.3.cloned.1.call-update) | async-done | bytes 4194320 | tf_op jit(solution)/shard_map/all_inputs/all_gather | solution.py:217
  126.5 12.0 %all_to_all.20 = bf16[4,128,1024]{2,1,0:T(8,128)(2,1)S(1)} all-to-all(bf16[4,128,1024]{2,1,0:T(8,128)(2,1)S(1)} %input_grad.1), channel_id=1, replica_groups=mesh['x'=4,'zh'=2,'c'=2,'y'=4,'zl'=8] {'y'}, dimensions={0} | all-to-all | bytes 2097152 | tf_op jit(solution)/shard_map/d_input/all_to_all | solution.py:227
  138.5 0.2 reduce_sum.24
  138.8 0.9 copy.14
  139.7 17.1 %all-to-all-start.3 = ((bf16[8,128,128]{2,1,0:T(8,128)(2,1)}), bf16[8,128,128]{2,1,0:T(8,128)(2,1)S(1)}, u32[]{:S(2)}, u32[]{:S(2)}) async-start(bf16[8,128,128]{2,1,0:T(8,128)(2,1)} %copy.14), calls=%async_computation.3 | async-start | bytes 524288 | tf_op jit(solution)/shard_map/d_input/all_to_all | solution.py:229
  156.8 15.1 %all-gather.5.cloned.1.call-done.d_ref = bf16[8,128,1024]{2,1,0:T(8,128)(2,1)} async-done(((bf16[2,128,1024]{2,1,0:T(8,128)(2,1)}), bf16[8,128,1024]{2,1,0:T(8,128)(2,1)}) %all-gather.5.cloned.1.call-update) | async-done | bytes 2097168 | tf_op jit(solution)/shard_map/d_over_x/all_gather | solution.py:232
  171.9 6.7 %weight_grad_other.1 = bf16[1024,1024]{1,0:T(8,128)(2,1)} custom-call(s32[3]{0:T(128)} %copy-done.4, bf16[16,128,1024]{2,1,0:T(8,128)(2,1)} %all-gather.3.cloned.1.call-done.x_ref, bf16[8,128,1024]{2,1,0:T(8,128)(2,1)} %all-gather.5.cloned.1.call-done.d_ref), custom_call_target="tpu_custom_call" | custom-call | flops 2147483648 | bytes 8388608 | tf_op jit(solution)/shard_map/weight_grads/weight_grad_other/pallas_call | solution.py:184
  178.6 2.6 %collective-permute-start.6 = (bf16[1024,1024]{1,0:T(8,128)(2,1)}, bf16[1024,1024]{1,0:T(8,128)(2,1)}, u32[]{:S(2)}, u32[]{:S(2)}) collective-permute-start(bf16[1024,1024]{1,0:T(8,128)(2,1)} %weight_grad_other.1), channel_id=1, source_target_pairs={{0,32},{32,0},{1,33},{33,1},{2,34},{34,2},{3,35},{35,3},{4,36},{36... | collective-permute-start | bytes 6291464 | tf_op jit(solution)/shard_map/weight_grads/ppermute | solution.py:25
  181.2 13.4 %collective-permute-start.5 = (bf16[128,128]{1,0:T(8,128)(2,1)S(1)}, bf16[128,128]{1,0:T(8,128)(2,1)S(1)}, u32[]{:S(2)}, u32[]{:S(2)}) collective-permute-start(bf16[128,128]{1,0:T(8,128)(2,1)S(1)} %reduce_sum.25), channel_id=1, source_target_pairs={{0,0},{8,8},{16,64},{24,72},{64,16},{72,24},{80,80},{88,88},{1,1},... | collective-permute-start | bytes 98312 | tf_op jit(solution)/shard_map/d_input/ppermute | solution.py:25
  194.6 7.2 %weight_grad_own.1 = (bf16[1024,512]{1,0:T(8,128)(2,1)}, bf16[1024,512]{1,0:T(8,128)(2,1)}) custom-call(s32[3]{0:T(128)} %copy-done.4, bf16[16,128,1024]{2,1,0:T(8,128)(2,1)} %all-gather.3.cloned.1.call-done.x_ref, bf16[8,128,1024]{2,1,0:T(8,128)(2,1)} %all-gather.5.cloned.1.call-done.d_ref, bf16[1024,1024]{1,0:T(8,128)(2,1)} %collective-permute-done.6.got_ref), custom_call_target="tpu_custom_call" | custom-call | flops 2147483648 | bytes 8388608 | tf_op jit(solution)/shard_map/weight_grads/weight_grad_own/pallas_call | solution.py:184
  201.8 0.6 copy.16
  (24 shorter events, 0.5 us)
Async XLA Ops:
  8.0 17.4 %collective-permute-start = (bf16[128,128]{1,0:T(8,128)(2,1)S(1)}, bf16[128,128]{1,0:T(8,128)(2,1)S(1)}, u32[]{:S(2)}, u32[]{:S(2)}) collective-permute-start(bf16[128,128]{1,0:T(8,128)(2,1)S(1)} %multiply_convert_fusion), channel_id=1, source_target_pairs={{0,0},{8,8},{16,64},{24,72},{64,16},{72,24},{80,80},{88,88},{1,1},... | collective-permute-start | bytes 98312 | tf_op jit(solution)/shard_map/gather_inputs/ppermute | solution.py:25
  26.2 22.5 %all-to-all-start = ((bf16[8,128,128]{2,1,0:T(8,128)(2,1)}), bf16[8,128,128]{2,1,0:T(8,128)(2,1)S(1)}, u32[]{:S(2)}, u32[]{:S(2)}) async-start(bf16[8,128,128]{2,1,0:T(8,128)(2,1)} %broadcast_in_dim.6), calls=%async_computation | async-start | bytes 524288 | tf_op jit(solution)/shard_map/gather_inputs/all_to_all | solution.py:48
  36.8 17.6 %collective-permute-start.1 = (bf16[1024,512]{1,0:T(8,128)(2,1)}, bf16[1024,512]{1,0:T(8,128)(2,1)}, u32[]{:S(2)}, u32[]{:S(2)}) collective-permute-start(bf16[1024,512]{1,0:T(8,128)(2,1)} %g0_ref.3), channel_id=1, source_target_pairs={{0,32},{32,0},{1,33},{33,1},{2,34},{34,2},{3,35},{35,3},{4,36},{36... | collective-permute-start | bytes 3145736 | tf_op jit(solution)/shard_map/gather_inputs/ppermute | solution.py:25
  40.8 13.6 %collective-permute-start.2 = (bf16[1024,512]{1,0:T(8,128)(2,1)}, bf16[1024,512]{1,0:T(8,128)(2,1)}, u32[]{:S(2)}, u32[]{:S(2)}) collective-permute-start(bf16[1024,512]{1,0:T(8,128)(2,1)} %u0_ref.3), channel_id=1, source_target_pairs={{0,32},{32,0},{1,33},{33,1},{2,34},{34,2},{3,35},{35,3},{4,36},{36... | collective-permute-start | bytes 3145736 | tf_op jit(solution)/shard_map/gather_inputs/ppermute | solution.py:25
  48.9 13.4 %copy-start.1 = (bf16[1024,512]{1,0:T(8,128)(2,1)S(1)}, bf16[1024,512]{1,0:T(8,128)(2,1)}, u32[]{:S(2)}) copy-start(bf16[1024,512]{1,0:T(8,128)(2,1)} %g0_ref.3) | copy-start | bytes 3145732
  48.9 13.4 %copy-start.2 = (bf16[1024,512]{1,0:T(8,128)(2,1)S(1)}, bf16[1024,512]{1,0:T(8,128)(2,1)}, u32[]{:S(2)}) copy-start(bf16[1024,512]{1,0:T(8,128)(2,1)} %u0_ref.3) | copy-start | bytes 3145732
  50.2 12.1 %all-to-all-start.1 = ((bf16[4,128,1024]{2,1,0:T(8,128)(2,1)}), bf16[4,128,1024]{2,1,0:T(8,128)(2,1)S(1)}, u32[]{:S(2)}, u32[]{:S(2)}) async-start(bf16[4,128,1024]{2,1,0:T(8,128)(2,1)} %broadcast_in_dim.15), calls=%async_computation.1 | async-start | bytes 2097152 | tf_op jit(solution)/shard_map/gather_inputs/all_to_all | solution.py:48
  54.3 72.2 %all-gather.3.cloned.1.call-start = ((), (), s32[]{:S(2)}) async-start(), calls=%async_computation.4 | async-start | bytes 5242880 | tf_op jit(solution)/shard_map/all_inputs/all_gather | solution.py:217
  54.4 55.3 %copy-start.4 = (s32[3]{0:T(128)}, s32[3]{0:T(128)S(1)}, u32[]{:S(2)}) copy-start(s32[3]{0:T(128)S(1)} %pad_add_fusion.place_ref) | copy-start | bytes 40
  62.3 3.2 %copy-start = (bf16[4,128,1024]{2,1,0:T(8,128)(2,1)}, bf16[4,128,1024]{2,1,0:T(8,128)(2,1)S(1)}, u32[]{:S(2)}) copy-start(bf16[4,128,1024]{2,1,0:T(8,128)(2,1)S(1)} %all-to-all-done.1.x_ref) | copy-start | bytes 3145732
  62.3 20.1 %copy-start.3 = (bf16[128,512]{1,0:T(8,128)(2,1)S(1)}, bf16[128,512]{1,0:T(8,128)(2,1)}, u32[]{:S(2)}) copy-start(bf16[128,512]{1,0:T(8,128)(2,1)} %grad_ref.1) | copy-start | bytes 393220
  65.5 0.7 copy-start.5
  66.3 105.6 %all-gather.5.cloned.1.call-start = ((), (), s32[]{:S(2)}) async-start(), calls=%async_computation.5 | async-start | bytes 2621440 | tf_op jit(solution)/shard_map/d_over_x/all_gather | solution.py:232
  66.3 16.1 %collective-permute-start.3 = (bf16[128,1024]{1,0:T(8,128)(2,1)}, bf16[128,1024]{1,0:T(8,128)(2,1)S(1)}, u32[]{:S(2)}, u32[]{:S(2)}) collective-permute-start(bf16[128,1024]{1,0:T(8,128)(2,1)} %copy-done.5), channel_id=1, source_target_pairs={{0,64},{64,0},{1,65},{65,1},{2,66},{66,2},{3,67},{67,3},{4,68},{68... | collective-permute-start | bytes 786440 | tf_op jit(solution)/shard_map/half_sum/ppermute | solution.py:25
  82.6 27.1 %collective-permute-start.4 = (bf16[128,1024]{1,0:T(8,128)(2,1)S(1)}, bf16[128,1024]{1,0:T(8,128)(2,1)S(1)}, u32[]{:S(2)}, u32[]{:S(2)}) collective-permute-start(bf16[128,1024]{1,0:T(8,128)(2,1)S(1)} %hidden_grad.1.d0_ref), channel_id=1, source_target_pairs={{0,64},{64,0},{1,65},{65,1},{2,66},{66,2},{3,67},{67,3},{4,68},{68... | collective-permute-start | bytes 786440 | tf_op jit(solution)/shard_map/d_far/ppermute | solution.py:25
  139.7 38.9 %all-to-all-start.3 = ((bf16[8,128,128]{2,1,0:T(8,128)(2,1)}), bf16[8,128,128]{2,1,0:T(8,128)(2,1)S(1)}, u32[]{:S(2)}, u32[]{:S(2)}) async-start(bf16[8,128,128]{2,1,0:T(8,128)(2,1)} %copy.14), calls=%async_computation.3 | async-start | bytes 524288 | tf_op jit(solution)/shard_map/d_input/all_to_all | solution.py:229
  178.6 16.0 %collective-permute-start.6 = (bf16[1024,1024]{1,0:T(8,128)(2,1)}, bf16[1024,1024]{1,0:T(8,128)(2,1)}, u32[]{:S(2)}, u32[]{:S(2)}) collective-permute-start(bf16[1024,1024]{1,0:T(8,128)(2,1)} %weight_grad_other.1), channel_id=1, source_target_pairs={{0,32},{32,0},{1,33},{33,1},{2,34},{34,2},{3,35},{35,3},{4,36},{36... | collective-permute-start | bytes 6291464 | tf_op jit(solution)/shard_map/weight_grads/ppermute | solution.py:25
  181.2 20.6 %collective-permute-start.5 = (bf16[128,128]{1,0:T(8,128)(2,1)S(1)}, bf16[128,128]{1,0:T(8,128)(2,1)S(1)}, u32[]{:S(2)}, u32[]{:S(2)}) collective-permute-start(bf16[128,128]{1,0:T(8,128)(2,1)S(1)} %reduce_sum.25), channel_id=1, source_target_pairs={{0,0},{8,8},{16,64},{24,72},{64,16},{72,24},{80,80},{88,88},{1,1},... | collective-permute-start | bytes 98312 | tf_op jit(solution)/shard_map/d_input/ppermute | solution.py:25
Sparse Core Ops, SparseCore 0:
  66.4 60.0 all-gather.2
  129.1 42.6 all-gather.4

commit v9 on v7

--- a/solution.py
+++ b/solution.py
@@ -49,6 +49,7 @@
 
 
 VMEM = pl.BlockSpec(memory_space=pltpu.VMEM)
+HBM = pl.BlockSpec(memory_space=pltpu.MemorySpace.HBM)
 SMEM = pl.BlockSpec(memory_space=pltpu.SMEM)
 PARAMS = pltpu.CompilerParams(vmem_limit_bytes=12 * 1024 * 1024)
 
@@ -65,7 +66,7 @@
         total = jnp.dot(near, w0[...], preferred_element_type=F32)
         total = total + jnp.dot(far, w1[...], preferred_element_type=F32)
         send_ref[:, k * ff : (k + 1) * ff] = total[:count].astype(BF16)
-        keep_ref[:, k * ff : (k + 1) * ff] = total[count:]
+        keep_ref[:, k * ff : (k + 1) * ff] = total[count:].astype(BF16)
 
 
 def partial_gate_up(place, x, weights):
@@ -74,7 +75,7 @@
     return pl.pallas_call(
         partial_kernel,
         out_shape=(
-            jax.ShapeDtypeStruct((count, 2 * ff), F32),
+            jax.ShapeDtypeStruct((count, 2 * ff), BF16),
             jax.ShapeDtypeStruct((count, 2 * ff), BF16),
         ),
         in_specs=[SMEM] + [VMEM] * 5,
@@ -87,8 +88,8 @@
 
 def hidden_grad_kernel(keep_ref, other_ref, grad_ref, out_ref):
     ff = grad_ref.shape[1]
-    gate = keep_ref[:, :ff] + other_ref[:, :ff].astype(F32)
-    up = keep_ref[:, ff:] + other_ref[:, ff:].astype(F32)
+    gate = keep_ref[:, :ff].astype(F32) + other_ref[:, :ff].astype(F32)
+    up = keep_ref[:, ff:].astype(F32) + other_ref[:, ff:].astype(F32)
     grad_out = grad_ref[...].astype(F32)
     sig = jax.nn.sigmoid(gate)
     out_ref[:, :ff] = (grad_out * up * sig * (1.0 + gate * (1.0 - sig))).astype(BF16)
@@ -133,42 +134,95 @@
     )(place, d_own, d_other, *weights)
 
 
-def weight_grad_rows(place_ref, x_ref, d_ref, other):
+def add_parts_kernel(parts_ref, out_ref):
+    width = out_ref.shape[2]
+    for z in range(out_ref.shape[0]):
+        total = parts_ref[0, :, z * width : (z + 1) * width].astype(F32)
+        for y in range(1, parts_ref.shape[0]):
+            total = total + parts_ref[y, :, z * width : (z + 1) * width].astype(F32)
+        out_ref[z] = total.astype(BF16)
+
+
+def add_parts(parts, width):
+    _, count, rows = parts.shape
+    return pl.pallas_call(
+        add_parts_kernel,
+        out_shape=jax.ShapeDtypeStruct((rows // width, count, width), BF16),
+        in_specs=[VMEM],
+        out_specs=VMEM,
+        compiler_params=PARAMS,
+        cost_estimate=pl.CostEstimate(flops=1 << 19, bytes_accessed=5 << 18, transcendentals=0),
+        name="add_parts",
+    )(parts)
+
+
+STEP = 256
+
+
+def weight_grad_kernel(
+    place_ref, x_ref, d_ref, sent_ref, keep_ref, x_held, d_held, out_held, x_sem, d_sem, out_sem
+):
     half, core = place_ref[0], place_ref[1]
-    b = 1 - core if other else core
-    step = 256
-    d = jnp.concatenate([d_ref[k] for k in range(8)], axis=0)
-    for i in range(0, x_ref.shape[2], step):
-        x = [x_ref[4 * k + 2 * a + b, :, i : i + step] for k in range(4) for a in (half, 1 - half)]
-        yield slice(i, i + step), lax.dot_general(
-            jnp.concatenate(x, axis=0), d, (((0,), (0,)), ((), ())), preferred_element_type=F32
-        )
-
-
-def weight_grad_other_kernel(place_ref, x_ref, d_ref, out_ref):
-    for at, total in weight_grad_rows(place_ref, x_ref, d_ref, True):
-        out_ref[at, :] = total.astype(BF16)
-
-
-def weight_grad_own_kernel(place_ref, x_ref, d_ref, got_ref, gate_ref, up_ref):
-    ff = gate_ref.shape[1]
-    for at, total in weight_grad_rows(place_ref, x_ref, d_ref, False):
-        total = (total + got_ref[at, :].astype(F32)).astype(BF16)
-        gate_ref[at, :] = total[:, :ff]
-        up_ref[at, :] = total[:, ff:]
-
-
-def weight_grad(kernel, name, place, inputs, d, got, shapes):
-    flops = 2 * 8 * d.shape[1] * inputs.shape[2] * d.shape[2]
-    return pl.pallas_call(
-        kernel,
-        out_shape=[jax.ShapeDtypeStruct(v, BF16) for v in shapes],
-        in_specs=[SMEM] + [VMEM] * (2 + len(got)),
-        out_specs=[VMEM] * len(shapes),
-        compiler_params=PARAMS,
-        cost_estimate=pl.CostEstimate(flops=flops, bytes_accessed=8 << 20, transcendentals=0),
-        name=name,
-    )(place, inputs, d, *got)
+    pairs = d_ref.shape[0]
+    tokens = pltpu.make_async_copy(d_ref, d_held, d_sem.at[0])
+    tokens.start()
+    fetches = []
+    for m in range(2):
+        b = 1 - core if m == 0 else core
+        for n in range(pairs):
+            a = half if n % 2 == 0 else 1 - half
+            fetches.append(
+                pltpu.make_async_copy(
+                    x_ref.at[4 * (n // 2) + 2 * a + b], x_held.at[m, n], x_sem.at[m, n]
+                )
+            )
+    for fetch in fetches:
+        fetch.start()
+    tokens.wait()
+    writes = []
+    for m, out_ref in enumerate((sent_ref, keep_ref)):
+        for fetch in fetches[m * pairs : (m + 1) * pairs]:
+            fetch.wait()
+        for i in range(out_ref.shape[0] // STEP):
+            at = slice(i * STEP, (i + 1) * STEP)
+            out_held[m, at, :] = lax.dot_general(
+                x_held[m, :, :, at].reshape(-1, STEP),
+                d_held[...].reshape(-1, d_held.shape[2]),
+                (((0,), (0,)), ((), ())),
+                preferred_element_type=F32,
+            ).astype(BF16)
+            write = pltpu.make_async_copy(
+                out_held.at[m, pl.ds(i * STEP, STEP)],
+                out_ref.at[pl.ds(i * STEP, STEP)],
+                out_sem.at[m, i],
+            )
+            write.start()
+            writes.append(write)
+    for write in writes:
+        write.wait()
+
+
+def weight_grad(place, inputs, d):
+    pairs, count, cols = d.shape
+    rows = inputs.shape[2]
+    flops = 2 * 2 * pairs * count * rows * cols
+    return pl.pallas_call(
+        weight_grad_kernel,
+        out_shape=[jax.ShapeDtypeStruct((rows, cols), BF16)] * 2,
+        in_specs=[SMEM, HBM, HBM],
+        out_specs=[HBM, HBM],
+        scratch_shapes=[
+            pltpu.VMEM((2, pairs, count, rows), BF16),
+            pltpu.VMEM((pairs, count, cols), BF16),
+            pltpu.VMEM((2, rows, cols), BF16),
+            pltpu.SemaphoreType.DMA((2, pairs)),
+            pltpu.SemaphoreType.DMA((1,)),
+            pltpu.SemaphoreType.DMA((2, rows // STEP)),
+        ],
+        compiler_params=pltpu.CompilerParams(vmem_limit_bytes=62 * 1024 * 1024),
+        cost_estimate=pl.CostEstimate(flops=flops, bytes_accessed=10 << 20, transcendentals=0),
+        name="weight_grad",
+    )(place, inputs, d)
 
 
 def shards(quantized, scales, d_hidden, w_gate, w_up):
@@ -196,25 +250,17 @@
     with jax.named_scope("d_input"):
         di = input_grad(place, d_own, d_far, weights)
         di, d_own, d_far = lax.optimization_barrier((di, d_own, d_far))
-        di = jnp.sum(lax.all_to_all(di, "y", 0, 0).astype(F32), axis=0).astype(BF16)
-        di = di.reshape(count, 8, width).transpose(1, 0, 2)
+        di = add_parts(lax.all_to_all(di, "y", 0, 0), width)
         di = lax.all_to_all(di, "zl", 0, 0)
     with jax.named_scope("d_over_x"):
         d_both, all_inputs = lax.optimization_barrier((jnp.stack([d_own, d_far]), all_inputs))
         d_all = lax.all_gather(d_both, "x", axis=0, tiled=True)
     with jax.named_scope("weight_grads"):
-        (sent,) = weight_grad(
-            weight_grad_other_kernel, "weight_grad_other", place, all_inputs, d_all, (), [(rows, 2 * ff)]
-        )
+        sent, keep = weight_grad(place, all_inputs, d_all)
         di, sent = lax.optimization_barrier((di, sent))
-        d_gate_weight, d_up_weight = weight_grad(
-            weight_grad_own_kernel,
-            "weight_grad_own",
-            place,
-            all_inputs,
-            d_all,
-            (swap_core(sent),),
-            [(rows, ff)] * 2,
+        got = swap_core(sent)
+        d_gate_weight, d_up_weight = (
+            (keep[:, k : k + ff].astype(F32) + got[:, k : k + ff].astype(F32)).astype(BF16) for k in (0, ff)
         )
     with jax.named_scope("d_input"):
         di = swap_half_y(jnp.sum(di.astype(F32), axis=0).astype(BF16))

time: 212 us -> 209 us (0.986)
  local copies, waits for them, and re-layouts: 13 us -> 3.49 us
  other arithmetic: 1.99 us -> 5.24 us
  waiting for transfers between devices: 69.4 us -> 72.4 us
  Pallas kernels: 14.2 us -> 16.4 us
    unnamed x23 -> x13, local copies, waits for them, and re-layouts: 9.82 us -> 1.34 us
    convert_element_type x0 -> x1, other arithmetic: none -> 3.45 us  [shards(): (keep[:, k:k + ff].astype(F32) + got[:, k:k + ff].astype(F32)).astype(BF16)]
    pallas_call x2, Pallas kernels: 7.96 us -> 10.2 us  [the longest x1 9.29 us: weight_grad(): pl.pallas_call(weight_grad_kernel, out_shape=[jax.ShapeDtypeStruct((rows,...]
  transfers between devices with their start and end apart: 12 -> 12, of which waited for: 7 -> 7; matrix products, arithmetic and copies ran while one was open for 2% -> 3% of each run, Pallas kernels for 5% -> 6%
where the time goes in v9:
time: 209 us; the launch traced here: 208 us
  starting transfers between devices  84.4 us (40%)
  waiting for transfers between devices  72.4 us (35%)
  Pallas kernels  16.4 us (8%)
  between operations  14.2 us (7%)
  blocking collectives  12 us (6%)
  other arithmetic  5.24 us (3%)
  local copies, waits for them, and re-layouts  3.49 us (2%)
    ppermute x7, starting transfers between devices, permute(): return lax.ppermute(value, axes if len(axes) > 1 else axes[0], pairs)  52.6 us
    ppermute x7, waiting for transfers between devices, permute(): return lax.ppermute(value, axes if len(axes) > 1 else axes[0], pairs)  29.9 us
    all_to_all x1, starting transfers between devices, shards(): di = lax.all_to_all(di, 'zl', 0, 0)  17.1 us
    all_gather x1, waiting for transfers between devices, shards(): d_all = lax.all_gather(d_both, 'x', axis=0, tiled=True)  15.4 us
    all_to_all x2, starting transfers between devices, spread(): lax.all_to_all(jnp.broadcast_to(value[None], (n,) + value.shape), axis, 0...  14.7 us
    all_to_all x2, waiting for transfers between devices, spread(): lax.all_to_all(jnp.broadcast_to(value[None], (n,) + value.shape), axis, 0...  13.9 us
    all_gather x1, waiting for transfers between devices, shards(): all_inputs = lax.all_gather(inputs, 'x', axis=0, tiled=True)  13 us
    all_to_all x1, blocking collectives, shards(): di = add_parts(lax.all_to_all(di, 'y', 0, 0), width)  12 us
  transfers between devices with their start and end apart: 12, of which 7 were waited for; matrix products, arithmetic and copies ran while one was open for 3% of the time, Pallas kernels for 6%

profile of v9, /device:TPU:25, one launch (start us, length us, event | category | flops | bytes accessed | tf_op | source)
XLA Modules:
  0.0 208.1 jit_solution(11436003898724934996)
XLA Ops:
  7.2 0.8 multiply_convert_fusion
  8.0 16.1 %collective-permute-start = (bf16[128,128]{1,0:T(8,128)(2,1)S(1)}, bf16[128,128]{1,0:T(8,128)(2,1)S(1)}, u32[]{:S(2)}, u32[]{:S(2)}) collective-permute-start(bf16[128,128]{1,0:T(8,128)(2,1)S(1)} %multiply_convert_fusion), channel_id=1, source_target_pairs={{0,0},{8,8},{16,64},{24,72},{64,16},{72,24},{80,80},{88,88},{1,1},... | collective-permute-start | bytes 98312 | tf_op jit(solution)/shard_map/gather_inputs/ppermute | solution.py:25
  24.1 1.3 collective-permute-done
  25.4 0.7 broadcast_in_dim.6
  26.2 10.6 %all-to-all-start = ((bf16[8,128,128]{2,1,0:T(8,128)(2,1)}), bf16[8,128,128]{2,1,0:T(8,128)(2,1)S(1)}, u32[]{:S(2)}, u32[]{:S(2)}) async-start(bf16[8,128,128]{2,1,0:T(8,128)(2,1)} %broadcast_in_dim.6), calls=%async_computation | async-start | bytes 524288 | tf_op jit(solution)/shard_map/gather_inputs/all_to_all | solution.py:48
  36.8 4.0 %collective-permute-start.1 = (bf16[1024,512]{1,0:T(8,128)(2,1)}, bf16[1024,512]{1,0:T(8,128)(2,1)}, u32[]{:S(2)}, u32[]{:S(2)}) collective-permute-start(bf16[1024,512]{1,0:T(8,128)(2,1)} %g0_ref.3), channel_id=1, source_target_pairs={{0,32},{32,0},{1,33},{33,1},{2,34},{34,2},{3,35},{35,3},{4,36},{36... | collective-permute-start | bytes 3145736 | tf_op jit(solution)/shard_map/gather_inputs/ppermute | solution.py:25
  40.8 1.9 collective-permute-start.2
  42.7 6.0 %all-to-all-done = bf16[8,128,128]{2,1,0:T(8,128)(2,1)S(1)} async-done(((bf16[8,128,128]{2,1,0:T(8,128)(2,1)}), bf16[8,128,128]{2,1,0:T(8,128)(2,1)S(1)}, u32[]{:S(2)}, u32[]{:S(2)}) %all-to-all-start) | async-done | bytes 262176 | tf_op jit(solution)/shard_map/gather_inputs/all_to_all | solution.py:48
  48.7 0.2 copy.8
  48.9 0.1 copy.9
  49.1 1.1 broadcast_in_dim.15
  50.2 4.1 %all-to-all-start.1 = ((bf16[4,128,1024]{2,1,0:T(8,128)(2,1)}), bf16[4,128,1024]{2,1,0:T(8,128)(2,1)S(1)}, u32[]{:S(2)}, u32[]{:S(2)}) async-start(bf16[4,128,1024]{2,1,0:T(8,128)(2,1)} %broadcast_in_dim.15), calls=%async_computation.1 | async-start | bytes 2097152 | tf_op jit(solution)/shard_map/gather_inputs/all_to_all | solution.py:48
  54.4 7.9 %all-to-all-done.1.x_ref = bf16[4,128,1024]{2,1,0:T(8,128)(2,1)S(1)} async-done(((bf16[4,128,1024]{2,1,0:T(8,128)(2,1)}), bf16[4,128,1024]{2,1,0:T(8,128)(2,1)S(1)}, u32[]{:S(2)}, u32[]{:S(2)}) %all-to-all-start.1) | async-done | bytes 1048608 | tf_op jit(solution)/shard_map/gather_inputs/all_to_all | solution.py:48
  62.3 3.2 %partial_gate_up.1 = (bf16[128,1024]{1,0:T(8,128)(2,1)S(1)}, bf16[128,1024]{1,0:T(8,128)(2,1)S(1)}) custom-call(s32[3]{0:T(128)S(1)} %pad_add_fusion.place_ref, bf16[4,128,1024]{2,1,0:T(8,128)(2,1)S(1)} %all-to-all-done.1.x_ref, bf16[1024,512]{1,0:T(8,128)(2,1)S(1)} %copy-done.1, bf16[1024,512]{1,0:T(8,128)(2,1)S(1)} %copy-done.2, ...), custom_call_target="tpu_custom_call" | custom-call | flops 1073741824 | bytes 6291456 | tf_op jit(solution)/shard_map/partial_gate_up/partial_gate_up/pallas_call | solution.py:75
  65.5 0.7 copy-done.5
  66.3 7.3 %collective-permute-start.3 = (bf16[128,1024]{1,0:T(8,128)(2,1)}, bf16[128,1024]{1,0:T(8,128)(2,1)S(1)}, u32[]{:S(2)}, u32[]{:S(2)}) collective-permute-start(bf16[128,1024]{1,0:T(8,128)(2,1)} %copy-done.5), channel_id=1, source_target_pairs={{0,64},{64,0},{1,65},{65,1},{2,66},{66,2},{3,67},{67,3},{4,68},{68... | collective-permute-start | bytes 786440 | tf_op jit(solution)/shard_map/half_sum/ppermute | solution.py:25
  73.6 8.9 %collective-permute-done.3.other_ref = bf16[128,1024]{1,0:T(8,128)(2,1)S(1)} collective-permute-done((bf16[128,1024]{1,0:T(8,128)(2,1)}, bf16[128,1024]{1,0:T(8,128)(2,1)S(1)}, u32[]{:S(2)}, u32[]{:S(2)}) %collective-permute-start.3) | collective-permute-done | bytes 262176 | tf_op jit(solution)/shard_map/half_sum/ppermute | solution.py:25
  82.4 0.2 hidden_grad.1.d0_ref
  82.6 7.3 %collective-permute-start.4 = (bf16[128,1024]{1,0:T(8,128)(2,1)S(1)}, bf16[128,1024]{1,0:T(8,128)(2,1)S(1)}, u32[]{:S(2)}, u32[]{:S(2)}) collective-permute-start(bf16[128,1024]{1,0:T(8,128)(2,1)S(1)} %hidden_grad.1.d0_ref), channel_id=1, source_target_pairs={{0,64},{64,0},{1,65},{65,1},{2,66},{66,2},{3,67},{67,3},{4,68},{68... | collective-permute-start | bytes 786440 | tf_op jit(solution)/shard_map/d_far/ppermute | solution.py:25
  89.9 19.8 %collective-permute-done.4.d1_ref = bf16[128,1024]{1,0:T(8,128)(2,1)S(1)} collective-permute-done((bf16[128,1024]{1,0:T(8,128)(2,1)S(1)}, bf16[128,1024]{1,0:T(8,128)(2,1)S(1)}, u32[]{:S(2)}, u32[]{:S(2)}) %collective-permute-start.4) | collective-permute-done | bytes 262176 | tf_op jit(solution)/shard_map/d_far/ppermute | solution.py:25
  109.7 2.9 %input_grad.1 = bf16[4,128,1024]{2,1,0:T(8,128)(2,1)S(1)} custom-call(s32[3]{0:T(128)S(1)} %pad_add_fusion.place_ref, bf16[128,1024]{1,0:T(8,128)(2,1)S(1)} %hidden_grad.1.d0_ref, bf16[128,1024]{1,0:T(8,128)(2,1)S(1)} %collective-permute-done.4.d1_ref, bf16[1024,512]{1,0:T(8,128)(2,1)S(1)} %copy-done.1, bf16[1024,512]{1,0:T(8,128)(2,1)S(1)} %copy-done.2, ...), custom_call_target="tpu_custom_call" | custom-call | flops 1073741824 | bytes 6291456 | tf_op jit(solution)/shard_map/d_input/input_grad/pallas_call | solution.py:126
  112.6 0.8 pad_maximum_fusion
  113.4 13.0 %all-gather.3.cloned.1.call-done.x_ref = bf16[16,128,1024]{2,1,0:T(8,128)(2,1)} async-done(((bf16[4,128,1024]{2,1,0:T(8,128)(2,1)}), bf16[16,128,1024]{2,1,0:T(8,128)(2,1)}) %all-gather.3.cloned.1.call-update) | async-done | bytes 4194320 | tf_op jit(solution)/shard_map/all_inputs/all_gather | solution.py:243
  126.5 12.0 %all_to_all.20.parts_ref = bf16[4,128,1024]{2,1,0:T(8,128)(2,1)S(1)} all-to-all(bf16[4,128,1024]{2,1,0:T(8,128)(2,1)S(1)} %input_grad.1), channel_id=1, replica_groups=mesh['x'=4,'zh'=2,'c'=2,'y'=4,'zl'=8] {'y'}, dimensions={0} | all-to-all | bytes 2097152 | tf_op jit(solution)/shard_map/d_input/all_to_all | solution.py:253
  138.5 0.9 add_parts.1
  139.3 17.1 %all-to-all-start.3 = ((bf16[8,128,128]{2,1,0:T(8,128)(2,1)}), bf16[8,128,128]{2,1,0:T(8,128)(2,1)S(1)}, u32[]{:S(2)}, u32[]{:S(2)}) async-start(bf16[8,128,128]{2,1,0:T(8,128)(2,1)} %add_parts.1), calls=%async_computation.3 | async-start | bytes 524288 | tf_op jit(solution)/shard_map/d_input/all_to_all | solution.py:254
  156.4 15.4 %all-gather.5.cloned.1.call-done.d_ref = bf16[8,128,1024]{2,1,0:T(8,128)(2,1)} async-done(((bf16[2,128,1024]{2,1,0:T(8,128)(2,1)}), bf16[8,128,1024]{2,1,0:T(8,128)(2,1)}) %all-gather.5.cloned.1.call-update) | async-done | bytes 2097168 | tf_op jit(solution)/shard_map/d_over_x/all_gather | solution.py:257
  171.9 9.3 %weight_grad.1 = (bf16[1024,1024]{1,0:T(8,128)(2,1)}, bf16[1024,1024]{1,0:T(8,128)(2,1)}) custom-call(s32[3]{0:T(128)} %copy-done.4, bf16[16,128,1024]{2,1,0:T(8,128)(2,1)} %all-gather.3.cloned.1.call-done.x_ref, bf16[8,128,1024]{2,1,0:T(8,128)(2,1)} %all-gather.5.cloned.1.call-done.d_ref), custom_call_target="tpu_custom_call" | custom-call | flops 4294967296 | bytes 10485760 | tf_op jit(solution)/shard_map/weight_grads/weight_grad/pallas_call | solution.py:209
  181.2 2.6 %collective-permute-start.6 = (bf16[1024,1024]{1,0:T(8,128)(2,1)}, bf16[1024,1024]{1,0:T(8,128)(2,1)S(1)}, u32[]{:S(2)}, u32[]{:S(2)}) collective-permute-start(bf16[1024,1024]{1,0:T(8,128)(2,1)} %get-tuple-element.34), channel_id=1, source_target_pairs={{0,32},{32,0},{1,33},{33,1},{2,34},{34,2},{3,35},{35,3},{4,36},{36... | collective-permute-start | bytes 6291464 | tf_op jit(solution)/shard_map/weight_grads/ppermute | solution.py:25
  183.8 13.4 %collective-permute-start.5 = (bf16[128,128]{1,0:T(8,128)(2,1)S(1)}, bf16[128,128]{1,0:T(8,128)(2,1)S(1)}, u32[]{:S(2)}, u32[]{:S(2)}) collective-permute-start(bf16[128,128]{1,0:T(8,128)(2,1)S(1)} %reduce_sum.12), channel_id=1, source_target_pairs={{0,0},{8,8},{16,64},{24,72},{64,16},{72,24},{80,80},{88,88},{1,1},... | collective-permute-start | bytes 98312 | tf_op jit(solution)/shard_map/d_input/ppermute | solution.py:25
  197.2 3.4 %add_convert_fusion = (bf16[1024,512]{1,0:T(8,128)(2,1)}, bf16[1024,512]{1,0:T(8,128)(2,1)}) fusion(bf16[1024,1024]{1,0:T(8,128)(2,1)S(1)} %collective-permute-done.6, bf16[1024,1024]{1,0:T(8,128)(2,1)} %get-tuple-element.33), kind=kLoop, calls=%fused_computation | loop fusion | flops 4194304 | bytes 6291456 | tf_op jit(solution)/shard_map/weight_grads/convert_element_type | solution.py:263
  200.7 0.6 copy.11
  (22 shorter events, 0.2 us)
Async XLA Ops:
  8.0 17.4 %collective-permute-start = (bf16[128,128]{1,0:T(8,128)(2,1)S(1)}, bf16[128,128]{1,0:T(8,128)(2,1)S(1)}, u32[]{:S(2)}, u32[]{:S(2)}) collective-permute-start(bf16[128,128]{1,0:T(8,128)(2,1)S(1)} %multiply_convert_fusion), channel_id=1, source_target_pairs={{0,0},{8,8},{16,64},{24,72},{64,16},{72,24},{80,80},{88,88},{1,1},... | collective-permute-start | bytes 98312 | tf_op jit(solution)/shard_map/gather_inputs/ppermute | solution.py:25
  26.2 22.5 %all-to-all-start = ((bf16[8,128,128]{2,1,0:T(8,128)(2,1)}), bf16[8,128,128]{2,1,0:T(8,128)(2,1)S(1)}, u32[]{:S(2)}, u32[]{:S(2)}) async-start(bf16[8,128,128]{2,1,0:T(8,128)(2,1)} %broadcast_in_dim.6), calls=%async_computation | async-start | bytes 524288 | tf_op jit(solution)/shard_map/gather_inputs/all_to_all | solution.py:48
  36.8 17.6 %collective-permute-start.1 = (bf16[1024,512]{1,0:T(8,128)(2,1)}, bf16[1024,512]{1,0:T(8,128)(2,1)}, u32[]{:S(2)}, u32[]{:S(2)}) collective-permute-start(bf16[1024,512]{1,0:T(8,128)(2,1)} %g0_ref.3), channel_id=1, source_target_pairs={{0,32},{32,0},{1,33},{33,1},{2,34},{34,2},{3,35},{35,3},{4,36},{36... | collective-permute-start | bytes 3145736 | tf_op jit(solution)/shard_map/gather_inputs/ppermute | solution.py:25
  40.8 13.6 %collective-permute-start.2 = (bf16[1024,512]{1,0:T(8,128)(2,1)}, bf16[1024,512]{1,0:T(8,128)(2,1)}, u32[]{:S(2)}, u32[]{:S(2)}) collective-permute-start(bf16[1024,512]{1,0:T(8,128)(2,1)} %u0_ref.3), channel_id=1, source_target_pairs={{0,32},{32,0},{1,33},{33,1},{2,34},{34,2},{3,35},{35,3},{4,36},{36... | collective-permute-start | bytes 3145736 | tf_op jit(solution)/shard_map/gather_inputs/ppermute | solution.py:25
  48.9 13.4 %copy-start.1 = (bf16[1024,512]{1,0:T(8,128)(2,1)S(1)}, bf16[1024,512]{1,0:T(8,128)(2,1)}, u32[]{:S(2)}) copy-start(bf16[1024,512]{1,0:T(8,128)(2,1)} %g0_ref.3) | copy-start | bytes 3145732
  48.9 13.4 %copy-start.2 = (bf16[1024,512]{1,0:T(8,128)(2,1)S(1)}, bf16[1024,512]{1,0:T(8,128)(2,1)}, u32[]{:S(2)}) copy-start(bf16[1024,512]{1,0:T(8,128)(2,1)} %u0_ref.3) | copy-start | bytes 3145732
  50.2 12.1 %all-to-all-start.1 = ((bf16[4,128,1024]{2,1,0:T(8,128)(2,1)}), bf16[4,128,1024]{2,1,0:T(8,128)(2,1)S(1)}, u32[]{:S(2)}, u32[]{:S(2)}) async-start(bf16[4,128,1024]{2,1,0:T(8,128)(2,1)} %broadcast_in_dim.15), calls=%async_computation.1 | async-start | bytes 2097152 | tf_op jit(solution)/shard_map/gather_inputs/all_to_all | solution.py:48
  54.3 72.2 %all-gather.3.cloned.1.call-start = ((), (), s32[]{:S(2)}) async-start(), calls=%async_computation.4 | async-start | bytes 5242880 | tf_op jit(solution)/shard_map/all_inputs/all_gather | solution.py:243
  54.4 55.3 %copy-start.4 = (s32[3]{0:T(128)}, s32[3]{0:T(128)S(1)}, u32[]{:S(2)}) copy-start(s32[3]{0:T(128)S(1)} %pad_add_fusion.place_ref) | copy-start | bytes 40
  62.3 3.2 %copy-start = (bf16[4,128,1024]{2,1,0:T(8,128)(2,1)}, bf16[4,128,1024]{2,1,0:T(8,128)(2,1)S(1)}, u32[]{:S(2)}) copy-start(bf16[4,128,1024]{2,1,0:T(8,128)(2,1)S(1)} %all-to-all-done.1.x_ref) | copy-start | bytes 3145732
  62.3 20.1 %copy-start.3 = (bf16[128,512]{1,0:T(8,128)(2,1)S(1)}, bf16[128,512]{1,0:T(8,128)(2,1)}, u32[]{:S(2)}) copy-start(bf16[128,512]{1,0:T(8,128)(2,1)} %grad_ref.1) | copy-start | bytes 393220
  65.5 0.7 copy-start.5
  66.3 105.6 %all-gather.5.cloned.1.call-start = ((), (), s32[]{:S(2)}) async-start(), calls=%async_computation.5 | async-start | bytes 2621440 | tf_op jit(solution)/shard_map/d_over_x/all_gather | solution.py:257
  66.3 16.1 %collective-permute-start.3 = (bf16[128,1024]{1,0:T(8,128)(2,1)}, bf16[128,1024]{1,0:T(8,128)(2,1)S(1)}, u32[]{:S(2)}, u32[]{:S(2)}) collective-permute-start(bf16[128,1024]{1,0:T(8,128)(2,1)} %copy-done.5), channel_id=1, source_target_pairs={{0,64},{64,0},{1,65},{65,1},{2,66},{66,2},{3,67},{67,3},{4,68},{68... | collective-permute-start | bytes 786440 | tf_op jit(solution)/shard_map/half_sum/ppermute | solution.py:25
  82.6 27.1 %collective-permute-start.4 = (bf16[128,1024]{1,0:T(8,128)(2,1)S(1)}, bf16[128,1024]{1,0:T(8,128)(2,1)S(1)}, u32[]{:S(2)}, u32[]{:S(2)}) collective-permute-start(bf16[128,1024]{1,0:T(8,128)(2,1)S(1)} %hidden_grad.1.d0_ref), channel_id=1, source_target_pairs={{0,64},{64,0},{1,65},{65,1},{2,66},{66,2},{3,67},{67,3},{4,68},{68... | collective-permute-start | bytes 786440 | tf_op jit(solution)/shard_map/d_far/ppermute | solution.py:25
  139.3 41.8 %all-to-all-start.3 = ((bf16[8,128,128]{2,1,0:T(8,128)(2,1)}), bf16[8,128,128]{2,1,0:T(8,128)(2,1)S(1)}, u32[]{:S(2)}, u32[]{:S(2)}) async-start(bf16[8,128,128]{2,1,0:T(8,128)(2,1)} %add_parts.1), calls=%async_computation.3 | async-start | bytes 524288 | tf_op jit(solution)/shard_map/d_input/all_to_all | solution.py:254
  181.2 16.0 %collective-permute-start.6 = (bf16[1024,1024]{1,0:T(8,128)(2,1)}, bf16[1024,1024]{1,0:T(8,128)(2,1)S(1)}, u32[]{:S(2)}, u32[]{:S(2)}) collective-permute-start(bf16[1024,1024]{1,0:T(8,128)(2,1)} %get-tuple-element.34), channel_id=1, source_target_pairs={{0,32},{32,0},{1,33},{33,1},{2,34},{34,2},{3,35},{35,3},{4,36},{36... | collective-permute-start | bytes 6291464 | tf_op jit(solution)/shard_map/weight_grads/ppermute | solution.py:25
  183.8 16.9 %collective-permute-start.5 = (bf16[128,128]{1,0:T(8,128)(2,1)S(1)}, bf16[128,128]{1,0:T(8,128)(2,1)S(1)}, u32[]{:S(2)}, u32[]{:S(2)}) collective-permute-start(bf16[128,128]{1,0:T(8,128)(2,1)S(1)} %reduce_sum.12), channel_id=1, source_target_pairs={{0,0},{8,8},{16,64},{24,72},{64,16},{72,24},{80,80},{88,88},{1,1},... | collective-permute-start | bytes 98312 | tf_op jit(solution)/shard_map/d_input/ppermute | solution.py:25
Sparse Core Ops, SparseCore 0:
  66.4 60.0 all-gather.2
  129.1 42.6 all-gather.4

commit v10 on v9

--- a/solution.py
+++ b/solution.py
@@ -249,7 +249,6 @@
         d_far = swap_half(d_own)
     with jax.named_scope("d_input"):
         di = input_grad(place, d_own, d_far, weights)
-        di, d_own, d_far = lax.optimization_barrier((di, d_own, d_far))
         di = add_parts(lax.all_to_all(di, "y", 0, 0), width)
         di = lax.all_to_all(di, "zl", 0, 0)
     with jax.named_scope("d_over_x"):

time: 209 us -> 206 us (0.986)
  starting transfers between devices: 84.4 us -> 81.6 us
    all_gather x1, waiting for transfers between devices: 13 us -> 15.9 us  [shards(): all_inputs = lax.all_gather(inputs, 'x', axis=0, tiled=True)]
    all_gather x1, waiting for transfers between devices: 15.4 us -> 12.6 us  [shards(): d_all = lax.all_gather(d_both, 'x', axis=0, tiled=True)]
    all_to_all x1, starting transfers between devices: 17.1 us -> 14.2 us  [shards(): di = lax.all_to_all(di, 'zl', 0, 0)]
where the time goes in v10:
time: 206 us; the launch traced here: 205 us
  starting transfers between devices  81.6 us (40%)
  waiting for transfers between devices  72.4 us (35%)
  Pallas kernels  16.4 us (8%)
  between operations  14.2 us (7%)
  blocking collectives  12 us (6%)
  other arithmetic  5.24 us (3%)
  local copies, waits for them, and re-layouts  3.49 us (2%)
    ppermute x7, starting transfers between devices, permute(): return lax.ppermute(value, axes if len(axes) > 1 else axes[0], pairs)  52.6 us
    ppermute x7, waiting for transfers between devices, permute(): return lax.ppermute(value, axes if len(axes) > 1 else axes[0], pairs)  29.9 us
    all_gather x1, waiting for transfers between devices, shards(): all_inputs = lax.all_gather(inputs, 'x', axis=0, tiled=True)  15.9 us
    all_to_all x2, starting transfers between devices, spread(): lax.all_to_all(jnp.broadcast_to(value[None], (n,) + value.shape), axis, 0...  14.7 us
    all_to_all x1, starting transfers between devices, shards(): di = lax.all_to_all(di, 'zl', 0, 0)  14.2 us
    all_to_all x2, waiting for transfers between devices, spread(): lax.all_to_all(jnp.broadcast_to(value[None], (n,) + value.shape), axis, 0...  13.9 us
    all_gather x1, waiting for transfers between devices, shards(): d_all = lax.all_gather(d_both, 'x', axis=0, tiled=True)  12.6 us
    all_to_all x1, blocking collectives, shards(): di = add_parts(lax.all_to_all(di, 'y', 0, 0), width)  12 us
  transfers between devices with their start and end apart: 12, of which 7 were waited for; matrix products, arithmetic and copies ran while one was open for 3% of the time, Pallas kernels for 6%

profile of v10, /device:TPU:25, one launch (start us, length us, event | category | flops | bytes accessed | tf_op | source)
XLA Modules:
  0.0 205.3 jit_solution(12189750241730696661)
XLA Ops:
  7.2 0.8 multiply_convert_fusion
  8.0 16.1 %collective-permute-start = (bf16[128,128]{1,0:T(8,128)(2,1)S(1)}, bf16[128,128]{1,0:T(8,128)(2,1)S(1)}, u32[]{:S(2)}, u32[]{:S(2)}) collective-permute-start(bf16[128,128]{1,0:T(8,128)(2,1)S(1)} %multiply_convert_fusion), channel_id=1, source_target_pairs={{0,0},{8,8},{16,64},{24,72},{64,16},{72,24},{80,80},{88,88},{1,1},... | collective-permute-start | bytes 98312 | tf_op jit(solution)/shard_map/gather_inputs/ppermute | solution.py:25
  24.1 1.3 collective-permute-done
  25.4 0.7 broadcast_in_dim.6
  26.2 10.6 %all-to-all-start = ((bf16[8,128,128]{2,1,0:T(8,128)(2,1)}), bf16[8,128,128]{2,1,0:T(8,128)(2,1)S(1)}, u32[]{:S(2)}, u32[]{:S(2)}) async-start(bf16[8,128,128]{2,1,0:T(8,128)(2,1)} %broadcast_in_dim.6), calls=%async_computation | async-start | bytes 524288 | tf_op jit(solution)/shard_map/gather_inputs/all_to_all | solution.py:48
  36.8 4.0 %collective-permute-start.1 = (bf16[1024,512]{1,0:T(8,128)(2,1)}, bf16[1024,512]{1,0:T(8,128)(2,1)}, u32[]{:S(2)}, u32[]{:S(2)}) collective-permute-start(bf16[1024,512]{1,0:T(8,128)(2,1)} %g0_ref.3), channel_id=1, source_target_pairs={{0,32},{32,0},{1,33},{33,1},{2,34},{34,2},{3,35},{35,3},{4,36},{36... | collective-permute-start | bytes 3145736 | tf_op jit(solution)/shard_map/gather_inputs/ppermute | solution.py:25
  40.8 1.9 collective-permute-start.2
  42.7 6.0 %all-to-all-done = bf16[8,128,128]{2,1,0:T(8,128)(2,1)S(1)} async-done(((bf16[8,128,128]{2,1,0:T(8,128)(2,1)}), bf16[8,128,128]{2,1,0:T(8,128)(2,1)S(1)}, u32[]{:S(2)}, u32[]{:S(2)}) %all-to-all-start) | async-done | bytes 262176 | tf_op jit(solution)/shard_map/gather_inputs/all_to_all | solution.py:48
  48.7 0.2 copy.8
  48.9 0.1 copy.9
  49.1 1.1 broadcast_in_dim.15
  50.2 4.1 %all-to-all-start.1 = ((bf16[4,128,1024]{2,1,0:T(8,128)(2,1)}), bf16[4,128,1024]{2,1,0:T(8,128)(2,1)S(1)}, u32[]{:S(2)}, u32[]{:S(2)}) async-start(bf16[4,128,1024]{2,1,0:T(8,128)(2,1)} %broadcast_in_dim.15), calls=%async_computation.1 | async-start | bytes 2097152 | tf_op jit(solution)/shard_map/gather_inputs/all_to_all | solution.py:48
  54.4 7.9 %all-to-all-done.1.x_ref = bf16[4,128,1024]{2,1,0:T(8,128)(2,1)S(1)} async-done(((bf16[4,128,1024]{2,1,0:T(8,128)(2,1)}), bf16[4,128,1024]{2,1,0:T(8,128)(2,1)S(1)}, u32[]{:S(2)}, u32[]{:S(2)}) %all-to-all-start.1) | async-done | bytes 1048608 | tf_op jit(solution)/shard_map/gather_inputs/all_to_all | solution.py:48
  62.3 3.2 %partial_gate_up.1 = (bf16[128,1024]{1,0:T(8,128)(2,1)S(1)}, bf16[128,1024]{1,0:T(8,128)(2,1)S(1)}) custom-call(s32[3]{0:T(128)S(1)} %pad_add_fusion.place_ref, bf16[4,128,1024]{2,1,0:T(8,128)(2,1)S(1)} %all-to-all-done.1.x_ref, bf16[1024,512]{1,0:T(8,128)(2,1)S(1)} %copy-done.1, bf16[1024,512]{1,0:T(8,128)(2,1)S(1)} %copy-done.2, ...), custom_call_target="tpu_custom_call" | custom-call | flops 1073741824 | bytes 6291456 | tf_op jit(solution)/shard_map/partial_gate_up/partial_gate_up/pallas_call | solution.py:75
  65.5 0.7 copy-done.5
  66.3 7.3 %collective-permute-start.3 = (bf16[128,1024]{1,0:T(8,128)(2,1)}, bf16[128,1024]{1,0:T(8,128)(2,1)S(1)}, u32[]{:S(2)}, u32[]{:S(2)}) collective-permute-start(bf16[128,1024]{1,0:T(8,128)(2,1)} %copy-done.5), channel_id=1, source_target_pairs={{0,64},{64,0},{1,65},{65,1},{2,66},{66,2},{3,67},{67,3},{4,68},{68... | collective-permute-start | bytes 786440 | tf_op jit(solution)/shard_map/half_sum/ppermute | solution.py:25
  73.6 8.9 %collective-permute-done.3.other_ref = bf16[128,1024]{1,0:T(8,128)(2,1)S(1)} collective-permute-done((bf16[128,1024]{1,0:T(8,128)(2,1)}, bf16[128,1024]{1,0:T(8,128)(2,1)S(1)}, u32[]{:S(2)}, u32[]{:S(2)}) %collective-permute-start.3) | collective-permute-done | bytes 262176 | tf_op jit(solution)/shard_map/half_sum/ppermute | solution.py:25
  82.4 0.2 hidden_grad.1.d0_ref
  82.6 7.3 %collective-permute-start.4 = (bf16[128,1024]{1,0:T(8,128)(2,1)S(1)}, bf16[128,1024]{1,0:T(8,128)(2,1)S(1)}, u32[]{:S(2)}, u32[]{:S(2)}) collective-permute-start(bf16[128,1024]{1,0:T(8,128)(2,1)S(1)} %hidden_grad.1.d0_ref), channel_id=1, source_target_pairs={{0,64},{64,0},{1,65},{65,1},{2,66},{66,2},{3,67},{67,3},{4,68},{68... | collective-permute-start | bytes 786440 | tf_op jit(solution)/shard_map/d_far/ppermute | solution.py:25
  89.9 19.8 %collective-permute-done.4.d1_ref = bf16[128,1024]{1,0:T(8,128)(2,1)S(1)} collective-permute-done((bf16[128,1024]{1,0:T(8,128)(2,1)S(1)}, bf16[128,1024]{1,0:T(8,128)(2,1)S(1)}, u32[]{:S(2)}, u32[]{:S(2)}) %collective-permute-start.4) | collective-permute-done | bytes 262176 | tf_op jit(solution)/shard_map/d_far/ppermute | solution.py:25
  109.7 0.8 pad_maximum_fusion
  110.5 15.9 %all-gather.3.cloned.1.call-done.x_ref = bf16[16,128,1024]{2,1,0:T(8,128)(2,1)} async-done(((bf16[4,128,1024]{2,1,0:T(8,128)(2,1)}), bf16[16,128,1024]{2,1,0:T(8,128)(2,1)}) %all-gather.3.cloned.1.call-update) | async-done | bytes 4194320 | tf_op jit(solution)/shard_map/all_inputs/all_gather | solution.py:243
  126.5 2.8 %input_grad.1 = bf16[4,128,1024]{2,1,0:T(8,128)(2,1)S(1)} custom-call(s32[3]{0:T(128)S(1)} %pad_add_fusion.place_ref, bf16[128,1024]{1,0:T(8,128)(2,1)S(1)} %hidden_grad.1.d0_ref, bf16[128,1024]{1,0:T(8,128)(2,1)S(1)} %collective-permute-done.4.d1_ref, bf16[1024,512]{1,0:T(8,128)(2,1)S(1)} %copy-done.1, bf16[1024,512]{1,0:T(8,128)(2,1)S(1)} %copy-done.2, ...), custom_call_target="tpu_custom_call" | custom-call | flops 1073741824 | bytes 6291456 | tf_op jit(solution)/shard_map/d_input/input_grad/pallas_call | solution.py:126
  129.3 12.0 %all_to_all.20.parts_ref = bf16[4,128,1024]{2,1,0:T(8,128)(2,1)S(1)} all-to-all(bf16[4,128,1024]{2,1,0:T(8,128)(2,1)S(1)} %input_grad.1), channel_id=1, replica_groups=mesh['x'=4,'zh'=2,'c'=2,'y'=4,'zl'=8] {'y'}, dimensions={0} | all-to-all | bytes 2097152 | tf_op jit(solution)/shard_map/d_input/all_to_all | solution.py:252
  141.3 0.9 add_parts.1
  142.2 14.2 %all-to-all-start.3 = ((bf16[8,128,128]{2,1,0:T(8,128)(2,1)}), bf16[8,128,128]{2,1,0:T(8,128)(2,1)S(1)}, u32[]{:S(2)}, u32[]{:S(2)}) async-start(bf16[8,128,128]{2,1,0:T(8,128)(2,1)} %add_parts.1), calls=%async_computation.3 | async-start | bytes 524288 | tf_op jit(solution)/shard_map/d_input/all_to_all | solution.py:253
  156.4 12.6 %all-gather.5.cloned.1.call-done.d_ref = bf16[8,128,1024]{2,1,0:T(8,128)(2,1)} async-done(((bf16[2,128,1024]{2,1,0:T(8,128)(2,1)}), bf16[8,128,1024]{2,1,0:T(8,128)(2,1)}) %all-gather.5.cloned.1.call-update) | async-done | bytes 2097168 | tf_op jit(solution)/shard_map/d_over_x/all_gather | solution.py:256
  169.0 9.3 %weight_grad.1 = (bf16[1024,1024]{1,0:T(8,128)(2,1)}, bf16[1024,1024]{1,0:T(8,128)(2,1)}) custom-call(s32[3]{0:T(128)} %copy-done.4, bf16[16,128,1024]{2,1,0:T(8,128)(2,1)} %all-gather.3.cloned.1.call-done.x_ref, bf16[8,128,1024]{2,1,0:T(8,128)(2,1)} %all-gather.5.cloned.1.call-done.d_ref), custom_call_target="tpu_custom_call" | custom-call | flops 4294967296 | bytes 10485760 | tf_op jit(solution)/shard_map/weight_grads/weight_grad/pallas_call | solution.py:209
  178.3 2.6 %collective-permute-start.6 = (bf16[1024,1024]{1,0:T(8,128)(2,1)}, bf16[1024,1024]{1,0:T(8,128)(2,1)S(1)}, u32[]{:S(2)}, u32[]{:S(2)}) collective-permute-start(bf16[1024,1024]{1,0:T(8,128)(2,1)} %get-tuple-element.28), channel_id=1, source_target_pairs={{0,32},{32,0},{1,33},{33,1},{2,34},{34,2},{3,35},{35,3},{4,36},{36... | collective-permute-start | bytes 6291464 | tf_op jit(solution)/shard_map/weight_grads/ppermute | solution.py:25
  181.0 13.4 %collective-permute-start.5 = (bf16[128,128]{1,0:T(8,128)(2,1)S(1)}, bf16[128,128]{1,0:T(8,128)(2,1)S(1)}, u32[]{:S(2)}, u32[]{:S(2)}) collective-permute-start(bf16[128,128]{1,0:T(8,128)(2,1)S(1)} %reduce_sum.12), channel_id=1, source_target_pairs={{0,0},{8,8},{16,64},{24,72},{64,16},{72,24},{80,80},{88,88},{1,1},... | collective-permute-start | bytes 98312 | tf_op jit(solution)/shard_map/d_input/ppermute | solution.py:25
  194.4 3.4 %add_convert_fusion = (bf16[1024,512]{1,0:T(8,128)(2,1)}, bf16[1024,512]{1,0:T(8,128)(2,1)}) fusion(bf16[1024,1024]{1,0:T(8,128)(2,1)S(1)} %collective-permute-done.6, bf16[1024,1024]{1,0:T(8,128)(2,1)} %get-tuple-element.27), kind=kLoop, calls=%fused_computation | loop fusion | flops 4194304 | bytes 6291456 | tf_op jit(solution)/shard_map/weight_grads/convert_element_type | solution.py:262
  197.8 0.6 copy.11
  (22 shorter events, 0.2 us)
Async XLA Ops:
  8.0 17.4 %collective-permute-start = (bf16[128,128]{1,0:T(8,128)(2,1)S(1)}, bf16[128,128]{1,0:T(8,128)(2,1)S(1)}, u32[]{:S(2)}, u32[]{:S(2)}) collective-permute-start(bf16[128,128]{1,0:T(8,128)(2,1)S(1)} %multiply_convert_fusion), channel_id=1, source_target_pairs={{0,0},{8,8},{16,64},{24,72},{64,16},{72,24},{80,80},{88,88},{1,1},... | collective-permute-start | bytes 98312 | tf_op jit(solution)/shard_map/gather_inputs/ppermute | solution.py:25
  26.2 22.5 %all-to-all-start = ((bf16[8,128,128]{2,1,0:T(8,128)(2,1)}), bf16[8,128,128]{2,1,0:T(8,128)(2,1)S(1)}, u32[]{:S(2)}, u32[]{:S(2)}) async-start(bf16[8,128,128]{2,1,0:T(8,128)(2,1)} %broadcast_in_dim.6), calls=%async_computation | async-start | bytes 524288 | tf_op jit(solution)/shard_map/gather_inputs/all_to_all | solution.py:48
  36.8 17.6 %collective-permute-start.1 = (bf16[1024,512]{1,0:T(8,128)(2,1)}, bf16[1024,512]{1,0:T(8,128)(2,1)}, u32[]{:S(2)}, u32[]{:S(2)}) collective-permute-start(bf16[1024,512]{1,0:T(8,128)(2,1)} %g0_ref.3), channel_id=1, source_target_pairs={{0,32},{32,0},{1,33},{33,1},{2,34},{34,2},{3,35},{35,3},{4,36},{36... | collective-permute-start | bytes 3145736 | tf_op jit(solution)/shard_map/gather_inputs/ppermute | solution.py:25
  40.8 13.6 %collective-permute-start.2 = (bf16[1024,512]{1,0:T(8,128)(2,1)}, bf16[1024,512]{1,0:T(8,128)(2,1)}, u32[]{:S(2)}, u32[]{:S(2)}) collective-permute-start(bf16[1024,512]{1,0:T(8,128)(2,1)} %u0_ref.3), channel_id=1, source_target_pairs={{0,32},{32,0},{1,33},{33,1},{2,34},{34,2},{3,35},{35,3},{4,36},{36... | collective-permute-start | bytes 3145736 | tf_op jit(solution)/shard_map/gather_inputs/ppermute | solution.py:25
  48.9 13.4 %copy-start.1 = (bf16[1024,512]{1,0:T(8,128)(2,1)S(1)}, bf16[1024,512]{1,0:T(8,128)(2,1)}, u32[]{:S(2)}) copy-start(bf16[1024,512]{1,0:T(8,128)(2,1)} %g0_ref.3) | copy-start | bytes 3145732
  48.9 13.4 %copy-start.2 = (bf16[1024,512]{1,0:T(8,128)(2,1)S(1)}, bf16[1024,512]{1,0:T(8,128)(2,1)}, u32[]{:S(2)}) copy-start(bf16[1024,512]{1,0:T(8,128)(2,1)} %u0_ref.3) | copy-start | bytes 3145732
  50.2 12.1 %all-to-all-start.1 = ((bf16[4,128,1024]{2,1,0:T(8,128)(2,1)}), bf16[4,128,1024]{2,1,0:T(8,128)(2,1)S(1)}, u32[]{:S(2)}, u32[]{:S(2)}) async-start(bf16[4,128,1024]{2,1,0:T(8,128)(2,1)} %broadcast_in_dim.15), calls=%async_computation.1 | async-start | bytes 2097152 | tf_op jit(solution)/shard_map/gather_inputs/all_to_all | solution.py:48
  54.3 72.2 %all-gather.3.cloned.1.call-start = ((), (), s32[]{:S(2)}) async-start(), calls=%async_computation.4 | async-start | bytes 5242880 | tf_op jit(solution)/shard_map/all_inputs/all_gather | solution.py:243
  54.4 72.1 %copy-start.4 = (s32[3]{0:T(128)}, s32[3]{0:T(128)S(1)}, u32[]{:S(2)}) copy-start(s32[3]{0:T(128)S(1)} %pad_add_fusion.place_ref) | copy-start | bytes 40
  62.3 3.2 %copy-start = (bf16[4,128,1024]{2,1,0:T(8,128)(2,1)}, bf16[4,128,1024]{2,1,0:T(8,128)(2,1)S(1)}, u32[]{:S(2)}) copy-start(bf16[4,128,1024]{2,1,0:T(8,128)(2,1)S(1)} %all-to-all-done.1.x_ref) | copy-start | bytes 3145732
  62.3 20.1 %copy-start.3 = (bf16[128,512]{1,0:T(8,128)(2,1)S(1)}, bf16[128,512]{1,0:T(8,128)(2,1)}, u32[]{:S(2)}) copy-start(bf16[128,512]{1,0:T(8,128)(2,1)} %grad_ref.1) | copy-start | bytes 393220
  65.5 0.7 copy-start.5
  66.3 102.8 %all-gather.5.cloned.1.call-start = ((), (), s32[]{:S(2)}) async-start(), calls=%async_computation.5 | async-start | bytes 2621440 | tf_op jit(solution)/shard_map/d_over_x/all_gather | solution.py:256
  66.3 16.1 %collective-permute-start.3 = (bf16[128,1024]{1,0:T(8,128)(2,1)}, bf16[128,1024]{1,0:T(8,128)(2,1)S(1)}, u32[]{:S(2)}, u32[]{:S(2)}) collective-permute-start(bf16[128,1024]{1,0:T(8,128)(2,1)} %copy-done.5), channel_id=1, source_target_pairs={{0,64},{64,0},{1,65},{65,1},{2,66},{66,2},{3,67},{67,3},{4,68},{68... | collective-permute-start | bytes 786440 | tf_op jit(solution)/shard_map/half_sum/ppermute | solution.py:25
  82.6 27.1 %collective-permute-start.4 = (bf16[128,1024]{1,0:T(8,128)(2,1)S(1)}, bf16[128,1024]{1,0:T(8,128)(2,1)S(1)}, u32[]{:S(2)}, u32[]{:S(2)}) collective-permute-start(bf16[128,1024]{1,0:T(8,128)(2,1)S(1)} %hidden_grad.1.d0_ref), channel_id=1, source_target_pairs={{0,64},{64,0},{1,65},{65,1},{2,66},{66,2},{3,67},{67,3},{4,68},{68... | collective-permute-start | bytes 786440 | tf_op jit(solution)/shard_map/d_far/ppermute | solution.py:25
  142.2 36.1 %all-to-all-start.3 = ((bf16[8,128,128]{2,1,0:T(8,128)(2,1)}), bf16[8,128,128]{2,1,0:T(8,128)(2,1)S(1)}, u32[]{:S(2)}, u32[]{:S(2)}) async-start(bf16[8,128,128]{2,1,0:T(8,128)(2,1)} %add_parts.1), calls=%async_computation.3 | async-start | bytes 524288 | tf_op jit(solution)/shard_map/d_input/all_to_all | solution.py:253
  178.3 16.0 %collective-permute-start.6 = (bf16[1024,1024]{1,0:T(8,128)(2,1)}, bf16[1024,1024]{1,0:T(8,128)(2,1)S(1)}, u32[]{:S(2)}, u32[]{:S(2)}) collective-permute-start(bf16[1024,1024]{1,0:T(8,128)(2,1)} %get-tuple-element.28), channel_id=1, source_target_pairs={{0,32},{32,0},{1,33},{33,1},{2,34},{34,2},{3,35},{35,3},{4,36},{36... | collective-permute-start | bytes 6291464 | tf_op jit(solution)/shard_map/weight_grads/ppermute | solution.py:25
  181.0 16.9 %collective-permute-start.5 = (bf16[128,128]{1,0:T(8,128)(2,1)S(1)}, bf16[128,128]{1,0:T(8,128)(2,1)S(1)}, u32[]{:S(2)}, u32[]{:S(2)}) collective-permute-start(bf16[128,128]{1,0:T(8,128)(2,1)S(1)} %reduce_sum.12), channel_id=1, source_target_pairs={{0,0},{8,8},{16,64},{24,72},{64,16},{72,24},{80,80},{88,88},{1,1},... | collective-permute-start | bytes 98312 | tf_op jit(solution)/shard_map/d_input/ppermute | solution.py:25
Sparse Core Ops, SparseCore 0:
  66.4 60.0 all-gather.2
  129.1 39.8 all-gather.4

commit v11 on v10

--- a/solution.py
+++ b/solution.py
@@ -160,12 +160,11 @@
 
 
 def weight_grad_kernel(
-    place_ref, x_ref, d_ref, sent_ref, keep_ref, x_held, d_held, out_held, x_sem, d_sem, out_sem
+    place_ref, x_ref, d_ref, sent_ref, keep_ref, x_held, d_held, total_held, out_held, x_sem, d_sem, out_sem
 ):
     half, core = place_ref[0], place_ref[1]
     pairs = d_ref.shape[0]
-    tokens = pltpu.make_async_copy(d_ref, d_held, d_sem.at[0])
-    tokens.start()
+    tokens = [pltpu.make_async_copy(d_ref.at[n], d_held.at[n], d_sem.at[n]) for n in range(pairs)]
     fetches = []
     for m in range(2):
         b = 1 - core if m == 0 else core
@@ -176,28 +175,45 @@
                     x_ref.at[4 * (n // 2) + 2 * a + b], x_held.at[m, n], x_sem.at[m, n]
                 )
             )
-    for fetch in fetches:
-        fetch.start()
-    tokens.wait()
+    for n in range(pairs):
+        tokens[n].start()
+        fetches[n].start()
+    for n in range(pairs):
+        fetches[pairs + n].start()
     writes = []
-    for m, out_ref in enumerate((sent_ref, keep_ref)):
-        for fetch in fetches[m * pairs : (m + 1) * pairs]:
-            fetch.wait()
-        for i in range(out_ref.shape[0] // STEP):
-            at = slice(i * STEP, (i + 1) * STEP)
-            out_held[m, at, :] = lax.dot_general(
-                x_held[m, :, :, at].reshape(-1, STEP),
-                d_held[...].reshape(-1, d_held.shape[2]),
-                (((0,), (0,)), ((), ())),
-                preferred_element_type=F32,
-            ).astype(BF16)
-            write = pltpu.make_async_copy(
-                out_held.at[m, pl.ds(i * STEP, STEP)],
-                out_ref.at[pl.ds(i * STEP, STEP)],
-                out_sem.at[m, i],
-            )
-            write.start()
-            writes.append(write)
+
+    def product(m, first, last, at):
+        return lax.dot_general(
+            x_held[m, first:last, :, at].reshape(-1, STEP),
+            d_held[first:last].reshape(-1, d_held.shape[2]),
+            (((0,), (0,)), ((), ())),
+            preferred_element_type=F32,
+        )
+
+    def write_out(m, i, out_ref, value):
+        out_held[m, i * STEP : (i + 1) * STEP, :] = value.astype(BF16)
+        write = pltpu.make_async_copy(
+            out_held.at[m, pl.ds(i * STEP, STEP)], out_ref.at[pl.ds(i * STEP, STEP)], out_sem.at[m, i]
+        )
+        write.start()
+        writes.append(write)
+
+    tiles = [(i, slice(i * STEP, (i + 1) * STEP)) for i in range(sent_ref.shape[0] // STEP)]
+    middle = pairs // 2
+    for n in range(middle):
+        tokens[n].wait()
+        fetches[n].wait()
+    for i, at in tiles:
+        total_held[at, :] = product(0, 0, middle, at)
+    for n in range(middle, pairs):
+        tokens[n].wait()
+        fetches[n].wait()
+    for i, at in tiles:
+        write_out(0, i, sent_ref, total_held[at, :] + product(0, middle, pairs, at))
+    for n in range(pairs):
+        fetches[pairs + n].wait()
+    for i, at in tiles:
+        write_out(1, i, keep_ref, product(1, 0, pairs, at))
     for write in writes:
         write.wait()
 
@@ -214,9 +230,10 @@
         scratch_shapes=[
             pltpu.VMEM((2, pairs, count, rows), BF16),
             pltpu.VMEM((pairs, count, cols), BF16),
+            pltpu.VMEM((rows, cols), F32),
             pltpu.VMEM((2, rows, cols), BF16),
             pltpu.SemaphoreType.DMA((2, pairs)),
-            pltpu.SemaphoreType.DMA((1,)),
+            pltpu.SemaphoreType.DMA((pairs,)),
             pltpu.SemaphoreType.DMA((2, rows // STEP)),
         ],
         compiler_params=pltpu.CompilerParams(vmem_limit_bytes=62 * 1024 * 1024),

time: 206 us -> 205 us (level)
  no operation moved by 1% of the time
where the time goes in v11:
time: 205 us
  starting transfers between devices  81.6 us (40%)
  waiting for transfers between devices  72.4 us (35%)
  Pallas kernels  15.8 us (8%)
  between operations  14.2 us (7%)
  blocking collectives  12 us (6%)
  other arithmetic  5.24 us (3%)
  local copies, waits for them, and re-layouts  3.49 us (2%)
    ppermute x7, starting transfers between devices, permute(): return lax.ppermute(value, axes if len(axes) > 1 else axes[0], pairs)  52.6 us
    ppermute x7, waiting for transfers between devices, permute(): return lax.ppermute(value, axes if len(axes) > 1 else axes[0], pairs)  29.9 us
    all_gather x1, waiting for transfers between devices, shards(): all_inputs = lax.all_gather(inputs, 'x', axis=0, tiled=True)  15.9 us
    all_to_all x2, starting transfers between devices, spread(): lax.all_to_all(jnp.broadcast_to(value[None], (n,) + value.shape), axis, 0...  14.7 us
    all_to_all x1, starting transfers between devices, shards(): di = lax.all_to_all(di, 'zl', 0, 0)  14.2 us
    all_to_all x2, waiting for transfers between devices, spread(): lax.all_to_all(jnp.broadcast_to(value[None], (n,) + value.shape), axis, 0...  13.9 us
    all_gather x1, waiting for transfers between devices, shards(): d_all = lax.all_gather(d_both, 'x', axis=0, tiled=True)  12.6 us
    all_to_all x1, blocking collectives, shards(): di = add_parts(lax.all_to_all(di, 'y', 0, 0), width)  12 us
  transfers between devices with their start and end apart: 12, of which 7 were waited for; matrix products, arithmetic and copies ran while one was open for 3% of the time, Pallas kernels for 6%

profile of v11, /device:TPU:25, one launch (start us, length us, event | category | flops | bytes accessed | tf_op | source)
XLA Modules:
  0.0 204.7 jit_solution(1814318394225728955)
XLA Ops:
  7.2 0.8 multiply_convert_fusion
  8.0 16.1 %collective-permute-start = (bf16[128,128]{1,0:T(8,128)(2,1)S(1)}, bf16[128,128]{1,0:T(8,128)(2,1)S(1)}, u32[]{:S(2)}, u32[]{:S(2)}) collective-permute-start(bf16[128,128]{1,0:T(8,128)(2,1)S(1)} %multiply_convert_fusion), channel_id=1, source_target_pairs={{0,0},{8,8},{16,64},{24,72},{64,16},{72,24},{80,80},{88,88},{1,1},... | collective-permute-start | bytes 98312 | tf_op jit(solution)/shard_map/gather_inputs/ppermute | solution.py:25
  24.1 1.3 collective-permute-done
  25.4 0.7 broadcast_in_dim.6
  26.2 10.6 %all-to-all-start = ((bf16[8,128,128]{2,1,0:T(8,128)(2,1)}), bf16[8,128,128]{2,1,0:T(8,128)(2,1)S(1)}, u32[]{:S(2)}, u32[]{:S(2)}) async-start(bf16[8,128,128]{2,1,0:T(8,128)(2,1)} %broadcast_in_dim.6), calls=%async_computation | async-start | bytes 524288 | tf_op jit(solution)/shard_map/gather_inputs/all_to_all | solution.py:48
  36.8 4.0 %collective-permute-start.1 = (bf16[1024,512]{1,0:T(8,128)(2,1)}, bf16[1024,512]{1,0:T(8,128)(2,1)}, u32[]{:S(2)}, u32[]{:S(2)}) collective-permute-start(bf16[1024,512]{1,0:T(8,128)(2,1)} %g0_ref.3), channel_id=1, source_target_pairs={{0,32},{32,0},{1,33},{33,1},{2,34},{34,2},{3,35},{35,3},{4,36},{36... | collective-permute-start | bytes 3145736 | tf_op jit(solution)/shard_map/gather_inputs/ppermute | solution.py:25
  40.8 1.9 collective-permute-start.2
  42.7 6.0 %all-to-all-done = bf16[8,128,128]{2,1,0:T(8,128)(2,1)S(1)} async-done(((bf16[8,128,128]{2,1,0:T(8,128)(2,1)}), bf16[8,128,128]{2,1,0:T(8,128)(2,1)S(1)}, u32[]{:S(2)}, u32[]{:S(2)}) %all-to-all-start) | async-done | bytes 262176 | tf_op jit(solution)/shard_map/gather_inputs/all_to_all | solution.py:48
  48.7 0.2 copy.8
  48.9 0.1 copy.9
  49.1 1.1 broadcast_in_dim.15
  50.2 4.1 %all-to-all-start.1 = ((bf16[4,128,1024]{2,1,0:T(8,128)(2,1)}), bf16[4,128,1024]{2,1,0:T(8,128)(2,1)S(1)}, u32[]{:S(2)}, u32[]{:S(2)}) async-start(bf16[4,128,1024]{2,1,0:T(8,128)(2,1)} %broadcast_in_dim.15), calls=%async_computation.1 | async-start | bytes 2097152 | tf_op jit(solution)/shard_map/gather_inputs/all_to_all | solution.py:48
  54.4 7.9 %all-to-all-done.1.x_ref = bf16[4,128,1024]{2,1,0:T(8,128)(2,1)S(1)} async-done(((bf16[4,128,1024]{2,1,0:T(8,128)(2,1)}), bf16[4,128,1024]{2,1,0:T(8,128)(2,1)S(1)}, u32[]{:S(2)}, u32[]{:S(2)}) %all-to-all-start.1) | async-done | bytes 1048608 | tf_op jit(solution)/shard_map/gather_inputs/all_to_all | solution.py:48
  62.3 3.2 %partial_gate_up.1 = (bf16[128,1024]{1,0:T(8,128)(2,1)S(1)}, bf16[128,1024]{1,0:T(8,128)(2,1)S(1)}) custom-call(s32[3]{0:T(128)S(1)} %pad_add_fusion.place_ref, bf16[4,128,1024]{2,1,0:T(8,128)(2,1)S(1)} %all-to-all-done.1.x_ref, bf16[1024,512]{1,0:T(8,128)(2,1)S(1)} %copy-done.1, bf16[1024,512]{1,0:T(8,128)(2,1)S(1)} %copy-done.2, ...), custom_call_target="tpu_custom_call" | custom-call | flops 1073741824 | bytes 6291456 | tf_op jit(solution)/shard_map/partial_gate_up/partial_gate_up/pallas_call | solution.py:75
  65.5 0.7 copy-done.5
  66.3 7.3 %collective-permute-start.3 = (bf16[128,1024]{1,0:T(8,128)(2,1)}, bf16[128,1024]{1,0:T(8,128)(2,1)S(1)}, u32[]{:S(2)}, u32[]{:S(2)}) collective-permute-start(bf16[128,1024]{1,0:T(8,128)(2,1)} %copy-done.5), channel_id=1, source_target_pairs={{0,64},{64,0},{1,65},{65,1},{2,66},{66,2},{3,67},{67,3},{4,68},{68... | collective-permute-start | bytes 786440 | tf_op jit(solution)/shard_map/half_sum/ppermute | solution.py:25
  73.6 8.9 %collective-permute-done.3.other_ref = bf16[128,1024]{1,0:T(8,128)(2,1)S(1)} collective-permute-done((bf16[128,1024]{1,0:T(8,128)(2,1)}, bf16[128,1024]{1,0:T(8,128)(2,1)S(1)}, u32[]{:S(2)}, u32[]{:S(2)}) %collective-permute-start.3) | collective-permute-done | bytes 262176 | tf_op jit(solution)/shard_map/half_sum/ppermute | solution.py:25
  82.4 0.2 hidden_grad.1.d0_ref
  82.6 7.3 %collective-permute-start.4 = (bf16[128,1024]{1,0:T(8,128)(2,1)S(1)}, bf16[128,1024]{1,0:T(8,128)(2,1)S(1)}, u32[]{:S(2)}, u32[]{:S(2)}) collective-permute-start(bf16[128,1024]{1,0:T(8,128)(2,1)S(1)} %hidden_grad.1.d0_ref), channel_id=1, source_target_pairs={{0,64},{64,0},{1,65},{65,1},{2,66},{66,2},{3,67},{67,3},{4,68},{68... | collective-permute-start | bytes 786440 | tf_op jit(solution)/shard_map/d_far/ppermute | solution.py:25
  89.9 19.8 %collective-permute-done.4.d1_ref = bf16[128,1024]{1,0:T(8,128)(2,1)S(1)} collective-permute-done((bf16[128,1024]{1,0:T(8,128)(2,1)S(1)}, bf16[128,1024]{1,0:T(8,128)(2,1)S(1)}, u32[]{:S(2)}, u32[]{:S(2)}) %collective-permute-start.4) | collective-permute-done | bytes 262176 | tf_op jit(solution)/shard_map/d_far/ppermute | solution.py:25
  109.7 0.8 pad_maximum_fusion
  110.5 15.9 %all-gather.3.cloned.1.call-done.x_ref = bf16[16,128,1024]{2,1,0:T(8,128)(2,1)} async-done(((bf16[4,128,1024]{2,1,0:T(8,128)(2,1)}), bf16[16,128,1024]{2,1,0:T(8,128)(2,1)}) %all-gather.3.cloned.1.call-update) | async-done | bytes 4194320 | tf_op jit(solution)/shard_map/all_inputs/all_gather | solution.py:260
  126.5 2.8 %input_grad.1 = bf16[4,128,1024]{2,1,0:T(8,128)(2,1)S(1)} custom-call(s32[3]{0:T(128)S(1)} %pad_add_fusion.place_ref, bf16[128,1024]{1,0:T(8,128)(2,1)S(1)} %hidden_grad.1.d0_ref, bf16[128,1024]{1,0:T(8,128)(2,1)S(1)} %collective-permute-done.4.d1_ref, bf16[1024,512]{1,0:T(8,128)(2,1)S(1)} %copy-done.1, bf16[1024,512]{1,0:T(8,128)(2,1)S(1)} %copy-done.2, ...), custom_call_target="tpu_custom_call" | custom-call | flops 1073741824 | bytes 6291456 | tf_op jit(solution)/shard_map/d_input/input_grad/pallas_call | solution.py:126
  129.3 12.0 %all_to_all.20.parts_ref = bf16[4,128,1024]{2,1,0:T(8,128)(2,1)S(1)} all-to-all(bf16[4,128,1024]{2,1,0:T(8,128)(2,1)S(1)} %input_grad.1), channel_id=1, replica_groups=mesh['x'=4,'zh'=2,'c'=2,'y'=4,'zl'=8] {'y'}, dimensions={0} | all-to-all | bytes 2097152 | tf_op jit(solution)/shard_map/d_input/all_to_all | solution.py:269
  141.3 0.9 add_parts.1
  142.2 14.2 %all-to-all-start.3 = ((bf16[8,128,128]{2,1,0:T(8,128)(2,1)}), bf16[8,128,128]{2,1,0:T(8,128)(2,1)S(1)}, u32[]{:S(2)}, u32[]{:S(2)}) async-start(bf16[8,128,128]{2,1,0:T(8,128)(2,1)} %add_parts.1), calls=%async_computation.3 | async-start | bytes 524288 | tf_op jit(solution)/shard_map/d_input/all_to_all | solution.py:270
  156.4 12.6 %all-gather.5.cloned.1.call-done.d_ref = bf16[8,128,1024]{2,1,0:T(8,128)(2,1)} async-done(((bf16[2,128,1024]{2,1,0:T(8,128)(2,1)}), bf16[8,128,1024]{2,1,0:T(8,128)(2,1)}) %all-gather.5.cloned.1.call-update) | async-done | bytes 2097168 | tf_op jit(solution)/shard_map/d_over_x/all_gather | solution.py:273
  169.0 8.7 %weight_grad.1 = (bf16[1024,1024]{1,0:T(8,128)(2,1)}, bf16[1024,1024]{1,0:T(8,128)(2,1)}) custom-call(s32[3]{0:T(128)} %copy-done.4, bf16[16,128,1024]{2,1,0:T(8,128)(2,1)} %all-gather.3.cloned.1.call-done.x_ref, bf16[8,128,1024]{2,1,0:T(8,128)(2,1)} %all-gather.5.cloned.1.call-done.d_ref), custom_call_target="tpu_custom_call" | custom-call | flops 4294967296 | bytes 10485760 | tf_op jit(solution)/shard_map/weight_grads/weight_grad/pallas_call | solution.py:225
  177.7 2.6 %collective-permute-start.6 = (bf16[1024,1024]{1,0:T(8,128)(2,1)}, bf16[1024,1024]{1,0:T(8,128)(2,1)S(1)}, u32[]{:S(2)}, u32[]{:S(2)}) collective-permute-start(bf16[1024,1024]{1,0:T(8,128)(2,1)} %get-tuple-element.28), channel_id=1, source_target_pairs={{0,32},{32,0},{1,33},{33,1},{2,34},{34,2},{3,35},{35,3},{4,36},{36... | collective-permute-start | bytes 6291464 | tf_op jit(solution)/shard_map/weight_grads/ppermute | solution.py:25
  180.4 13.4 %collective-permute-start.5 = (bf16[128,128]{1,0:T(8,128)(2,1)S(1)}, bf16[128,128]{1,0:T(8,128)(2,1)S(1)}, u32[]{:S(2)}, u32[]{:S(2)}) collective-permute-start(bf16[128,128]{1,0:T(8,128)(2,1)S(1)} %reduce_sum.12), channel_id=1, source_target_pairs={{0,0},{8,8},{16,64},{24,72},{64,16},{72,24},{80,80},{88,88},{1,1},... | collective-permute-start | bytes 98312 | tf_op jit(solution)/shard_map/d_input/ppermute | solution.py:25
  193.8 3.4 %add_convert_fusion = (bf16[1024,512]{1,0:T(8,128)(2,1)}, bf16[1024,512]{1,0:T(8,128)(2,1)}) fusion(bf16[1024,1024]{1,0:T(8,128)(2,1)S(1)} %collective-permute-done.6, bf16[1024,1024]{1,0:T(8,128)(2,1)} %get-tuple-element.27), kind=kLoop, calls=%fused_computation | loop fusion | flops 4194304 | bytes 6291456 | tf_op jit(solution)/shard_map/weight_grads/convert_element_type | solution.py:279
  197.2 0.6 copy.11
  (22 shorter events, 0.2 us)
Async XLA Ops:
  8.0 17.4 %collective-permute-start = (bf16[128,128]{1,0:T(8,128)(2,1)S(1)}, bf16[128,128]{1,0:T(8,128)(2,1)S(1)}, u32[]{:S(2)}, u32[]{:S(2)}) collective-permute-start(bf16[128,128]{1,0:T(8,128)(2,1)S(1)} %multiply_convert_fusion), channel_id=1, source_target_pairs={{0,0},{8,8},{16,64},{24,72},{64,16},{72,24},{80,80},{88,88},{1,1},... | collective-permute-start | bytes 98312 | tf_op jit(solution)/shard_map/gather_inputs/ppermute | solution.py:25
  26.2 22.5 %all-to-all-start = ((bf16[8,128,128]{2,1,0:T(8,128)(2,1)}), bf16[8,128,128]{2,1,0:T(8,128)(2,1)S(1)}, u32[]{:S(2)}, u32[]{:S(2)}) async-start(bf16[8,128,128]{2,1,0:T(8,128)(2,1)} %broadcast_in_dim.6), calls=%async_computation | async-start | bytes 524288 | tf_op jit(solution)/shard_map/gather_inputs/all_to_all | solution.py:48
  36.8 17.6 %collective-permute-start.1 = (bf16[1024,512]{1,0:T(8,128)(2,1)}, bf16[1024,512]{1,0:T(8,128)(2,1)}, u32[]{:S(2)}, u32[]{:S(2)}) collective-permute-start(bf16[1024,512]{1,0:T(8,128)(2,1)} %g0_ref.3), channel_id=1, source_target_pairs={{0,32},{32,0},{1,33},{33,1},{2,34},{34,2},{3,35},{35,3},{4,36},{36... | collective-permute-start | bytes 3145736 | tf_op jit(solution)/shard_map/gather_inputs/ppermute | solution.py:25
  40.8 13.6 %collective-permute-start.2 = (bf16[1024,512]{1,0:T(8,128)(2,1)}, bf16[1024,512]{1,0:T(8,128)(2,1)}, u32[]{:S(2)}, u32[]{:S(2)}) collective-permute-start(bf16[1024,512]{1,0:T(8,128)(2,1)} %u0_ref.3), channel_id=1, source_target_pairs={{0,32},{32,0},{1,33},{33,1},{2,34},{34,2},{3,35},{35,3},{4,36},{36... | collective-permute-start | bytes 3145736 | tf_op jit(solution)/shard_map/gather_inputs/ppermute | solution.py:25
  48.9 13.4 %copy-start.1 = (bf16[1024,512]{1,0:T(8,128)(2,1)S(1)}, bf16[1024,512]{1,0:T(8,128)(2,1)}, u32[]{:S(2)}) copy-start(bf16[1024,512]{1,0:T(8,128)(2,1)} %g0_ref.3) | copy-start | bytes 3145732
  48.9 13.4 %copy-start.2 = (bf16[1024,512]{1,0:T(8,128)(2,1)S(1)}, bf16[1024,512]{1,0:T(8,128)(2,1)}, u32[]{:S(2)}) copy-start(bf16[1024,512]{1,0:T(8,128)(2,1)} %u0_ref.3) | copy-start | bytes 3145732
  50.2 12.1 %all-to-all-start.1 = ((bf16[4,128,1024]{2,1,0:T(8,128)(2,1)}), bf16[4,128,1024]{2,1,0:T(8,128)(2,1)S(1)}, u32[]{:S(2)}, u32[]{:S(2)}) async-start(bf16[4,128,1024]{2,1,0:T(8,128)(2,1)} %broadcast_in_dim.15), calls=%async_computation.1 | async-start | bytes 2097152 | tf_op jit(solution)/shard_map/gather_inputs/all_to_all | solution.py:48
  54.3 72.2 %all-gather.3.cloned.1.call-start = ((), (), s32[]{:S(2)}) async-start(), calls=%async_computation.4 | async-start | bytes 5242880 | tf_op jit(solution)/shard_map/all_inputs/all_gather | solution.py:260
  54.4 72.1 %copy-start.4 = (s32[3]{0:T(128)}, s32[3]{0:T(128)S(1)}, u32[]{:S(2)}) copy-start(s32[3]{0:T(128)S(1)} %pad_add_fusion.place_ref) | copy-start | bytes 40
  62.3 3.2 %copy-start = (bf16[4,128,1024]{2,1,0:T(8,128)(2,1)}, bf16[4,128,1024]{2,1,0:T(8,128)(2,1)S(1)}, u32[]{:S(2)}) copy-start(bf16[4,128,1024]{2,1,0:T(8,128)(2,1)S(1)} %all-to-all-done.1.x_ref) | copy-start | bytes 3145732
  62.3 20.1 %copy-start.3 = (bf16[128,512]{1,0:T(8,128)(2,1)S(1)}, bf16[128,512]{1,0:T(8,128)(2,1)}, u32[]{:S(2)}) copy-start(bf16[128,512]{1,0:T(8,128)(2,1)} %grad_ref.1) | copy-start | bytes 393220
  65.5 0.7 copy-start.5
  66.3 102.8 %all-gather.5.cloned.1.call-start = ((), (), s32[]{:S(2)}) async-start(), calls=%async_computation.5 | async-start | bytes 2621440 | tf_op jit(solution)/shard_map/d_over_x/all_gather | solution.py:273
  66.3 16.1 %collective-permute-start.3 = (bf16[128,1024]{1,0:T(8,128)(2,1)}, bf16[128,1024]{1,0:T(8,128)(2,1)S(1)}, u32[]{:S(2)}, u32[]{:S(2)}) collective-permute-start(bf16[128,1024]{1,0:T(8,128)(2,1)} %copy-done.5), channel_id=1, source_target_pairs={{0,64},{64,0},{1,65},{65,1},{2,66},{66,2},{3,67},{67,3},{4,68},{68... | collective-permute-start | bytes 786440 | tf_op jit(solution)/shard_map/half_sum/ppermute | solution.py:25
  82.6 27.1 %collective-permute-start.4 = (bf16[128,1024]{1,0:T(8,128)(2,1)S(1)}, bf16[128,1024]{1,0:T(8,128)(2,1)S(1)}, u32[]{:S(2)}, u32[]{:S(2)}) collective-permute-start(bf16[128,1024]{1,0:T(8,128)(2,1)S(1)} %hidden_grad.1.d0_ref), channel_id=1, source_target_pairs={{0,64},{64,0},{1,65},{65,1},{2,66},{66,2},{3,67},{67,3},{4,68},{68... | collective-permute-start | bytes 786440 | tf_op jit(solution)/shard_map/d_far/ppermute | solution.py:25
  142.2 35.5 %all-to-all-start.3 = ((bf16[8,128,128]{2,1,0:T(8,128)(2,1)}), bf16[8,128,128]{2,1,0:T(8,128)(2,1)S(1)}, u32[]{:S(2)}, u32[]{:S(2)}) async-start(bf16[8,128,128]{2,1,0:T(8,128)(2,1)} %add_parts.1), calls=%async_computation.3 | async-start | bytes 524288 | tf_op jit(solution)/shard_map/d_input/all_to_all | solution.py:270
  177.7 16.0 %collective-permute-start.6 = (bf16[1024,1024]{1,0:T(8,128)(2,1)}, bf16[1024,1024]{1,0:T(8,128)(2,1)S(1)}, u32[]{:S(2)}, u32[]{:S(2)}) collective-permute-start(bf16[1024,1024]{1,0:T(8,128)(2,1)} %get-tuple-element.28), channel_id=1, source_target_pairs={{0,32},{32,0},{1,33},{33,1},{2,34},{34,2},{3,35},{35,3},{4,36},{36... | collective-permute-start | bytes 6291464 | tf_op jit(solution)/shard_map/weight_grads/ppermute | solution.py:25
  180.4 16.9 %collective-permute-start.5 = (bf16[128,128]{1,0:T(8,128)(2,1)S(1)}, bf16[128,128]{1,0:T(8,128)(2,1)S(1)}, u32[]{:S(2)}, u32[]{:S(2)}) collective-permute-start(bf16[128,128]{1,0:T(8,128)(2,1)S(1)} %reduce_sum.12), channel_id=1, source_target_pairs={{0,0},{8,8},{16,64},{24,72},{64,16},{72,24},{80,80},{88,88},{1,1},... | collective-permute-start | bytes 98312 | tf_op jit(solution)/shard_map/d_input/ppermute | solution.py:25
Sparse Core Ops, SparseCore 0:
  66.4 60.0 all-gather.2
  129.1 39.8 all-gather.4

commit v12 on v11

--- a/solution.py
+++ b/solution.py
@@ -156,7 +156,7 @@
     )(parts)
 
 
-STEP = 256
+STEP = 512
 
 
 def weight_grad_kernel(

time: 205 us -> 206 us (level)
  no operation moved by 1% of the time
where the time goes in v12:
time: 206 us; the launch traced here: 205 us
  starting transfers between devices  81.6 us (40%)
  waiting for transfers between devices  72.4 us (35%)
  Pallas kernels  15.9 us (8%)
  between operations  14.2 us (7%)
  blocking collectives  12 us (6%)
  other arithmetic  5.24 us (3%)
  local copies, waits for them, and re-layouts  3.49 us (2%)
    ppermute x7, starting transfers between devices, permute(): return lax.ppermute(value, axes if len(axes) > 1 else axes[0], pairs)  52.6 us
    ppermute x7, waiting for transfers between devices, permute(): return lax.ppermute(value, axes if len(axes) > 1 else axes[0], pairs)  29.9 us
    all_gather x1, waiting for transfers between devices, shards(): all_inputs = lax.all_gather(inputs, 'x', axis=0, tiled=True)  15.9 us
    all_to_all x2, starting transfers between devices, spread(): lax.all_to_all(jnp.broadcast_to(value[None], (n,) + value.shape), axis, 0...  14.7 us
    all_to_all x1, starting transfers between devices, shards(): di = lax.all_to_all(di, 'zl', 0, 0)  14.2 us
    all_to_all x2, waiting for transfers between devices, spread(): lax.all_to_all(jnp.broadcast_to(value[None], (n,) + value.shape), axis, 0...  13.9 us
    all_gather x1, waiting for transfers between devices, shards(): d_all = lax.all_gather(d_both, 'x', axis=0, tiled=True)  12.6 us
    all_to_all x1, blocking collectives, shards(): di = add_parts(lax.all_to_all(di, 'y', 0, 0), width)  12 us
  transfers between devices with their start and end apart: 12, of which 7 were waited for; matrix products, arithmetic and copies ran while one was open for 3% of the time, Pallas kernels for 6%

profile of v12, /device:TPU:25, one launch (start us, length us, event | category | flops | bytes accessed | tf_op | source)
XLA Modules:
  0.0 204.8 jit_solution(4423305240827764973)
XLA Ops:
  7.2 0.8 multiply_convert_fusion
  8.0 16.1 %collective-permute-start = (bf16[128,128]{1,0:T(8,128)(2,1)S(1)}, bf16[128,128]{1,0:T(8,128)(2,1)S(1)}, u32[]{:S(2)}, u32[]{:S(2)}) collective-permute-start(bf16[128,128]{1,0:T(8,128)(2,1)S(1)} %multiply_convert_fusion), channel_id=1, source_target_pairs={{0,0},{8,8},{16,64},{24,72},{64,16},{72,24},{80,80},{88,88},{1,1},... | collective-permute-start | bytes 98312 | tf_op jit(solution)/shard_map/gather_inputs/ppermute | solution.py:25
  24.1 1.3 collective-permute-done
  25.4 0.7 broadcast_in_dim.6
  26.2 10.6 %all-to-all-start = ((bf16[8,128,128]{2,1,0:T(8,128)(2,1)}), bf16[8,128,128]{2,1,0:T(8,128)(2,1)S(1)}, u32[]{:S(2)}, u32[]{:S(2)}) async-start(bf16[8,128,128]{2,1,0:T(8,128)(2,1)} %broadcast_in_dim.6), calls=%async_computation | async-start | bytes 524288 | tf_op jit(solution)/shard_map/gather_inputs/all_to_all | solution.py:48
  36.8 4.0 %collective-permute-start.1 = (bf16[1024,512]{1,0:T(8,128)(2,1)}, bf16[1024,512]{1,0:T(8,128)(2,1)}, u32[]{:S(2)}, u32[]{:S(2)}) collective-permute-start(bf16[1024,512]{1,0:T(8,128)(2,1)} %g0_ref.3), channel_id=1, source_target_pairs={{0,32},{32,0},{1,33},{33,1},{2,34},{34,2},{3,35},{35,3},{4,36},{36... | collective-permute-start | bytes 3145736 | tf_op jit(solution)/shard_map/gather_inputs/ppermute | solution.py:25
  40.8 1.9 collective-permute-start.2
  42.7 6.0 %all-to-all-done = bf16[8,128,128]{2,1,0:T(8,128)(2,1)S(1)} async-done(((bf16[8,128,128]{2,1,0:T(8,128)(2,1)}), bf16[8,128,128]{2,1,0:T(8,128)(2,1)S(1)}, u32[]{:S(2)}, u32[]{:S(2)}) %all-to-all-start) | async-done | bytes 262176 | tf_op jit(solution)/shard_map/gather_inputs/all_to_all | solution.py:48
  48.7 0.2 copy.8
  48.9 0.1 copy.9
  49.1 1.1 broadcast_in_dim.15
  50.2 4.1 %all-to-all-start.1 = ((bf16[4,128,1024]{2,1,0:T(8,128)(2,1)}), bf16[4,128,1024]{2,1,0:T(8,128)(2,1)S(1)}, u32[]{:S(2)}, u32[]{:S(2)}) async-start(bf16[4,128,1024]{2,1,0:T(8,128)(2,1)} %broadcast_in_dim.15), calls=%async_computation.1 | async-start | bytes 2097152 | tf_op jit(solution)/shard_map/gather_inputs/all_to_all | solution.py:48
  54.4 7.9 %all-to-all-done.1.x_ref = bf16[4,128,1024]{2,1,0:T(8,128)(2,1)S(1)} async-done(((bf16[4,128,1024]{2,1,0:T(8,128)(2,1)}), bf16[4,128,1024]{2,1,0:T(8,128)(2,1)S(1)}, u32[]{:S(2)}, u32[]{:S(2)}) %all-to-all-start.1) | async-done | bytes 1048608 | tf_op jit(solution)/shard_map/gather_inputs/all_to_all | solution.py:48
  62.3 3.2 %partial_gate_up.1 = (bf16[128,1024]{1,0:T(8,128)(2,1)S(1)}, bf16[128,1024]{1,0:T(8,128)(2,1)S(1)}) custom-call(s32[3]{0:T(128)S(1)} %pad_add_fusion.place_ref, bf16[4,128,1024]{2,1,0:T(8,128)(2,1)S(1)} %all-to-all-done.1.x_ref, bf16[1024,512]{1,0:T(8,128)(2,1)S(1)} %copy-done.1, bf16[1024,512]{1,0:T(8,128)(2,1)S(1)} %copy-done.2, ...), custom_call_target="tpu_custom_call" | custom-call | flops 1073741824 | bytes 6291456 | tf_op jit(solution)/shard_map/partial_gate_up/partial_gate_up/pallas_call | solution.py:75
  65.5 0.7 copy-done.5
  66.3 7.3 %collective-permute-start.3 = (bf16[128,1024]{1,0:T(8,128)(2,1)}, bf16[128,1024]{1,0:T(8,128)(2,1)S(1)}, u32[]{:S(2)}, u32[]{:S(2)}) collective-permute-start(bf16[128,1024]{1,0:T(8,128)(2,1)} %copy-done.5), channel_id=1, source_target_pairs={{0,64},{64,0},{1,65},{65,1},{2,66},{66,2},{3,67},{67,3},{4,68},{68... | collective-permute-start | bytes 786440 | tf_op jit(solution)/shard_map/half_sum/ppermute | solution.py:25
  73.6 8.9 %collective-permute-done.3.other_ref = bf16[128,1024]{1,0:T(8,128)(2,1)S(1)} collective-permute-done((bf16[128,1024]{1,0:T(8,128)(2,1)}, bf16[128,1024]{1,0:T(8,128)(2,1)S(1)}, u32[]{:S(2)}, u32[]{:S(2)}) %collective-permute-start.3) | collective-permute-done | bytes 262176 | tf_op jit(solution)/shard_map/half_sum/ppermute | solution.py:25
  82.4 0.2 hidden_grad.1.d0_ref
  82.6 7.3 %collective-permute-start.4 = (bf16[128,1024]{1,0:T(8,128)(2,1)S(1)}, bf16[128,1024]{1,0:T(8,128)(2,1)S(1)}, u32[]{:S(2)}, u32[]{:S(2)}) collective-permute-start(bf16[128,1024]{1,0:T(8,128)(2,1)S(1)} %hidden_grad.1.d0_ref), channel_id=1, source_target_pairs={{0,64},{64,0},{1,65},{65,1},{2,66},{66,2},{3,67},{67,3},{4,68},{68... | collective-permute-start | bytes 786440 | tf_op jit(solution)/shard_map/d_far/ppermute | solution.py:25
  89.9 19.8 %collective-permute-done.4.d1_ref = bf16[128,1024]{1,0:T(8,128)(2,1)S(1)} collective-permute-done((bf16[128,1024]{1,0:T(8,128)(2,1)S(1)}, bf16[128,1024]{1,0:T(8,128)(2,1)S(1)}, u32[]{:S(2)}, u32[]{:S(2)}) %collective-permute-start.4) | collective-permute-done | bytes 262176 | tf_op jit(solution)/shard_map/d_far/ppermute | solution.py:25
  109.7 0.8 pad_maximum_fusion
  110.5 15.9 %all-gather.3.cloned.1.call-done.x_ref = bf16[16,128,1024]{2,1,0:T(8,128)(2,1)} async-done(((bf16[4,128,1024]{2,1,0:T(8,128)(2,1)}), bf16[16,128,1024]{2,1,0:T(8,128)(2,1)}) %all-gather.3.cloned.1.call-update) | async-done | bytes 4194320 | tf_op jit(solution)/shard_map/all_inputs/all_gather | solution.py:260
  126.5 2.8 %input_grad.1 = bf16[4,128,1024]{2,1,0:T(8,128)(2,1)S(1)} custom-call(s32[3]{0:T(128)S(1)} %pad_add_fusion.place_ref, bf16[128,1024]{1,0:T(8,128)(2,1)S(1)} %hidden_grad.1.d0_ref, bf16[128,1024]{1,0:T(8,128)(2,1)S(1)} %collective-permute-done.4.d1_ref, bf16[1024,512]{1,0:T(8,128)(2,1)S(1)} %copy-done.1, bf16[1024,512]{1,0:T(8,128)(2,1)S(1)} %copy-done.2, ...), custom_call_target="tpu_custom_call" | custom-call | flops 1073741824 | bytes 6291456 | tf_op jit(solution)/shard_map/d_input/input_grad/pallas_call | solution.py:126
  129.3 12.0 %all_to_all.20.parts_ref = bf16[4,128,1024]{2,1,0:T(8,128)(2,1)S(1)} all-to-all(bf16[4,128,1024]{2,1,0:T(8,128)(2,1)S(1)} %input_grad.1), channel_id=1, replica_groups=mesh['x'=4,'zh'=2,'c'=2,'y'=4,'zl'=8] {'y'}, dimensions={0} | all-to-all | bytes 2097152 | tf_op jit(solution)/shard_map/d_input/all_to_all | solution.py:269
  141.3 0.9 add_parts.1
  142.2 14.2 %all-to-all-start.3 = ((bf16[8,128,128]{2,1,0:T(8,128)(2,1)}), bf16[8,128,128]{2,1,0:T(8,128)(2,1)S(1)}, u32[]{:S(2)}, u32[]{:S(2)}) async-start(bf16[8,128,128]{2,1,0:T(8,128)(2,1)} %add_parts.1), calls=%async_computation.3 | async-start | bytes 524288 | tf_op jit(solution)/shard_map/d_input/all_to_all | solution.py:270
  156.4 12.6 %all-gather.5.cloned.1.call-done.d_ref = bf16[8,128,1024]{2,1,0:T(8,128)(2,1)} async-done(((bf16[2,128,1024]{2,1,0:T(8,128)(2,1)}), bf16[8,128,1024]{2,1,0:T(8,128)(2,1)}) %all-gather.5.cloned.1.call-update) | async-done | bytes 2097168 | tf_op jit(solution)/shard_map/d_over_x/all_gather | solution.py:273
  169.0 8.8 %weight_grad.1 = (bf16[1024,1024]{1,0:T(8,128)(2,1)}, bf16[1024,1024]{1,0:T(8,128)(2,1)}) custom-call(s32[3]{0:T(128)} %copy-done.4, bf16[16,128,1024]{2,1,0:T(8,128)(2,1)} %all-gather.3.cloned.1.call-done.x_ref, bf16[8,128,1024]{2,1,0:T(8,128)(2,1)} %all-gather.5.cloned.1.call-done.d_ref), custom_call_target="tpu_custom_call" | custom-call | flops 4294967296 | bytes 10485760 | tf_op jit(solution)/shard_map/weight_grads/weight_grad/pallas_call | solution.py:225
  177.9 2.6 %collective-permute-start.6 = (bf16[1024,1024]{1,0:T(8,128)(2,1)}, bf16[1024,1024]{1,0:T(8,128)(2,1)S(1)}, u32[]{:S(2)}, u32[]{:S(2)}) collective-permute-start(bf16[1024,1024]{1,0:T(8,128)(2,1)} %get-tuple-element.28), channel_id=1, source_target_pairs={{0,32},{32,0},{1,33},{33,1},{2,34},{34,2},{3,35},{35,3},{4,36},{36... | collective-permute-start | bytes 6291464 | tf_op jit(solution)/shard_map/weight_grads/ppermute | solution.py:25
  180.5 13.4 %collective-permute-start.5 = (bf16[128,128]{1,0:T(8,128)(2,1)S(1)}, bf16[128,128]{1,0:T(8,128)(2,1)S(1)}, u32[]{:S(2)}, u32[]{:S(2)}) collective-permute-start(bf16[128,128]{1,0:T(8,128)(2,1)S(1)} %reduce_sum.12), channel_id=1, source_target_pairs={{0,0},{8,8},{16,64},{24,72},{64,16},{72,24},{80,80},{88,88},{1,1},... | collective-permute-start | bytes 98312 | tf_op jit(solution)/shard_map/d_input/ppermute | solution.py:25
  193.9 3.4 %add_convert_fusion = (bf16[1024,512]{1,0:T(8,128)(2,1)}, bf16[1024,512]{1,0:T(8,128)(2,1)}) fusion(bf16[1024,1024]{1,0:T(8,128)(2,1)S(1)} %collective-permute-done.6, bf16[1024,1024]{1,0:T(8,128)(2,1)} %get-tuple-element.27), kind=kLoop, calls=%fused_computation | loop fusion | flops 4194304 | bytes 6291456 | tf_op jit(solution)/shard_map/weight_grads/convert_element_type | solution.py:279
  197.3 0.6 copy.11
  (22 shorter events, 0.2 us)
Async XLA Ops:
  8.0 17.4 %collective-permute-start = (bf16[128,128]{1,0:T(8,128)(2,1)S(1)}, bf16[128,128]{1,0:T(8,128)(2,1)S(1)}, u32[]{:S(2)}, u32[]{:S(2)}) collective-permute-start(bf16[128,128]{1,0:T(8,128)(2,1)S(1)} %multiply_convert_fusion), channel_id=1, source_target_pairs={{0,0},{8,8},{16,64},{24,72},{64,16},{72,24},{80,80},{88,88},{1,1},... | collective-permute-start | bytes 98312 | tf_op jit(solution)/shard_map/gather_inputs/ppermute | solution.py:25
  26.2 22.5 %all-to-all-start = ((bf16[8,128,128]{2,1,0:T(8,128)(2,1)}), bf16[8,128,128]{2,1,0:T(8,128)(2,1)S(1)}, u32[]{:S(2)}, u32[]{:S(2)}) async-start(bf16[8,128,128]{2,1,0:T(8,128)(2,1)} %broadcast_in_dim.6), calls=%async_computation | async-start | bytes 524288 | tf_op jit(solution)/shard_map/gather_inputs/all_to_all | solution.py:48
  36.8 17.6 %collective-permute-start.1 = (bf16[1024,512]{1,0:T(8,128)(2,1)}, bf16[1024,512]{1,0:T(8,128)(2,1)}, u32[]{:S(2)}, u32[]{:S(2)}) collective-permute-start(bf16[1024,512]{1,0:T(8,128)(2,1)} %g0_ref.3), channel_id=1, source_target_pairs={{0,32},{32,0},{1,33},{33,1},{2,34},{34,2},{3,35},{35,3},{4,36},{36... | collective-permute-start | bytes 3145736 | tf_op jit(solution)/shard_map/gather_inputs/ppermute | solution.py:25
  40.8 13.6 %collective-permute-start.2 = (bf16[1024,512]{1,0:T(8,128)(2,1)}, bf16[1024,512]{1,0:T(8,128)(2,1)}, u32[]{:S(2)}, u32[]{:S(2)}) collective-permute-start(bf16[1024,512]{1,0:T(8,128)(2,1)} %u0_ref.3), channel_id=1, source_target_pairs={{0,32},{32,0},{1,33},{33,1},{2,34},{34,2},{3,35},{35,3},{4,36},{36... | collective-permute-start | bytes 3145736 | tf_op jit(solution)/shard_map/gather_inputs/ppermute | solution.py:25
  48.9 13.4 %copy-start.1 = (bf16[1024,512]{1,0:T(8,128)(2,1)S(1)}, bf16[1024,512]{1,0:T(8,128)(2,1)}, u32[]{:S(2)}) copy-start(bf16[1024,512]{1,0:T(8,128)(2,1)} %g0_ref.3) | copy-start | bytes 3145732
  48.9 13.4 %copy-start.2 = (bf16[1024,512]{1,0:T(8,128)(2,1)S(1)}, bf16[1024,512]{1,0:T(8,128)(2,1)}, u32[]{:S(2)}) copy-start(bf16[1024,512]{1,0:T(8,128)(2,1)} %u0_ref.3) | copy-start | bytes 3145732
  50.2 12.1 %all-to-all-start.1 = ((bf16[4,128,1024]{2,1,0:T(8,128)(2,1)}), bf16[4,128,1024]{2,1,0:T(8,128)(2,1)S(1)}, u32[]{:S(2)}, u32[]{:S(2)}) async-start(bf16[4,128,1024]{2,1,0:T(8,128)(2,1)} %broadcast_in_dim.15), calls=%async_computation.1 | async-start | bytes 2097152 | tf_op jit(solution)/shard_map/gather_inputs/all_to_all | solution.py:48
  54.3 72.2 %all-gather.3.cloned.1.call-start = ((), (), s32[]{:S(2)}) async-start(), calls=%async_computation.4 | async-start | bytes 5242880 | tf_op jit(solution)/shard_map/all_inputs/all_gather | solution.py:260
  54.4 72.1 %copy-start.4 = (s32[3]{0:T(128)}, s32[3]{0:T(128)S(1)}, u32[]{:S(2)}) copy-start(s32[3]{0:T(128)S(1)} %pad_add_fusion.place_ref) | copy-start | bytes 40
  62.3 3.2 %copy-start = (bf16[4,128,1024]{2,1,0:T(8,128)(2,1)}, bf16[4,128,1024]{2,1,0:T(8,128)(2,1)S(1)}, u32[]{:S(2)}) copy-start(bf16[4,128,1024]{2,1,0:T(8,128)(2,1)S(1)} %all-to-all-done.1.x_ref) | copy-start | bytes 3145732
  62.3 20.1 %copy-start.3 = (bf16[128,512]{1,0:T(8,128)(2,1)S(1)}, bf16[128,512]{1,0:T(8,128)(2,1)}, u32[]{:S(2)}) copy-start(bf16[128,512]{1,0:T(8,128)(2,1)} %grad_ref.1) | copy-start | bytes 393220
  65.5 0.7 copy-start.5
  66.3 102.8 %all-gather.5.cloned.1.call-start = ((), (), s32[]{:S(2)}) async-start(), calls=%async_computation.5 | async-start | bytes 2621440 | tf_op jit(solution)/shard_map/d_over_x/all_gather | solution.py:273
  66.3 16.1 %collective-permute-start.3 = (bf16[128,1024]{1,0:T(8,128)(2,1)}, bf16[128,1024]{1,0:T(8,128)(2,1)S(1)}, u32[]{:S(2)}, u32[]{:S(2)}) collective-permute-start(bf16[128,1024]{1,0:T(8,128)(2,1)} %copy-done.5), channel_id=1, source_target_pairs={{0,64},{64,0},{1,65},{65,1},{2,66},{66,2},{3,67},{67,3},{4,68},{68... | collective-permute-start | bytes 786440 | tf_op jit(solution)/shard_map/half_sum/ppermute | solution.py:25
  82.6 27.1 %collective-permute-start.4 = (bf16[128,1024]{1,0:T(8,128)(2,1)S(1)}, bf16[128,1024]{1,0:T(8,128)(2,1)S(1)}, u32[]{:S(2)}, u32[]{:S(2)}) collective-permute-start(bf16[128,1024]{1,0:T(8,128)(2,1)S(1)} %hidden_grad.1.d0_ref), channel_id=1, source_target_pairs={{0,64},{64,0},{1,65},{65,1},{2,66},{66,2},{3,67},{67,3},{4,68},{68... | collective-permute-start | bytes 786440 | tf_op jit(solution)/shard_map/d_far/ppermute | solution.py:25
  142.2 35.7 %all-to-all-start.3 = ((bf16[8,128,128]{2,1,0:T(8,128)(2,1)}), bf16[8,128,128]{2,1,0:T(8,128)(2,1)S(1)}, u32[]{:S(2)}, u32[]{:S(2)}) async-start(bf16[8,128,128]{2,1,0:T(8,128)(2,1)} %add_parts.1), calls=%async_computation.3 | async-start | bytes 524288 | tf_op jit(solution)/shard_map/d_input/all_to_all | solution.py:270
  177.9 16.0 %collective-permute-start.6 = (bf16[1024,1024]{1,0:T(8,128)(2,1)}, bf16[1024,1024]{1,0:T(8,128)(2,1)S(1)}, u32[]{:S(2)}, u32[]{:S(2)}) collective-permute-start(bf16[1024,1024]{1,0:T(8,128)(2,1)} %get-tuple-element.28), channel_id=1, source_target_pairs={{0,32},{32,0},{1,33},{33,1},{2,34},{34,2},{3,35},{35,3},{4,36},{36... | collective-permute-start | bytes 6291464 | tf_op jit(solution)/shard_map/weight_grads/ppermute | solution.py:25
  180.5 16.9 %collective-permute-start.5 = (bf16[128,128]{1,0:T(8,128)(2,1)S(1)}, bf16[128,128]{1,0:T(8,128)(2,1)S(1)}, u32[]{:S(2)}, u32[]{:S(2)}) collective-permute-start(bf16[128,128]{1,0:T(8,128)(2,1)S(1)} %reduce_sum.12), channel_id=1, source_target_pairs={{0,0},{8,8},{16,64},{24,72},{64,16},{72,24},{80,80},{88,88},{1,1},... | collective-permute-start | bytes 98312 | tf_op jit(solution)/shard_map/d_input/ppermute | solution.py:25
Sparse Core Ops, SparseCore 0:
  66.4 60.0 all-gather.2
  129.1 39.8 all-gather.4

commit v13 on v11

--- a/solution.py
+++ b/solution.py
@@ -276,7 +276,7 @@
         di, sent = lax.optimization_barrier((di, sent))
         got = swap_core(sent)
         d_gate_weight, d_up_weight = (
-            (keep[:, k : k + ff].astype(F32) + got[:, k : k + ff].astype(F32)).astype(BF16) for k in (0, ff)
+            keep[:, k : k + ff] + got[:, k : k + ff] for k in (0, ff)
         )
     with jax.named_scope("d_input"):
         di = swap_half_y(jnp.sum(di.astype(F32), axis=0).astype(BF16))

time: 205 us -> 205 us (level)
    convert_element_type x1 -> x0, other arithmetic: 3.45 us -> none  [shards(): (keep[:, k:k + ff].astype(F32) + got[:, k:k + ff].astype(F32)).astype(BF16)]
    add x0 -> x1, other arithmetic: none -> 3.06 us  [shards(): keep[:, k:k + ff] + got[:, k:k + ff]]
where the time goes in v13:
time: 205 us; the launch traced here: 204 us
  starting transfers between devices  81.6 us (40%)
  waiting for transfers between devices  72.4 us (35%)
  Pallas kernels  15.8 us (8%)
  between operations  14.2 us (7%)
  blocking collectives  12 us (6%)
  other arithmetic  4.86 us (2%)
  local copies, waits for them, and re-layouts  3.49 us (2%)
    ppermute x7, starting transfers between devices, permute(): return lax.ppermute(value, axes if len(axes) > 1 else axes[0], pairs)  52.6 us
    ppermute x7, waiting for transfers between devices, permute(): return lax.ppermute(value, axes if len(axes) > 1 else axes[0], pairs)  29.9 us
    all_gather x1, waiting for transfers between devices, shards(): all_inputs = lax.all_gather(inputs, 'x', axis=0, tiled=True)  15.9 us
    all_to_all x2, starting transfers between devices, spread(): lax.all_to_all(jnp.broadcast_to(value[None], (n,) + value.shape), axis, 0...  14.7 us
    all_to_all x1, starting transfers between devices, shards(): di = lax.all_to_all(di, 'zl', 0, 0)  14.2 us
    all_to_all x2, waiting for transfers between devices, spread(): lax.all_to_all(jnp.broadcast_to(value[None], (n,) + value.shape), axis, 0...  13.9 us
    all_gather x1, waiting for transfers between devices, shards(): d_all = lax.all_gather(d_both, 'x', axis=0, tiled=True)  12.6 us
    all_to_all x1, blocking collectives, shards(): di = add_parts(lax.all_to_all(di, 'y', 0, 0), width)  12 us
  transfers between devices with their start and end apart: 12, of which 7 were waited for; matrix products, arithmetic and copies ran while one was open for 3% of the time, Pallas kernels for 6%

profile of v13, /device:TPU:25, one launch (start us, length us, event | category | flops | bytes accessed | tf_op | source)
XLA Modules:
  0.0 204.3 jit_solution(16829735717996716923)
XLA Ops:
  7.2 0.8 multiply_convert_fusion
  8.0 16.1 %collective-permute-start = (bf16[128,128]{1,0:T(8,128)(2,1)S(1)}, bf16[128,128]{1,0:T(8,128)(2,1)S(1)}, u32[]{:S(2)}, u32[]{:S(2)}) collective-permute-start(bf16[128,128]{1,0:T(8,128)(2,1)S(1)} %multiply_convert_fusion), channel_id=1, source_target_pairs={{0,0},{8,8},{16,64},{24,72},{64,16},{72,24},{80,80},{88,88},{1,1},... | collective-permute-start | bytes 98312 | tf_op jit(solution)/shard_map/gather_inputs/ppermute | solution.py:25
  24.1 1.3 collective-permute-done
  25.4 0.7 broadcast_in_dim.6
  26.2 10.6 %all-to-all-start = ((bf16[8,128,128]{2,1,0:T(8,128)(2,1)}), bf16[8,128,128]{2,1,0:T(8,128)(2,1)S(1)}, u32[]{:S(2)}, u32[]{:S(2)}) async-start(bf16[8,128,128]{2,1,0:T(8,128)(2,1)} %broadcast_in_dim.6), calls=%async_computation | async-start | bytes 524288 | tf_op jit(solution)/shard_map/gather_inputs/all_to_all | solution.py:48
  36.8 4.0 %collective-permute-start.1 = (bf16[1024,512]{1,0:T(8,128)(2,1)}, bf16[1024,512]{1,0:T(8,128)(2,1)}, u32[]{:S(2)}, u32[]{:S(2)}) collective-permute-start(bf16[1024,512]{1,0:T(8,128)(2,1)} %g0_ref.3), channel_id=1, source_target_pairs={{0,32},{32,0},{1,33},{33,1},{2,34},{34,2},{3,35},{35,3},{4,36},{36... | collective-permute-start | bytes 3145736 | tf_op jit(solution)/shard_map/gather_inputs/ppermute | solution.py:25
  40.8 1.9 collective-permute-start.2
  42.7 6.0 %all-to-all-done = bf16[8,128,128]{2,1,0:T(8,128)(2,1)S(1)} async-done(((bf16[8,128,128]{2,1,0:T(8,128)(2,1)}), bf16[8,128,128]{2,1,0:T(8,128)(2,1)S(1)}, u32[]{:S(2)}, u32[]{:S(2)}) %all-to-all-start) | async-done | bytes 262176 | tf_op jit(solution)/shard_map/gather_inputs/all_to_all | solution.py:48
  48.7 0.2 copy.8
  48.9 0.1 copy.9
  49.1 1.1 broadcast_in_dim.15
  50.2 4.1 %all-to-all-start.1 = ((bf16[4,128,1024]{2,1,0:T(8,128)(2,1)}), bf16[4,128,1024]{2,1,0:T(8,128)(2,1)S(1)}, u32[]{:S(2)}, u32[]{:S(2)}) async-start(bf16[4,128,1024]{2,1,0:T(8,128)(2,1)} %broadcast_in_dim.15), calls=%async_computation.1 | async-start | bytes 2097152 | tf_op jit(solution)/shard_map/gather_inputs/all_to_all | solution.py:48
  54.4 7.9 %all-to-all-done.1.x_ref = bf16[4,128,1024]{2,1,0:T(8,128)(2,1)S(1)} async-done(((bf16[4,128,1024]{2,1,0:T(8,128)(2,1)}), bf16[4,128,1024]{2,1,0:T(8,128)(2,1)S(1)}, u32[]{:S(2)}, u32[]{:S(2)}) %all-to-all-start.1) | async-done | bytes 1048608 | tf_op jit(solution)/shard_map/gather_inputs/all_to_all | solution.py:48
  62.3 3.2 %partial_gate_up.1 = (bf16[128,1024]{1,0:T(8,128)(2,1)S(1)}, bf16[128,1024]{1,0:T(8,128)(2,1)S(1)}) custom-call(s32[3]{0:T(128)S(1)} %pad_add_fusion.place_ref, bf16[4,128,1024]{2,1,0:T(8,128)(2,1)S(1)} %all-to-all-done.1.x_ref, bf16[1024,512]{1,0:T(8,128)(2,1)S(1)} %copy-done.1, bf16[1024,512]{1,0:T(8,128)(2,1)S(1)} %copy-done.2, ...), custom_call_target="tpu_custom_call" | custom-call | flops 1073741824 | bytes 6291456 | tf_op jit(solution)/shard_map/partial_gate_up/partial_gate_up/pallas_call | solution.py:75
  65.5 0.7 copy-done.5
  66.3 7.3 %collective-permute-start.3 = (bf16[128,1024]{1,0:T(8,128)(2,1)}, bf16[128,1024]{1,0:T(8,128)(2,1)S(1)}, u32[]{:S(2)}, u32[]{:S(2)}) collective-permute-start(bf16[128,1024]{1,0:T(8,128)(2,1)} %copy-done.5), channel_id=1, source_target_pairs={{0,64},{64,0},{1,65},{65,1},{2,66},{66,2},{3,67},{67,3},{4,68},{68... | collective-permute-start | bytes 786440 | tf_op jit(solution)/shard_map/half_sum/ppermute | solution.py:25
  73.6 8.9 %collective-permute-done.3.other_ref = bf16[128,1024]{1,0:T(8,128)(2,1)S(1)} collective-permute-done((bf16[128,1024]{1,0:T(8,128)(2,1)}, bf16[128,1024]{1,0:T(8,128)(2,1)S(1)}, u32[]{:S(2)}, u32[]{:S(2)}) %collective-permute-start.3) | collective-permute-done | bytes 262176 | tf_op jit(solution)/shard_map/half_sum/ppermute | solution.py:25
  82.4 0.2 hidden_grad.1.d0_ref
  82.6 7.3 %collective-permute-start.4 = (bf16[128,1024]{1,0:T(8,128)(2,1)S(1)}, bf16[128,1024]{1,0:T(8,128)(2,1)S(1)}, u32[]{:S(2)}, u32[]{:S(2)}) collective-permute-start(bf16[128,1024]{1,0:T(8,128)(2,1)S(1)} %hidden_grad.1.d0_ref), channel_id=1, source_target_pairs={{0,64},{64,0},{1,65},{65,1},{2,66},{66,2},{3,67},{67,3},{4,68},{68... | collective-permute-start | bytes 786440 | tf_op jit(solution)/shard_map/d_far/ppermute | solution.py:25
  89.9 19.8 %collective-permute-done.4.d1_ref = bf16[128,1024]{1,0:T(8,128)(2,1)S(1)} collective-permute-done((bf16[128,1024]{1,0:T(8,128)(2,1)S(1)}, bf16[128,1024]{1,0:T(8,128)(2,1)S(1)}, u32[]{:S(2)}, u32[]{:S(2)}) %collective-permute-start.4) | collective-permute-done | bytes 262176 | tf_op jit(solution)/shard_map/d_far/ppermute | solution.py:25
  109.7 0.8 pad_maximum_fusion
  110.5 15.9 %all-gather.3.cloned.1.call-done.x_ref = bf16[16,128,1024]{2,1,0:T(8,128)(2,1)} async-done(((bf16[4,128,1024]{2,1,0:T(8,128)(2,1)}), bf16[16,128,1024]{2,1,0:T(8,128)(2,1)}) %all-gather.3.cloned.1.call-update) | async-done | bytes 4194320 | tf_op jit(solution)/shard_map/all_inputs/all_gather | solution.py:260
  126.5 2.8 %input_grad.1 = bf16[4,128,1024]{2,1,0:T(8,128)(2,1)S(1)} custom-call(s32[3]{0:T(128)S(1)} %pad_add_fusion.place_ref, bf16[128,1024]{1,0:T(8,128)(2,1)S(1)} %hidden_grad.1.d0_ref, bf16[128,1024]{1,0:T(8,128)(2,1)S(1)} %collective-permute-done.4.d1_ref, bf16[1024,512]{1,0:T(8,128)(2,1)S(1)} %copy-done.1, bf16[1024,512]{1,0:T(8,128)(2,1)S(1)} %copy-done.2, ...), custom_call_target="tpu_custom_call" | custom-call | flops 1073741824 | bytes 6291456 | tf_op jit(solution)/shard_map/d_input/input_grad/pallas_call | solution.py:126
  129.3 12.0 %all_to_all.20.parts_ref = bf16[4,128,1024]{2,1,0:T(8,128)(2,1)S(1)} all-to-all(bf16[4,128,1024]{2,1,0:T(8,128)(2,1)S(1)} %input_grad.1), channel_id=1, replica_groups=mesh['x'=4,'zh'=2,'c'=2,'y'=4,'zl'=8] {'y'}, dimensions={0} | all-to-all | bytes 2097152 | tf_op jit(solution)/shard_map/d_input/all_to_all | solution.py:269
  141.3 0.9 add_parts.1
  142.2 14.2 %all-to-all-start.3 = ((bf16[8,128,128]{2,1,0:T(8,128)(2,1)}), bf16[8,128,128]{2,1,0:T(8,128)(2,1)S(1)}, u32[]{:S(2)}, u32[]{:S(2)}) async-start(bf16[8,128,128]{2,1,0:T(8,128)(2,1)} %add_parts.1), calls=%async_computation.3 | async-start | bytes 524288 | tf_op jit(solution)/shard_map/d_input/all_to_all | solution.py:270
  156.4 12.6 %all-gather.5.cloned.1.call-done.d_ref = bf16[8,128,1024]{2,1,0:T(8,128)(2,1)} async-done(((bf16[2,128,1024]{2,1,0:T(8,128)(2,1)}), bf16[8,128,1024]{2,1,0:T(8,128)(2,1)}) %all-gather.5.cloned.1.call-update) | async-done | bytes 2097168 | tf_op jit(solution)/shard_map/d_over_x/all_gather | solution.py:273
  169.0 8.7 %weight_grad.1 = (bf16[1024,1024]{1,0:T(8,128)(2,1)}, bf16[1024,1024]{1,0:T(8,128)(2,1)}) custom-call(s32[3]{0:T(128)} %copy-done.4, bf16[16,128,1024]{2,1,0:T(8,128)(2,1)} %all-gather.3.cloned.1.call-done.x_ref, bf16[8,128,1024]{2,1,0:T(8,128)(2,1)} %all-gather.5.cloned.1.call-done.d_ref), custom_call_target="tpu_custom_call" | custom-call | flops 4294967296 | bytes 10485760 | tf_op jit(solution)/shard_map/weight_grads/weight_grad/pallas_call | solution.py:225
  177.7 2.6 %collective-permute-start.6 = (bf16[1024,1024]{1,0:T(8,128)(2,1)}, bf16[1024,1024]{1,0:T(8,128)(2,1)S(1)}, u32[]{:S(2)}, u32[]{:S(2)}) collective-permute-start(bf16[1024,1024]{1,0:T(8,128)(2,1)} %get-tuple-element.28), channel_id=1, source_target_pairs={{0,32},{32,0},{1,33},{33,1},{2,34},{34,2},{3,35},{35,3},{4,36},{36... | collective-permute-start | bytes 6291464 | tf_op jit(solution)/shard_map/weight_grads/ppermute | solution.py:25
  180.4 13.4 %collective-permute-start.5 = (bf16[128,128]{1,0:T(8,128)(2,1)S(1)}, bf16[128,128]{1,0:T(8,128)(2,1)S(1)}, u32[]{:S(2)}, u32[]{:S(2)}) collective-permute-start(bf16[128,128]{1,0:T(8,128)(2,1)S(1)} %reduce_sum.12), channel_id=1, source_target_pairs={{0,0},{8,8},{16,64},{24,72},{64,16},{72,24},{80,80},{88,88},{1,1},... | collective-permute-start | bytes 98312 | tf_op jit(solution)/shard_map/d_input/ppermute | solution.py:25
  193.8 3.1 %slice_add_fusion = (bf16[1024,512]{1,0:T(8,128)(2,1)}, bf16[1024,512]{1,0:T(8,128)(2,1)}) fusion(bf16[1024,1024]{1,0:T(8,128)(2,1)S(1)} %collective-permute-done.6, bf16[1024,1024]{1,0:T(8,128)(2,1)} %get-tuple-element.27), kind=kLoop, calls=%fused_computation | loop fusion | flops 1048576 | bytes 6291456 | tf_op jit(solution)/shard_map/weight_grads/add | solution.py:279
  196.8 0.6 copy.11
  (22 shorter events, 0.2 us)
Async XLA Ops:
  8.0 17.4 %collective-permute-start = (bf16[128,128]{1,0:T(8,128)(2,1)S(1)}, bf16[128,128]{1,0:T(8,128)(2,1)S(1)}, u32[]{:S(2)}, u32[]{:S(2)}) collective-permute-start(bf16[128,128]{1,0:T(8,128)(2,1)S(1)} %multiply_convert_fusion), channel_id=1, source_target_pairs={{0,0},{8,8},{16,64},{24,72},{64,16},{72,24},{80,80},{88,88},{1,1},... | collective-permute-start | bytes 98312 | tf_op jit(solution)/shard_map/gather_inputs/ppermute | solution.py:25
  26.2 22.5 %all-to-all-start = ((bf16[8,128,128]{2,1,0:T(8,128)(2,1)}), bf16[8,128,128]{2,1,0:T(8,128)(2,1)S(1)}, u32[]{:S(2)}, u32[]{:S(2)}) async-start(bf16[8,128,128]{2,1,0:T(8,128)(2,1)} %broadcast_in_dim.6), calls=%async_computation | async-start | bytes 524288 | tf_op jit(solution)/shard_map/gather_inputs/all_to_all | solution.py:48
  36.8 17.6 %collective-permute-start.1 = (bf16[1024,512]{1,0:T(8,128)(2,1)}, bf16[1024,512]{1,0:T(8,128)(2,1)}, u32[]{:S(2)}, u32[]{:S(2)}) collective-permute-start(bf16[1024,512]{1,0:T(8,128)(2,1)} %g0_ref.3), channel_id=1, source_target_pairs={{0,32},{32,0},{1,33},{33,1},{2,34},{34,2},{3,35},{35,3},{4,36},{36... | collective-permute-start | bytes 3145736 | tf_op jit(solution)/shard_map/gather_inputs/ppermute | solution.py:25
  40.8 13.6 %collective-permute-start.2 = (bf16[1024,512]{1,0:T(8,128)(2,1)}, bf16[1024,512]{1,0:T(8,128)(2,1)}, u32[]{:S(2)}, u32[]{:S(2)}) collective-permute-start(bf16[1024,512]{1,0:T(8,128)(2,1)} %u0_ref.3), channel_id=1, source_target_pairs={{0,32},{32,0},{1,33},{33,1},{2,34},{34,2},{3,35},{35,3},{4,36},{36... | collective-permute-start | bytes 3145736 | tf_op jit(solution)/shard_map/gather_inputs/ppermute | solution.py:25
  48.9 13.4 %copy-start.1 = (bf16[1024,512]{1,0:T(8,128)(2,1)S(1)}, bf16[1024,512]{1,0:T(8,128)(2,1)}, u32[]{:S(2)}) copy-start(bf16[1024,512]{1,0:T(8,128)(2,1)} %g0_ref.3) | copy-start | bytes 3145732
  48.9 13.4 %copy-start.2 = (bf16[1024,512]{1,0:T(8,128)(2,1)S(1)}, bf16[1024,512]{1,0:T(8,128)(2,1)}, u32[]{:S(2)}) copy-start(bf16[1024,512]{1,0:T(8,128)(2,1)} %u0_ref.3) | copy-start | bytes 3145732
  50.2 12.1 %all-to-all-start.1 = ((bf16[4,128,1024]{2,1,0:T(8,128)(2,1)}), bf16[4,128,1024]{2,1,0:T(8,128)(2,1)S(1)}, u32[]{:S(2)}, u32[]{:S(2)}) async-start(bf16[4,128,1024]{2,1,0:T(8,128)(2,1)} %broadcast_in_dim.15), calls=%async_computation.1 | async-start | bytes 2097152 | tf_op jit(solution)/shard_map/gather_inputs/all_to_all | solution.py:48
  54.3 72.2 %all-gather.3.cloned.1.call-start = ((), (), s32[]{:S(2)}) async-start(), calls=%async_computation.4 | async-start | bytes 5242880 | tf_op jit(solution)/shard_map/all_inputs/all_gather | solution.py:260
  54.4 72.1 %copy-start.4 = (s32[3]{0:T(128)}, s32[3]{0:T(128)S(1)}, u32[]{:S(2)}) copy-start(s32[3]{0:T(128)S(1)} %pad_add_fusion.place_ref) | copy-start | bytes 40
  62.3 3.2 %copy-start = (bf16[4,128,1024]{2,1,0:T(8,128)(2,1)}, bf16[4,128,1024]{2,1,0:T(8,128)(2,1)S(1)}, u32[]{:S(2)}) copy-start(bf16[4,128,1024]{2,1,0:T(8,128)(2,1)S(1)} %all-to-all-done.1.x_ref) | copy-start | bytes 3145732
  62.3 20.1 %copy-start.3 = (bf16[128,512]{1,0:T(8,128)(2,1)S(1)}, bf16[128,512]{1,0:T(8,128)(2,1)}, u32[]{:S(2)}) copy-start(bf16[128,512]{1,0:T(8,128)(2,1)} %grad_ref.1) | copy-start | bytes 393220
  65.5 0.7 copy-start.5
  66.3 102.8 %all-gather.5.cloned.1.call-start = ((), (), s32[]{:S(2)}) async-start(), calls=%async_computation.5 | async-start | bytes 2621440 | tf_op jit(solution)/shard_map/d_over_x/all_gather | solution.py:273
  66.3 16.1 %collective-permute-start.3 = (bf16[128,1024]{1,0:T(8,128)(2,1)}, bf16[128,1024]{1,0:T(8,128)(2,1)S(1)}, u32[]{:S(2)}, u32[]{:S(2)}) collective-permute-start(bf16[128,1024]{1,0:T(8,128)(2,1)} %copy-done.5), channel_id=1, source_target_pairs={{0,64},{64,0},{1,65},{65,1},{2,66},{66,2},{3,67},{67,3},{4,68},{68... | collective-permute-start | bytes 786440 | tf_op jit(solution)/shard_map/half_sum/ppermute | solution.py:25
  82.6 27.1 %collective-permute-start.4 = (bf16[128,1024]{1,0:T(8,128)(2,1)S(1)}, bf16[128,1024]{1,0:T(8,128)(2,1)S(1)}, u32[]{:S(2)}, u32[]{:S(2)}) collective-permute-start(bf16[128,1024]{1,0:T(8,128)(2,1)S(1)} %hidden_grad.1.d0_ref), channel_id=1, source_target_pairs={{0,64},{64,0},{1,65},{65,1},{2,66},{66,2},{3,67},{67,3},{4,68},{68... | collective-permute-start | bytes 786440 | tf_op jit(solution)/shard_map/d_far/ppermute | solution.py:25
  142.2 35.5 %all-to-all-start.3 = ((bf16[8,128,128]{2,1,0:T(8,128)(2,1)}), bf16[8,128,128]{2,1,0:T(8,128)(2,1)S(1)}, u32[]{:S(2)}, u32[]{:S(2)}) async-start(bf16[8,128,128]{2,1,0:T(8,128)(2,1)} %add_parts.1), calls=%async_computation.3 | async-start | bytes 524288 | tf_op jit(solution)/shard_map/d_input/all_to_all | solution.py:270
  177.7 16.0 %collective-permute-start.6 = (bf16[1024,1024]{1,0:T(8,128)(2,1)}, bf16[1024,1024]{1,0:T(8,128)(2,1)S(1)}, u32[]{:S(2)}, u32[]{:S(2)}) collective-permute-start(bf16[1024,1024]{1,0:T(8,128)(2,1)} %get-tuple-element.28), channel_id=1, source_target_pairs={{0,32},{32,0},{1,33},{33,1},{2,34},{34,2},{3,35},{35,3},{4,36},{36... | collective-permute-start | bytes 6291464 | tf_op jit(solution)/shard_map/weight_grads/ppermute | solution.py:25
  180.4 16.5 %collective-permute-start.5 = (bf16[128,128]{1,0:T(8,128)(2,1)S(1)}, bf16[128,128]{1,0:T(8,128)(2,1)S(1)}, u32[]{:S(2)}, u32[]{:S(2)}) collective-permute-start(bf16[128,128]{1,0:T(8,128)(2,1)S(1)} %reduce_sum.12), channel_id=1, source_target_pairs={{0,0},{8,8},{16,64},{24,72},{64,16},{72,24},{80,80},{88,88},{1,1},... | collective-permute-start | bytes 98312 | tf_op jit(solution)/shard_map/d_input/ppermute | solution.py:25
Sparse Core Ops, SparseCore 0:
  66.4 60.0 all-gather.2
  129.1 39.8 all-gather.4
